TPU v7x, 32 devices: a whole 2x2x4 slice. The times are simulated.
32 devices in a mesh: dp: 2 (over y), cell: 4 (over z), gene: 4 (over x, core).
Axes of the slice: x: 2, y: 2, z: 4, core: 2. Of those that a mesh axis runs over, the one named last changes fastest.
Arguments:
- expression: bfloat16 [4000, 8192], P('gene', ('dp', 'cell')), may hold values from 0.15 to 40
- usage_init: float32 [64, 8192], P(None, ('dp', 'cell')), may hold values from 0.1 to 1.5
- shared_factor: float32 [64, 4000], P(None, 'gene'), may hold values from 0.03 to 1
- dataset_factors: float32 [10, 64, 4000], P('dp', None, 'gene'), may hold values from 0.03 to 1
- cell_dataset: int32 [8192], P(('dp', 'cell')), may hold values from 0 to 5, as said below
- dataset_sizes: int32 [10], P('dp'), may hold values from 1 to 4092, as said below
Outputs:
- new_usage: float32 [64, 8192], P(None, ('dp', 'cell'))
- new_dataset_factors: float32 [10, 64, 4000], P('dp', None, 'gene')
- new_shared_factor: float32 [64, 4000], P(None, 'gene')
Inputs may be any that keep to these rules, and one draw needn't show every extreme that they name: `cell_dataset`: each group's live slots come first, a value of 5 marks an empty slot, every dataset has at least one live slot in every group, and one group has all its 4096 slots live. `dataset_sizes`: the number of live slots of each dataset within its group, as counted from cell_dataset; some dataset has exactly 4092 of them.
All inputs are finite; a program needn't handle non-finite values.
Results may differ from a plain program's by a relative error of at most 0.0003.
The roundings to bfloat16 on the way count: a program that leaves them out, or rounds other values in their place, can miss the bound.
Values sent between devices are 32-bit elements; how exact they have to be, the bound alone decides.
No kernel may reach another device: no remote copies, remote signals or barrier semaphores. Data moves between devices by JAX's collectives and lax.ppermute only.
A program may use at most 64 MiB of HBM per device.

v0:
```python
import jax
import jax.numpy as jnp
from jax import lax
from jax.sharding import PartitionSpec as P

ITERS = 3


penalty = 5.0
precise = lax.Precision.HIGHEST


def shared_update(shared_now, total_cross, total_gram, total_pull):
    for sweep in range(ITERS):
        shared_now = (
            shared_now
            * total_cross
            / (jnp.dot(total_gram, shared_now, precision=precise) + total_pull)
        )
    return shared_now


def body(expression, usage_init, shared_factor, dataset_factors, cell_dataset, dataset_sizes):
    dataset_count = dataset_factors.shape[0]
    factor_rank = shared_factor.shape[0]
    gene_count = shared_factor.shape[1]
    slot_count = expression.shape[1]
    counted = dataset_sizes.astype(jnp.float32)
    onehot = (cell_dataset[None, :] == jnp.arange(dataset_count, dtype=jnp.int32)[:, None]).astype(
        jnp.float32
    )
    alive_mask = cell_dataset < dataset_count
    stacked_low = jnp.concatenate([shared_factor[None], dataset_factors], axis=0).astype(
        jnp.bfloat16
    )
    products = jnp.dot(
        stacked_low.reshape((dataset_count + 1) * factor_rank, gene_count),
        expression,
        preferred_element_type=jnp.float32,
    ).reshape(dataset_count + 1, factor_rank, slot_count)
    cross_part = products[0] + jnp.sum(onehot[:, None, :] * products[1:], axis=0)
    combined = shared_factor[None] + dataset_factors
    gram_part = jnp.einsum(
        "dkg,dlg->dkl", combined, combined, precision=precise
    ) + penalty * jnp.einsum("dkg,dlg->dkl", dataset_factors, dataset_factors, precision=precise)
    cross_sum, gram_full = lax.psum((cross_part, gram_part), "gene")
    usage_now = usage_init
    for sweep in range(ITERS):
        stacked = jnp.dot(
            gram_full.reshape(dataset_count * factor_rank, factor_rank),
            usage_now,
            precision=precise,
        ).reshape(dataset_count, factor_rank, slot_count)
        divisor = jnp.sum(onehot[:, None, :] * stacked, axis=0)
        divisor = jnp.where(alive_mask[None, :], divisor, 1.0)
        usage_now = jnp.where(alive_mask[None, :], usage_now * cross_sum / divisor, usage_now)
    masked_usage = onehot[:, None, :] * usage_now[None]
    low_usage = masked_usage.astype(jnp.bfloat16).reshape(dataset_count * factor_rank, slot_count)
    cross_stat_part = lax.dot_general(
        low_usage, expression, (((1,), (1,)), ((), ())), preferred_element_type=jnp.float32
    ).reshape(dataset_count, factor_rank, gene_count)
    cross_stat_part = cross_stat_part / counted[:, None, None]
    gram_stat_part = (
        jnp.einsum("dkc,dlc->dkl", masked_usage, masked_usage, precision=precise)
        / counted[:, None, None]
    )
    stat_cross, stat_gram = lax.psum((cross_stat_part, gram_stat_part), "cell")
    total_cross = jnp.sum(stat_cross, axis=0)
    total_gram = jnp.sum(stat_gram, axis=0)
    factor_now = dataset_factors
    for sweep in range(ITERS):
        divisor = jnp.einsum("dkl,lg->dkg", stat_gram, shared_factor, precision=precise) + (
            1.0 + penalty
        ) * jnp.einsum("dkl,dlg->dkg", stat_gram, factor_now, precision=precise)
        factor_now = factor_now * stat_cross / divisor
    total_pull = jnp.einsum("dkl,dlg->kg", stat_gram, factor_now, precision=precise)
    total_cross, total_gram, total_pull = lax.psum((total_cross, total_gram, total_pull), "dp")
    shared_now = shared_update(shared_factor, total_cross, total_gram, total_pull)
    return (usage_now, factor_now, shared_now)


def solution(mesh):
    return jax.shard_map(
        body,
        mesh=mesh,
        in_specs=(
            P("gene", ("dp", "cell")),
            P(None, ("dp", "cell")),
            P(None, "gene"),
            P("dp", None, "gene"),
            P(("dp", "cell")),
            P("dp"),
        ),
        out_specs=(P(None, ("dp", "cell")), P("dp", None, "gene"), P(None, "gene")),
        check_vma=False,
    )
```

profile of v0, /device:TPU:0, one launch (start us, length us, event | category | flops | bytes accessed | tf_op | source)
XLA Modules:
  0.0 176.1 jit_solution(13196399215512112390)
XLA Ops:
  7.2 0.0 copy-start
  7.2 0.0 copy-start.1
  7.2 0.0 all-reduce.7.cloned.1.call-start
  7.2 1.6 convert.8
  8.8 0.2 copy-done.1
  9.0 1.3 convolution_multiply_fusion.6
  10.4 0.0 copy-done.13
  10.4 0.0 copy-done.6
  10.4 0.1 pad_maximum_fusion
  10.5 0.0 copy-done
  10.5 1.0 fusion.38
  11.5 0.1 slice.14
  11.7 0.1 multiply_reduce_fusion
  11.8 0.7 slice_add_fusion
  12.6 2.0 %fusion.21 = f32[5,64,64]{2,1,0:T(8,128)} fusion(f32[5,64,64]{2,1,0:T(8,128)S(1)} %convolution_multiply_fusion.6, f32[5,64,1000]{2,1,0:T(8,128)S(1)} %copy-done.1, f32[64,1000]{1,0:T(8,128)S(1)} %copy-done.6), kind=kOutput, calls=%fused_computation.31 | convolution fusion | flops 246100480 | bytes 1699840 | tf_op jit(solution)/shard_map/dkg,dlg->dkl/dot_general | solution.py:43
  14.6 0.0 all-reduce.7.cloned.1.call-update
  14.6 0.0 all-reduce.9.cloned.1.call-start
  14.7 0.0 copy-done.14
  14.7 35.6 %all-reduce.7.cloned.1.call-done = (f32[5,64,64]{2,1,0:T(8,128)}, f32[64,1024]{1,0:T(8,128)}) async-done(((f32[5,64,64]{2,1,0:T(8,128)}, f32[64,1024]{1,0:T(8,128)}), (f32[5,64,64]{2,1,0:T(8,128)}, f32[64,1024]{1,0:T(8,128)})) %all-reduce.7.cloned.1.call-update) | async-done | bytes 344080 | tf_op jit(solution)/shard_map/psum | solution.py:46
  50.3 2.3 %fusion.12 = f32[64,1024]{1,0:T(8,128)S(1)} fusion(f32[5,64,64]{2,1,0:T(8,128)} %get-tuple-element.3, f32[5,1024]{1,0:T(8,128)S(1)} %fusion.37, f32[64,1024]{1,0:T(8,128)} %param.7), kind=kOutput, calls=%fused_computation.20 | convolution fusion | flops 252248064 | bytes 626688 | tf_op jit(solution)/shard_map/dot_general | solution.py:49
  52.6 2.4 %fusion.13 = f32[64,1024]{1,0:T(8,128)S(1)} fusion(f32[5,64,64]{2,1,0:T(8,128)} %get-tuple-element.3, f32[5,1024]{1,0:T(8,128)S(1)} %fusion.37, f32[64,1024]{1,0:T(8,128)} %param.7, f32[64,1024]{1,0:T(8,128)S(1)} %fusion.12, f32[64,1024]{1,0:T(8,128)} %get-tuple-element.4, pred[1024]{0:T(1024)(128)(4,1)S(1)} %broadcast_compare_fusion), kind=kOutput, calls=%fused_computation.21 | convolution fusion | flops 252510208 | bytes 1152000 | tf_op jit(solution)/shard_map/dot_general | solution.py:49
  55.0 0.0 copy-done.9
  55.0 0.0 copy-done.10
  55.1 0.1 divide_select_fusion.1
  55.2 0.0 copy-done.11
  55.2 1.2 fusion.14
  56.4 0.1 divide_select_fusion
  56.5 0.0 copy-start.12
  56.5 1.9 %fusion.15 = f32[5,64,1000]{2,1,0:T(8,128)} fusion(bf16[1000,1024]{1,0:T(8,128)(2,1)S(1)} %copy-done, f32[5]{0:T(128)S(1)} %convert_element_type.23, f32[64,1024]{1,0:T(8,128)S(1)} %divide_select_fusion, f32[5,1024]{1,0:T(8,128)S(1)} %fusion.37), kind=kOutput, calls=%fused_computation.23 | convolution fusion | flops 656335360 | bytes 3610644 | tf_op jit(solution)/shard_map/dot_general | solution.py:59
  58.4 0.0 copy-done.12
  58.4 2.0 %fusion.24 = f32[5,64,64]{2,1,0:T(8,128)} fusion(f32[64,1024]{1,0:T(8,128)S(1)} %divide_select_fusion, f32[5,1024]{1,0:T(8,128)S(1)} %fusion.37, f32[5]{0:T(128)S(1)} %convert_element_type.23), kind=kOutput, calls=%fused_computation.32 | convolution fusion | flops 252006400 | bytes 364564 | tf_op jit(solution)/shard_map/dkc,dlc->dkl/dot_general | solution.py:64
  60.4 0.0 all-reduce.9.cloned.1.call-update
  60.4 0.2 all-reduce.11.cloned.1.call-start
  60.7 66.2 %all-reduce.9.cloned.1.call-done = (f32[5,64,64]{2,1,0:T(8,128)}, f32[5,64,1000]{2,1,0:T(8,128)}) async-done(((f32[5,64,64]{2,1,0:T(8,128)}, f32[5,64,1000]{2,1,0:T(8,128)}), (f32[5,64,64]{2,1,0:T(8,128)}, f32[5,64,1000]{2,1,0:T(8,128)})) %all-reduce.9.cloned.1.call-update) | async-done | bytes 1361936 | tf_op jit(solution)/shard_map/psum | solution.py:67
  126.9 2.3 %fusion.32 = f32[5,64,1000]{2,1,0:T(8,128)S(1)} fusion(f32[5,64,64]{2,1,0:T(8,128)} %get-tuple-element.5, f32[64,1000]{1,0:T(8,128)} %param.8), kind=kOutput, calls=%fused_computation.41 | convolution fusion | flops 245760000 | bytes 1617920 | tf_op jit(solution)/shard_map/dkl,lg->dkg/dot_general | solution.py:72
  129.2 1.5 fusion.7
  130.7 1.5 fusion.8
  132.2 1.5 fusion.9
  133.7 0.0 copy-start.5
  133.8 1.0 copy-done.5
  134.8 1.7 convolution_bitcast_fusion
  136.5 0.8 reduce_sum.58
  137.3 0.0 all-reduce.11.cloned.1.call-update
  137.4 8.5 %psum.54 = f32[64,64]{1,0:T(8,128)S(1)} all-reduce(f32[64,64]{1,0:T(8,128)S(1)} %reduce_sum.59), channel_id=1, replica_groups=mesh['dp'=2,'cell'=4,'gene'=4] {'dp'}, use_global_device_ids=true, to_apply=%region_11.12 | all-reduce | flops 4096 | bytes 32768 | tf_op jit(solution)/shard_map/psum | solution.py:77
  145.9 19.5 %all-reduce.11.cloned.1.call-done = (f32[64,1000]{1,0:T(8,128)}, f32[64,1000]{1,0:T(8,128)}) async-done(((f32[64,1000]{1,0:T(8,128)}, f32[64,1000]{1,0:T(8,128)}), (f32[64,1000]{1,0:T(8,128)}, f32[64,1000]{1,0:T(8,128)})) %all-reduce.11.cloned.1.call-update) | async-done | bytes 512016 | tf_op jit(solution)/shard_map/psum | solution.py:77
  165.4 1.6 fusion.20
  167.1 1.4 fusion.19
  168.5 1.1 fusion.18
  (21 shorter events, 0.1 us)
Async XLA Ops:
  7.2 3.3 %copy-start = (bf16[1000,1024]{1,0:T(8,128)(2,1)S(1)}, bf16[1000,1024]{1,0:T(8,128)(2,1)}, u32[]{:S(2)}) copy-start(bf16[1000,1024]{1,0:T(8,128)(2,1)} %param.6) | copy-start | bytes 6144004
  7.2 1.9 %copy-start.1 = (f32[5,64,1000]{2,1,0:T(8,128)S(1)}, f32[5,64,1000]{2,1,0:T(8,128)}, u32[]{:S(2)}) copy-start(f32[5,64,1000]{2,1,0:T(8,128)} %param.9) | copy-start | bytes 3840004
  7.2 43.1 %all-reduce.7.cloned.1.call-start = ((), (), s32[]{:S(2)}) async-start(), calls=%async_computation | async-start | bytes 851968 | tf_op jit(solution)/shard_map/psum | solution.py:46
  9.0 1.3 copy-start.13
  9.0 1.3 copy-start.6
  12.6 2.1 %copy-start.14 = (s32[5]{0:T(128)S(1)}, s32[5]{0:T(128)}, u32[]{:S(2)}) copy-start(s32[5]{0:T(128)} %param.11) | copy-start | bytes 64
  14.6 112.2 %all-reduce.9.cloned.1.call-start = ((), (), s32[]{:S(2)}) async-start(), calls=%async_computation.1 | async-start | bytes 2949120 | tf_op jit(solution)/shard_map/psum | solution.py:67
  50.3 4.7 %copy-start.9 = (f32[64,1024]{1,0:T(8,128)S(1)}, f32[64,1024]{1,0:T(8,128)}, u32[]{:S(2)}) copy-start(f32[64,1024]{1,0:T(8,128)} %get-tuple-element.4) | copy-start | bytes 786436
  50.3 4.8 %copy-start.10 = (f32[64,1024]{1,0:T(8,128)S(1)}, f32[64,1024]{1,0:T(8,128)}, u32[]{:S(2)}) copy-start(f32[64,1024]{1,0:T(8,128)} %param.7) | copy-start | bytes 786436
  52.6 2.6 %copy-start.11 = (f32[5,64,64]{2,1,0:T(8,128)S(1)}, f32[5,64,64]{2,1,0:T(8,128)}, u32[]{:S(2)}) copy-start(f32[5,64,64]{2,1,0:T(8,128)} %get-tuple-element.3) | copy-start | bytes 245764
  56.5 2.0 %copy-start.12 = (f32[64,1024]{1,0:T(8,128)}, f32[64,1024]{1,0:T(8,128)S(1)}, u32[]{:S(2)}) copy-start(f32[64,1024]{1,0:T(8,128)S(1)} %divide_select_fusion) | copy-start | bytes 786436
  60.4 105.0 %all-reduce.11.cloned.1.call-start = ((), (), s32[]{:S(2)}) async-start(), calls=%async_computation.2 | async-start | bytes 1048576 | tf_op jit(solution)/shard_map/psum | solution.py:77
  126.8 2.3 %copy-start.2 = (f32[5,64,1000]{2,1,0:T(8,128)S(1)}, f32[5,64,1000]{2,1,0:T(8,128)}, u32[]{:S(2)}) copy-start(f32[5,64,1000]{2,1,0:T(8,128)} %get-tuple-element.6) | copy-start | bytes 3840004
  126.8 2.3 %copy-start.4 = (f32[5,64,64]{2,1,0:T(8,128)S(1)}, f32[5,64,64]{2,1,0:T(8,128)}, u32[]{:S(2)}) copy-start(f32[5,64,64]{2,1,0:T(8,128)} %get-tuple-element.5) | copy-start | bytes 245764
  133.7 1.1 copy-start.5
  134.8 1.7 copy-start.3
  165.4 3.1 %copy-start.7 = (f32[64,1000]{1,0:T(8,128)S(1)}, f32[64,1000]{1,0:T(8,128)}, u32[]{:S(2)}) copy-start(f32[64,1000]{1,0:T(8,128)} %get-tuple-element.7) | copy-start | bytes 768004
  165.4 3.1 %copy-start.8 = (f32[64,1000]{1,0:T(8,128)S(1)}, f32[64,1000]{1,0:T(8,128)}, u32[]{:S(2)}) copy-start(f32[64,1000]{1,0:T(8,128)} %get-tuple-element.8) | copy-start | bytes 768004
Sparse Core Ops, SparseCore 0:
  14.7 35.5 all-reduce.6
  60.6 66.2 all-reduce.8
  137.5 27.8 all-reduce.10
where the time goes:
time: 176 us
  waiting for transfers between devices  121 us (69%)
  matrix products  26.9 us (15%)
  between operations  14 us (8%)
  blocking collectives  8.54 us (5%)
  other arithmetic  3.58 us (2%)
    psum x1, waiting for transfers between devices, body(): stat_cross, stat_gram = lax.psum((cross_stat_part, gram_stat_part), 'cell')  66.2 us
    psum x1, waiting for transfers between devices, body(): cross_sum, gram_full = lax.psum((cross_part, gram_part), 'gene')  35.6 us
    psum x1, waiting for transfers between devices, body(): lax.psum((total_cross, total_gram, total_pull), 'dp')  19.5 us
    psum x1, blocking collectives, body(): lax.psum((total_cross, total_gram, total_pull), 'dp')  8.54 us
    dot_general x3, matrix products, body(): jnp.dot(gram_full.reshape(dataset_count * factor_rank, factor_rank), usag...  5.91 us
    dot_general x3, matrix products, body(): jnp.einsum('dkl,dlg->dkg', stat_gram, factor_now, precision=precise)  4.54 us
    dot_general x3, matrix products, shared_update(): jnp.dot(total_gram, shared_now, precision=precise) + total_pull  4.12 us
  transfers between devices with their start and end apart: 3, of which 3 were waited for; matrix products, arithmetic and copies ran while one was open for 0% of the time, Pallas kernels for 0%

commit v1 on v0

--- a/solution.py
+++ b/solution.py
@@ -1,13 +1,20 @@
+import functools
+
 import jax
 import jax.numpy as jnp
 from jax import lax
+from jax.experimental import pallas as pl
+from jax.experimental.pallas import tpu as pltpu
 from jax.sharding import PartitionSpec as P
 
 ITERS = 3
-
-
 penalty = 5.0
 precise = lax.Precision.HIGHEST
+f32 = jnp.float32
+bf16 = jnp.bfloat16
+
+GENE_TILE = 256
+VMEM = pl.BlockSpec(memory_space=pltpu.VMEM)
 
 
 def shared_update(shared_now, total_cross, total_gram, total_pull):
@@ -20,23 +27,19 @@
     return shared_now
 
 
-def body(expression, usage_init, shared_factor, dataset_factors, cell_dataset, dataset_sizes):
+def plain_body(expression, usage_init, shared_factor, dataset_factors, cell_dataset, dataset_sizes):
     dataset_count = dataset_factors.shape[0]
     factor_rank = shared_factor.shape[0]
     gene_count = shared_factor.shape[1]
     slot_count = expression.shape[1]
-    counted = dataset_sizes.astype(jnp.float32)
-    onehot = (cell_dataset[None, :] == jnp.arange(dataset_count, dtype=jnp.int32)[:, None]).astype(
-        jnp.float32
-    )
+    counted = dataset_sizes.astype(f32)
+    onehot = (cell_dataset[None, :] == jnp.arange(dataset_count, dtype=jnp.int32)[:, None]).astype(f32)
     alive_mask = cell_dataset < dataset_count
-    stacked_low = jnp.concatenate([shared_factor[None], dataset_factors], axis=0).astype(
-        jnp.bfloat16
-    )
+    stacked_low = jnp.concatenate([shared_factor[None], dataset_factors], axis=0).astype(bf16)
     products = jnp.dot(
         stacked_low.reshape((dataset_count + 1) * factor_rank, gene_count),
         expression,
-        preferred_element_type=jnp.float32,
+        preferred_element_type=f32,
     ).reshape(dataset_count + 1, factor_rank, slot_count)
     cross_part = products[0] + jnp.sum(onehot[:, None, :] * products[1:], axis=0)
     combined = shared_factor[None] + dataset_factors
@@ -55,9 +58,9 @@
         divisor = jnp.where(alive_mask[None, :], divisor, 1.0)
         usage_now = jnp.where(alive_mask[None, :], usage_now * cross_sum / divisor, usage_now)
     masked_usage = onehot[:, None, :] * usage_now[None]
-    low_usage = masked_usage.astype(jnp.bfloat16).reshape(dataset_count * factor_rank, slot_count)
+    low_usage = masked_usage.astype(bf16).reshape(dataset_count * factor_rank, slot_count)
     cross_stat_part = lax.dot_general(
-        low_usage, expression, (((1,), (1,)), ((), ())), preferred_element_type=jnp.float32
+        low_usage, expression, (((1,), (1,)), ((), ())), preferred_element_type=f32
     ).reshape(dataset_count, factor_rank, gene_count)
     cross_stat_part = cross_stat_part / counted[:, None, None]
     gram_stat_part = (
@@ -79,9 +82,383 @@
     return (usage_now, factor_now, shared_now)
 
 
+def halves(value):
+    high = value.astype(bf16)
+    low = (value - high.astype(f32)).astype(bf16)
+    return high, low
+
+
+def nt_dot(a, b):
+    return lax.dot_general(a, b, (((1,), (1,)), ((), ())), preferred_element_type=f32)
+
+
+def symmetric_product(high, low):
+    rank = high.shape[0]
+    both = nt_dot(high, jnp.concatenate([high, low], axis=0))
+    mixed = both[:, rank:]
+    return both[:, :rank] + mixed + mixed.T
+
+
+def left_cat(matrix):
+    high, low = halves(matrix)
+    return jnp.concatenate([high, low, high], axis=1)
+
+
+def right_cat(value):
+    high, low = halves(value)
+    return jnp.concatenate([high, high, low], axis=0)
+
+
+def pack_rows(blocks, groups):
+    rows = []
+    for b in range(groups):
+        other = blocks[b + groups] if b + groups < len(blocks) else jnp.zeros_like(blocks[b])
+        rows.append(jnp.concatenate([blocks[b], other], axis=1))
+    return jnp.concatenate(rows, axis=0)
+
+
+def unpack(packed, e, groups, rank):
+    row = (e % groups) * rank
+    lane = (e // groups) * rank
+    return packed[row : row + rank, lane : lane + rank]
+
+
+def gram_kernel(shared_ref, factors_ref, gram_ref, low_ref):
+    count, rank, genes = factors_ref.shape
+    shared = shared_ref[...]
+    low_ref[:rank, :] = shared.astype(bf16)
+    blocks = []
+    for e in range(count):
+        own = factors_ref[e]
+        own_high, own_low = halves(own)
+        low_ref[(e + 1) * rank : (e + 2) * rank, :] = own_high
+        both_high, both_low = halves(shared + own)
+        blocks.append(
+            symmetric_product(both_high, both_low) + penalty * symmetric_product(own_high, own_low)
+        )
+    gram_ref[...] = pack_rows(blocks, (count + 1) // 2)
+
+
+def cross_kernel(index_ref, low_ref, expression_ref, label_ref, send_ref, keep_ref):
+    step = pl.program_id(0)
+    rank = send_ref.shape[0]
+    count = low_ref.shape[0] // rank - 1
+    width = expression_ref.shape[1]
+    products = jnp.dot(low_ref[...], expression_ref[...], preferred_element_type=f32)
+    label = label_ref[...]
+    total = products[:rank]
+    for e in range(count):
+        total += jnp.where(label == e, products[(e + 1) * rank : (e + 2) * rank], 0.0)
+    tiles = send_ref.shape[1] // width
+    for t in range(tiles):
+        @pl.when(step == t)
+        def _():
+            send_ref[:, t * width : (t + 1) * width] = total
+
+        @pl.when(step == tiles + t)
+        def _():
+            keep_ref[:, t * width : (t + 1) * width] = total
+
+
+def usage_kernel(index_ref, own_ref, other_ref, gram_ref, more_ref, usage_ref, label_ref, out_ref):
+    rank = usage_ref.shape[0]
+    groups = gram_ref.shape[0] // rank
+    count = 2 * groups - 1
+    gram = gram_ref[...] + more_ref[...]
+    left = left_cat(jnp.concatenate([unpack(gram, e, groups, rank) for e in range(count)], axis=0))
+    cross = own_ref[...] + other_ref[...]
+    label = label_ref[...]
+    alive = label < count
+    usage = usage_ref[...]
+    for sweep in range(ITERS):
+        stacked = jnp.dot(left, right_cat(usage), preferred_element_type=f32)
+        divisor = jnp.where(alive, 0.0, 1.0)
+        for e in range(count):
+            divisor += jnp.where(label == e, stacked[e * rank : (e + 1) * rank], 0.0)
+        usage = jnp.where(alive, usage * cross / divisor, usage)
+    out_ref[...] = usage
+
+
+def stat_kernel(
+    index_ref, own_ref, other_ref, label_ref, expression_ref,
+    usage_ref, gram_ref, own_out, out1, out2, out3, low_ref,
+):
+    step = pl.program_id(0)
+    rank, half = own_ref.shape
+    count = low_ref.shape[0] // rank
+    groups = (count + 1) // 2
+
+    @pl.when(step == 0)
+    def _():
+        core = index_ref[0]
+        usage_ref[:, pl.ds(pl.multiple_of(core * half, half), half)] = own_ref[...]
+        usage_ref[:, pl.ds(pl.multiple_of((1 - core) * half, half), half)] = other_ref[...]
+        usage = usage_ref[...]
+        label = label_ref[...]
+        high, low = halves(usage)
+        right = jnp.concatenate([high, low], axis=0)
+        blocks = []
+        for e in range(count):
+            mask = label == e
+            masked = jnp.where(mask, high, jnp.zeros_like(high))
+            low_ref[e * rank : (e + 1) * rank, :] = masked
+            both = nt_dot(masked, right)
+            mixed = both[:, rank:]
+            blocks.append(both[:, :rank] + mixed + mixed.T)
+        gram_ref[...] = pack_rows(blocks, groups)
+
+    result = nt_dot(low_ref[...], expression_ref[...])
+    for t, ref in enumerate((out3, out2, out1, own_out)):
+        @pl.when(step == t)
+        def _():
+            ref[...] = result
+
+
+def factor_kernel(
+    index_ref, size_ref, cross0, cross1, cross2, cross3, gram_ref, shared_ref, factors_ref,
+    out_ref, total_ref,
+):
+    count, rank, width = factors_ref.shape
+    groups = (count + 1) // 2
+    gram = gram_ref[...]
+    shared = shared_ref[...]
+    total_cross = jnp.zeros((rank, width), f32)
+    total_pull = jnp.zeros((rank, width), f32)
+    for e in range(count):
+        rows = slice(e * rank, (e + 1) * rank)
+        cross = (cross0[rows, :] + cross1[rows, :]) + (cross2[rows, :] + cross3[rows, :])
+        cross = cross / size_ref[e].astype(f32)
+        left = left_cat(unpack(gram, e, groups, rank))
+        factor = factors_ref[e]
+        for sweep in range(ITERS):
+            divisor = jnp.dot(
+                left, right_cat(shared + (1.0 + penalty) * factor), preferred_element_type=f32
+            )
+            factor = factor * cross / divisor
+        out_ref[rows, :] = factor
+        total_cross += cross
+        total_pull += jnp.dot(left, right_cat(factor), preferred_element_type=f32)
+    total_ref[:rank, :] = total_cross
+    total_ref[rank:, :] = total_pull
+
+
+def gram_total_kernel(index_ref, size_ref, own_ref, other_ref, gram_ref, total_ref):
+    half = own_ref.shape[0]
+    rank = total_ref.shape[0]
+    groups = gram_ref.shape[0] // rank
+    count = 2 * groups - 1
+    core = index_ref[0]
+    gram_ref[pl.ds(pl.multiple_of(core * half, half), half), :] = own_ref[...]
+    gram_ref[pl.ds(pl.multiple_of((1 - core) * half, half), half), :] = other_ref[...]
+    total = jnp.zeros((rank, rank), f32)
+    for e in range(count):
+        row = (e % groups) * rank
+        lane = (e // groups) * rank
+        scaled = gram_ref[row : row + rank, lane : lane + rank] / size_ref[e].astype(f32)
+        gram_ref[row : row + rank, lane : lane + rank] = scaled
+        total += scaled
+    total_ref[...] = jnp.concatenate([total, jnp.zeros_like(total)], axis=1)
+
+
+def shared_kernel(index_ref, own_ref, other_ref, gram_own, gram_other, shared_ref, out_ref):
+    rank = shared_ref.shape[0]
+    total = own_ref[...] + other_ref[...]
+    left = left_cat((gram_own[...] + gram_other[...])[:, :rank])
+    shared = shared_ref[...]
+    for sweep in range(ITERS):
+        divisor = jnp.dot(left, right_cat(shared), preferred_element_type=f32) + total[rank:]
+        shared = shared * total[:rank] / divisor
+    out_ref[...] = shared
+
+
+def place_kernel(index_ref, f0, f1, f2, f3, s0, s1, s2, s3, factors_ref, shared_ref):
+    step = pl.program_id(0)
+    count, rank, width = factors_ref.shape
+    for t, (f, s) in enumerate(((f0, s0), (f1, s1), (f2, s2), (f3, s3))):
+        @pl.when(step == t)
+        def _():
+            factors_ref[...] = f[...].reshape(count, rank, width)
+            shared_ref[...] = s[...]
+
+
+def struct(*shape, dtype=f32):
+    return jax.ShapeDtypeStruct(shape, dtype)
+
+
+def whole(shape):
+    return pl.BlockSpec(shape, lambda *_: (0,) * len(shape))
+
+
+def call(kernel, index, args, in_specs, out_shape, out_specs, grid=(1,), scratch=(), cost=None):
+    return pl.pallas_call(
+        kernel,
+        grid_spec=pltpu.PrefetchScalarGridSpec(
+            num_scalar_prefetch=len(index),
+            grid=grid,
+            in_specs=in_specs,
+            out_specs=out_specs,
+            scratch_shapes=list(scratch),
+        ),
+        out_shape=out_shape,
+        compiler_params=pltpu.CompilerParams(vmem_limit_bytes=32 * 1024 * 1024),
+        cost_estimate=cost,
+    )(*index, *args)
+
+
+def cost(flops, moved):
+    return pl.CostEstimate(flops=int(flops), bytes_accessed=int(moved), transcendentals=0)
+
+
+def fast_body(expression, usage_init, shared_factor, dataset_factors, cell_dataset, dataset_sizes):
+    count, rank, genes = dataset_factors.shape
+    cells = expression.shape[1]
+    half = cells // 2
+    tile = GENE_TILE
+    groups = (count + 1) // 2
+    core = lax.axis_index("gene") % 2
+    depth = lax.axis_index("cell")
+    index = jnp.stack([core, depth]).astype(jnp.int32)
+    label = cell_dataset.reshape(1, cells)
+
+    def swap(value, axis, offset, size):
+        return lax.ppermute(value, axis, [(i, i ^ offset) for i in range(size)])
+
+    gram_part, low = pl.pallas_call(
+        gram_kernel,
+        in_specs=[VMEM, VMEM],
+        out_specs=[VMEM, VMEM],
+        out_shape=[struct(groups * rank, 2 * rank), struct((count + 1) * rank, genes, dtype=bf16)],
+        cost_estimate=cost(4 * 4 * count * rank * rank * genes, 8 * count * rank * genes),
+    )(shared_factor, dataset_factors)
+    gram_part = gram_part + swap(gram_part, "gene", 2, 4)
+    gram_more = swap(gram_part, "gene", 1, 4)
+
+    cell_tile = 256
+    tiles = half // cell_tile
+
+    def cell_block(i, idx):
+        other = i // tiles == 0
+        which = jnp.where(other, 1 - idx[0], idx[0])
+        return which * tiles + i % tiles
+
+    send, keep = call(
+        cross_kernel,
+        (index,),
+        (low, expression, label),
+        [
+            whole(low.shape),
+            pl.BlockSpec((genes, cell_tile), lambda i, idx: (0, cell_block(i, idx))),
+            pl.BlockSpec((1, cell_tile), lambda i, idx: (0, cell_block(i, idx))),
+        ],
+        [struct(rank, half), struct(rank, half)],
+        [whole((rank, half)), whole((rank, half))],
+        grid=(2 * tiles,),
+        cost=cost(2 * low.shape[0] * genes * cells, 2 * genes * cells),
+    )
+    cross = keep + swap(send, "gene", 1, 4)
+    cross_more = swap(cross, "gene", 2, 4)
+
+    usage_half = call(
+        usage_kernel,
+        (index,),
+        (cross, cross_more, gram_part, gram_more, usage_init, label),
+        [
+            whole(cross.shape),
+            whole(cross.shape),
+            whole(gram_part.shape),
+            whole(gram_part.shape),
+            pl.BlockSpec((rank, half), lambda i, idx: (0, idx[0])),
+            pl.BlockSpec((1, half), lambda i, idx: (0, idx[0])),
+        ],
+        struct(rank, half),
+        whole((rank, half)),
+        cost=cost(2 * ITERS * 3 * count * rank * rank * half, 16 * rank * half),
+    )
+    usage_other = swap(usage_half, "gene", 1, 4)
+
+    rows = count * rank
+    usage, stat_gram, part0, part1, part2, part3 = call(
+        stat_kernel,
+        (index,),
+        (usage_half, usage_other, label, expression),
+        [
+            whole((rank, half)),
+            whole((rank, half)),
+            whole((1, cells)),
+            pl.BlockSpec((tile, cells), lambda i, idx: (idx[1] ^ (3 - i), 0)),
+        ],
+        [struct(rank, cells), struct(groups * rank, 2 * rank)] + [struct(rows, tile)] * 4,
+        [whole((rank, cells)), whole((groups * rank, 2 * rank))] + [whole((rows, tile))] * 4,
+        grid=(4,),
+        scratch=[pltpu.VMEM((rows, cells), bf16)],
+        cost=cost(2 * rows * genes * cells, 2 * genes * cells),
+    )
+
+    got3 = swap(part3, "cell", 3, 4)
+    got2 = swap(part2, "cell", 2, 4)
+    got1 = swap(part1, "cell", 1, 4)
+    gram_rows = groups * rank // 2
+    gram_half = lax.dynamic_slice_in_dim(stat_gram, core * gram_rows, gram_rows, 0)
+    gram_half = gram_half + swap(gram_half, "cell", 1, 4)
+    gram_half = gram_half + swap(gram_half, "cell", 2, 4)
+    gram_next = swap(gram_half, "gene", 1, 4)
+    gram_scaled, gram_total = call(
+        gram_total_kernel,
+        (index, dataset_sizes),
+        (gram_half, gram_next),
+        [whole((gram_rows, 2 * rank))] * 2,
+        [struct(groups * rank, 2 * rank), struct(rank, 2 * rank)],
+        [whole((groups * rank, 2 * rank)), whole((rank, 2 * rank))],
+    )
+    gram_total_other = swap(gram_total, "dp", 1, 2)
+
+    gene_block = pl.BlockSpec((rank, tile), lambda i, idx, *_: (0, idx[1]))
+    own_factor, total = call(
+        factor_kernel,
+        (index, dataset_sizes),
+        (part0, got1, got2, got3, gram_scaled, shared_factor, dataset_factors),
+        [whole((rows, tile))] * 4
+        + [
+            whole((groups * rank, 2 * rank)),
+            gene_block,
+            pl.BlockSpec((count, rank, tile), lambda i, idx, *_: (0, 0, idx[1])),
+        ],
+        [struct(rows, tile), struct(2 * rank, tile)],
+        [whole((rows, tile)), whole((2 * rank, tile))],
+        cost=cost(2 * 4 * 3 * rows * rank * tile, 6 * 4 * rows * tile),
+    )
+    total_other = swap(total, "dp", 1, 2)
+    factors = [own_factor] + [swap(own_factor, "cell", d, 4) for d in (1, 2, 3)]
+    own_shared = call(
+        shared_kernel,
+        (index,),
+        (total, total_other, gram_total, gram_total_other, shared_factor),
+        [whole((2 * rank, tile))] * 2 + [whole((rank, 2 * rank))] * 2 + [gene_block],
+        struct(rank, tile),
+        whole((rank, tile)),
+        cost=cost(2 * 3 * 3 * rank * rank * tile, 6 * 4 * rank * tile),
+    )
+    shareds = [own_shared] + [swap(own_shared, "cell", d, 4) for d in (1, 2, 3)]
+    new_factors, new_shared = call(
+        place_kernel,
+        (index,),
+        (*factors, *shareds),
+        [whole((rows, tile))] * 4 + [whole((rank, tile))] * 4,
+        [struct(count, rank, genes), struct(rank, genes)],
+        [
+            pl.BlockSpec((count, rank, tile), lambda i, idx: (0, 0, idx[1] ^ i)),
+            pl.BlockSpec((rank, tile), lambda i, idx: (0, idx[1] ^ i)),
+        ],
+        grid=(4,),
+        cost=cost(0, 8 * rows * genes),
+    )
+    return usage, new_factors, new_shared
+
+
 def solution(mesh):
+    sizes = (mesh.shape["dp"], mesh.shape["cell"], mesh.shape["gene"])
     return jax.shard_map(
-        body,
+        fast_body if sizes == (2, 4, 4) else plain_body,
         mesh=mesh,
         in_specs=(
             P("gene", ("dp", "cell")),

time: 176 us -> 106 us (0.60)
  waiting for transfers between devices: 121 us -> 54 us
  starting transfers between devices: 0.3 us -> 31.2 us
  matrix products: 26.9 us -> 0 us
  Pallas kernels: 0 us -> 17 us
  between operations: 14 us -> 0.82 us
  blocking collectives: 8.54 us -> 0 us
  other arithmetic: 3.58 us -> 0.12 us
    psum x3 -> x0, waiting for transfers between devices: 121 us -> none  [the longest x1 66.2 us: body(): stat_cross, stat_gram = lax.psum((cross_stat_part, gram_stat_part), 'cell')]
    ppermute x0 -> x19, waiting for transfers between devices: none -> 54 us  [swap(): return lax.ppermute(value, axis, [(i, i ^ offset) for i in range(size)])]
    ppermute x0 -> x19, starting transfers between devices: none -> 31.2 us  [swap(): return lax.ppermute(value, axis, [(i, i ^ offset) for i in range(size)])]
    dot_general x16 -> x0, matrix products: 26.9 us -> none  [the longest x3 5.91 us: body(): jnp.dot(gram_full.reshape(dataset_count * factor_rank, factor_rank), usag...]
    pallas_call x0 -> x8, Pallas kernels: none -> 17 us  [the longest x7 13.7 us: call(): pl.pallas_call(kernel, grid_spec=pltpu.PrefetchScalarGridSpec(num_scalar_...]
    psum x1 -> x0, blocking collectives: 8.54 us -> none  [body(): lax.psum((total_cross, total_gram, total_pull), 'dp')]
  transfers between devices with their start and end apart: 3 -> 19, of which waited for: 3 -> 10; matrix products, arithmetic and copies ran while one was open for 0% -> 0% of each run, Pallas kernels for 0% -> 2%
where the time goes in v1:
time: 106 us
  waiting for transfers between devices  54 us (51%)
  starting transfers between devices  31.2 us (29%)
  Pallas kernels  17 us (16%)
  local copies, waits for them, and re-layouts  2.75 us (3%)
    ppermute x19, waiting for transfers between devices, swap(): return lax.ppermute(value, axis, [(i, i ^ offset) for i in range(size)])  54 us
    ppermute x19, starting transfers between devices, swap(): return lax.ppermute(value, axis, [(i, i ^ offset) for i in range(size)])  31.2 us
    pallas_call x7, Pallas kernels, call(): pl.pallas_call(kernel, grid_spec=pltpu.PrefetchScalarGridSpec(num_scalar_...  13.7 us
    pallas_call x1, Pallas kernels, fast_body(): pl.pallas_call(gram_kernel, in_specs=[VMEM, VMEM], out_specs=[VMEM, VMEM]...  3.32 us
    unnamed x18, local copies, waits for them, and re-layouts  2.74 us
  transfers between devices with their start and end apart: 19, of which 10 were waited for; matrix products, arithmetic and copies ran while one was open for 0% of the time, Pallas kernels for 2%

profile of v1, /device:TPU:0, one launch (start us, length us, event | category | flops | bytes accessed | tf_op | source)
XLA Modules:
  0.0 105.9 jit_solution(4569281411772448361)
XLA Ops:
  0.7 0.1 pad_add_fusion.index_ref
  0.7 3.3 %shard_map.85 = (f32[192,128]{1,0:T(8,128)}, bf16[384,1000]{1,0:T(8,128)(2,1)}) custom-call(f32[64,1000]{1,0:T(8,128)} %shared_ref.5, f32[5,64,1000]{2,1,0:T(8,128)} %factors_ref.3), custom_call_target="tpu_custom_call" | custom-call | flops 327680000 | bytes 2560000 | tf_op jit(solution)/shard_map/pallas_call | solution.py:326
  4.1 1.6 %copy-done.5 = bf16[1000,1024]{1,0:T(8,128)(2,1)S(1)} copy-done((bf16[1000,1024]{1,0:T(8,128)(2,1)S(1)}, bf16[1000,1024]{1,0:T(8,128)(2,1)}, u32[]{:S(2)}) %copy-start.5) | copy-done | bytes 2048024
  5.6 1.1 %copy-done.7 = bf16[384,1000]{1,0:T(8,128)(2,1)S(1)} copy-done((bf16[384,1000]{1,0:T(8,128)(2,1)S(1)}, bf16[384,1000]{1,0:T(8,128)(2,1)}, u32[]{:S(2)}) %copy-start.7) | copy-done | bytes 768024
  6.8 2.5 %shard_map.86 = (f32[64,512]{1,0:T(8,128)S(1)}, f32[64,512]{1,0:T(8,128)S(1)}) custom-call(s32[2]{0:T(128)S(1)} %pad_add_fusion.index_ref, bf16[384,1000]{1,0:T(8,128)(2,1)S(1)} %copy-done.7, bf16[1000,1024]{1,0:T(8,128)(2,1)S(1)} %copy-done.5, s32[1,1024]{1,0:T(1,128)S(1)} %bitcast.3), custom_call_target="tpu_custom_call" | custom-call | flops 786432000 | bytes 2048000 | tf_op jit(solution)/shard_map/pallas_call | solution.py:293
  9.3 0.5 collective-permute-start
  9.8 2.6 %collective-permute-start.2 = (f32[192,128]{1,0:T(8,128)S(1)}, f32[192,128]{1,0:T(8,128)S(1)}, u32[]{:S(2)}, u32[]{:S(2)}) collective-permute-start(f32[192,128]{1,0:T(8,128)S(1)} %copy-done.8), channel_id=1, source_target_pairs={{0,2},{1,3},{2,0},{3,1},{4,6},{5,7},{6,4},{7,5},{8,10},{9,11},{10,... | collective-permute-start | bytes 294920 | tf_op jit(solution)/shard_map/ppermute | solution.py:324
  12.4 1.3 %collective-permute-start.1 = (f32[64,512]{1,0:T(8,128)S(1)}, f32[64,512]{1,0:T(8,128)S(1)}, u32[]{:S(2)}, u32[]{:S(2)}) collective-permute-start(f32[64,512]{1,0:T(8,128)S(1)} %add.20.own_ref), channel_id=1, source_target_pairs={{0,2},{1,3},{2,0},{3,1},{4,6},{5,7},{6,4},{7,5},{8,10},{9,11},{10,... | collective-permute-start | bytes 393224 | tf_op jit(solution)/shard_map/ppermute | solution.py:324
  13.7 2.3 %collective-permute-done.2 = f32[192,128]{1,0:T(8,128)S(1)} collective-permute-done((f32[192,128]{1,0:T(8,128)S(1)}, f32[192,128]{1,0:T(8,128)S(1)}, u32[]{:S(2)}, u32[]{:S(2)}) %collective-permute-start.2) | collective-permute-done | bytes 98336 | tf_op jit(solution)/shard_map/ppermute | solution.py:324
  16.1 0.1 collective-permute-start.3
  16.1 1.3 %collective-permute-done.3.more_ref = f32[192,128]{1,0:T(8,128)S(1)} collective-permute-done((f32[192,128]{1,0:T(8,128)S(1)}, f32[192,128]{1,0:T(8,128)S(1)}, u32[]{:S(2)}, u32[]{:S(2)}) %collective-permute-start.3) | collective-permute-done | bytes 98336 | tf_op jit(solution)/shard_map/ppermute | solution.py:324
  17.4 1.2 %collective-permute-done.1.other_ref = f32[64,512]{1,0:T(8,128)S(1)} collective-permute-done((f32[64,512]{1,0:T(8,128)S(1)}, f32[64,512]{1,0:T(8,128)S(1)}, u32[]{:S(2)}, u32[]{:S(2)}) %collective-permute-start.1) | collective-permute-done | bytes 131104 | tf_op jit(solution)/shard_map/ppermute | solution.py:324
  18.6 1.4 %shard_map.87.own_ref = f32[64,512]{1,0:T(8,128)S(1)} custom-call(s32[2]{0:T(128)S(1)} %pad_add_fusion.index_ref, f32[64,512]{1,0:T(8,128)S(1)} %add.20.own_ref, f32[64,512]{1,0:T(8,128)S(1)} %collective-permute-done.1.other_ref, f32[192,128]{1,0:T(8,128)S(1)} %add.21.gram_ref, f32[192,128]{1,0:T(8,128)S(1)} %collective-permute-done.3.more_ref, ...), custom_call_target="tpu_custom_call" | custom-call | flops 188743680 | bytes 524288 | tf_op jit(solution)/shard_map/pallas_call | solution.py:293
  20.0 0.1 collective-permute-start.4
  20.1 0.0 copy-start.4
  20.1 0.0 copy-start
  20.1 0.0 copy-start.1
  20.1 1.3 %collective-permute-done.4.other_ref = f32[64,512]{1,0:T(8,128)S(1)} collective-permute-done((f32[64,512]{1,0:T(8,128)S(1)}, f32[64,512]{1,0:T(8,128)S(1)}, u32[]{:S(2)}, u32[]{:S(2)}) %collective-permute-start.4) | collective-permute-done | bytes 131104 | tf_op jit(solution)/shard_map/ppermute | solution.py:324
  21.4 3.7 %shard_map.88 = (f32[64,1024]{1,0:T(8,128)}, f32[192,128]{1,0:T(8,128)S(1)}, f32[320,256]{1,0:T(8,128)S(1)}, f32[320,256]{1,0:T(8,128)S(1)}, f32[320,256]{1,0:T(8,128)S(1)}, /*index=5*/f32[320,256]{1,0:T(8,128)S(1)}) custom-call(s32[2]{0:T(128)S(1)} %pad_add_fusion.index_ref, f32[64,512]{1,0:T(8,128)S(1)} %shard_map.87.own_ref, ...), custom_call_target="tpu_custom_call" | custom-call | flops 655360000 | bytes 2048000 | tf_op jit(solution)/shard_map/pallas_call | solution.py:293
  25.1 1.8 %collective-permute-start.8 = (f32[96,128]{1,0:T(8,128)S(1)}, f32[96,128]{1,0:T(8,128)S(1)}, u32[]{:S(2)}, u32[]{:S(2)}) collective-permute-start(f32[96,128]{1,0:T(8,128)S(1)} %constant_dynamic-slice_fusion), channel_id=1, source_target_pairs={{0,4},{4,0},{8,12},{12,8},{1,5},{5,1},{9,13},{13,9},{2,6},{6,2},{1... | collective-permute-start | bytes 147464 | tf_op jit(solution)/shard_map/ppermute | solution.py:324
  27.0 0.2 collective-permute-start.5
  27.1 2.9 %collective-permute-start.6 = (f32[320,256]{1,0:T(8,128)S(1)}, f32[320,256]{1,0:T(8,128)S(1)}, u32[]{:S(2)}, u32[]{:S(2)}) collective-permute-start(f32[320,256]{1,0:T(8,128)S(1)} %get-tuple-element.26), channel_id=1, source_target_pairs={{0,8},{4,12},{8,0},{12,4},{1,9},{5,13},{9,1},{13,5},{2,10},{6,14},... | collective-permute-start | bytes 983048 | tf_op jit(solution)/shard_map/ppermute | solution.py:324
  30.0 1.3 %collective-permute-start.7 = (f32[320,256]{1,0:T(8,128)S(1)}, f32[320,256]{1,0:T(8,128)S(1)}, u32[]{:S(2)}, u32[]{:S(2)}) collective-permute-start(f32[320,256]{1,0:T(8,128)S(1)} %get-tuple-element.27), channel_id=1, source_target_pairs={{0,12},{4,8},{8,4},{12,0},{1,13},{5,9},{9,5},{13,1},{2,14},{6,10},... | collective-permute-start | bytes 983048 | tf_op jit(solution)/shard_map/ppermute | solution.py:324
  31.3 0.0 collective-permute-done.8
  31.4 1.8 %collective-permute-start.9 = (f32[96,128]{1,0:T(8,128)S(1)}, f32[96,128]{1,0:T(8,128)S(1)}, u32[]{:S(2)}, u32[]{:S(2)}) collective-permute-start(f32[96,128]{1,0:T(8,128)S(1)} %fusion), channel_id=1, source_target_pairs={{0,8},{4,12},{8,0},{12,4},{1,9},{5,13},{9,1},{13,5},{2,10},{6,14},... | collective-permute-start | bytes 147464 | tf_op jit(solution)/shard_map/ppermute | solution.py:324
  33.1 27.6 %collective-permute-done.9 = f32[96,128]{1,0:T(8,128)S(1)} collective-permute-done((f32[96,128]{1,0:T(8,128)S(1)}, f32[96,128]{1,0:T(8,128)S(1)}, u32[]{:S(2)}, u32[]{:S(2)}) %collective-permute-start.9) | collective-permute-done | bytes 49184 | tf_op jit(solution)/shard_map/ppermute | solution.py:324
  60.7 0.1 collective-permute-start.10
  60.8 1.2 %collective-permute-done.10.other_ref = f32[96,128]{1,0:T(8,128)S(1)} collective-permute-done((f32[96,128]{1,0:T(8,128)S(1)}, f32[96,128]{1,0:T(8,128)S(1)}, u32[]{:S(2)}, u32[]{:S(2)}) %collective-permute-start.10) | collective-permute-done | bytes 49184 | tf_op jit(solution)/shard_map/ppermute | solution.py:324
  62.0 0.6 shard_map.89
  62.6 0.0 collective-permute-done.5.cross1
  62.6 0.0 collective-permute-done.7.cross3
  62.7 2.1 %shard_map.90 = (f32[320,256]{1,0:T(8,128)S(1)}, f32[128,256]{1,0:T(8,128)S(1)}) custom-call(s32[2]{0:T(128)S(1)} %pad_add_fusion.index_ref, s32[5]{0:T(128)S(1)} %copy-done.4, f32[320,256]{1,0:T(8,128)S(1)} %get-tuple-element.24.cross0, f32[320,256]{1,0:T(8,128)S(1)} %collective-permute-done.5.cross1, f32[320,256]{1,0:T(8,128)S(1)} %collective-permute-done.6.cross2, ...), custom_call_target="tpu_custom_call" | custom-call | flops 125829120 | bytes 1966080 | tf_op jit(solution)/shard_map/pallas_call | solution.py:293
  64.8 3.7 %collective-permute-start.13 = (f32[320,256]{1,0:T(8,128)S(1)}, f32[320,256]{1,0:T(8,128)S(1)}, u32[]{:S(2)}, u32[]{:S(2)}) collective-permute-start(f32[320,256]{1,0:T(8,128)S(1)} %get-tuple-element.30.f0), channel_id=1, source_target_pairs={{0,12},{4,8},{8,4},{12,0},{1,13},{5,9},{9,5},{13,1},{2,14},{6,10},... | collective-permute-start | bytes 983048 | tf_op jit(solution)/shard_map/ppermute | solution.py:324
  68.5 0.0 collective-permute-start.12
  68.5 0.7 collective-permute-start.11
  69.3 1.6 %collective-permute-start.14 = (f32[128,256]{1,0:T(8,128)S(1)}, f32[128,256]{1,0:T(8,128)S(1)}, u32[]{:S(2)}, u32[]{:S(2)}) collective-permute-start(f32[128,256]{1,0:T(8,128)S(1)} %get-tuple-element.31.own_ref), channel_id=1, source_target_pairs={{0,16},{16,0},{1,17},{17,1},{2,18},{18,2},{3,19},{19,3},{4,20},{20... | collective-permute-start | bytes 393224 | tf_op jit(solution)/shard_map/ppermute | solution.py:324
  70.8 0.5 collective-permute-start.15
  71.3 3.6 %collective-permute-done.15.gram_other = f32[64,128]{1,0:T(8,128)S(1)} collective-permute-done((f32[64,128]{1,0:T(8,128)S(1)}, f32[64,128]{1,0:T(8,128)S(1)}, u32[]{:S(2)}, u32[]{:S(2)}) %collective-permute-start.15) | collective-permute-done | bytes 32800 | tf_op jit(solution)/shard_map/ppermute | solution.py:324
  74.9 0.0 collective-permute-done.14.other_ref
  74.9 1.1 shard_map.91.s0
  75.9 3.5 %collective-permute-start.18 = (f32[64,256]{1,0:T(8,128)S(1)}, f32[64,256]{1,0:T(8,128)S(1)}, u32[]{:S(2)}, u32[]{:S(2)}) collective-permute-start(f32[64,256]{1,0:T(8,128)S(1)} %shard_map.91.s0), channel_id=1, source_target_pairs={{0,12},{4,8},{8,4},{12,0},{1,13},{5,9},{9,5},{13,1},{2,14},{6,10},... | collective-permute-start | bytes 196616 | tf_op jit(solution)/shard_map/ppermute | solution.py:324
  79.5 0.0 collective-permute-start.17
  79.5 13.4 %collective-permute-done.18.s3 = f32[64,256]{1,0:T(8,128)S(1)} collective-permute-done((f32[64,256]{1,0:T(8,128)S(1)}, f32[64,256]{1,0:T(8,128)S(1)}, u32[]{:S(2)}, u32[]{:S(2)}) %collective-permute-start.18) | collective-permute-done | bytes 65568 | tf_op jit(solution)/shard_map/ppermute | solution.py:324
  92.9 8.6 %collective-permute-start.16 = (f32[64,256]{1,0:T(8,128)S(1)}, f32[64,256]{1,0:T(8,128)S(1)}, u32[]{:S(2)}, u32[]{:S(2)}) collective-permute-start(f32[64,256]{1,0:T(8,128)S(1)} %shard_map.91.s0), channel_id=1, source_target_pairs={{0,4},{4,0},{8,12},{12,8},{1,5},{5,1},{9,13},{13,9},{2,6},{6,2},{1... | collective-permute-start | bytes 196616 | tf_op jit(solution)/shard_map/ppermute | solution.py:324
  101.4 0.2 collective-permute-done.17.s2
  101.7 2.0 %collective-permute-done.16.s1 = f32[64,256]{1,0:T(8,128)S(1)} collective-permute-done((f32[64,256]{1,0:T(8,128)S(1)}, f32[64,256]{1,0:T(8,128)S(1)}, u32[]{:S(2)}, u32[]{:S(2)}) %collective-permute-start.16) | collective-permute-done | bytes 65568 | tf_op jit(solution)/shard_map/ppermute | solution.py:324
  103.7 0.0 collective-permute-done.11.f1
  103.7 2.3 %shard_map.92 = (f32[5,64,1000]{2,1,0:T(8,128)}, f32[64,1000]{1,0:T(8,128)}) custom-call(s32[2]{0:T(128)S(1)} %pad_add_fusion.index_ref, f32[320,256]{1,0:T(8,128)S(1)} %get-tuple-element.30.f0, f32[320,256]{1,0:T(8,128)S(1)} %collective-permute-done.11.f1, f32[320,256]{1,0:T(8,128)S(1)} %collective-permute-done.12.f2, ...), custom_call_target="tpu_custom_call" | custom-call | bytes 2560000 | tf_op jit(solution)/shard_map/pallas_call | solution.py:293
  (22 shorter events, 0.1 us)
Async XLA Ops:
  0.6 3.4 %copy-start.3 = (s32[1024]{0:T(1024)S(1)}, s32[1024]{0:T(1024)}, u32[]{:S(2)}) copy-start(s32[1024]{0:T(1024)} %param.10) | copy-start | bytes 12292
  4.1 1.6 %copy-start.5 = (bf16[1000,1024]{1,0:T(8,128)(2,1)S(1)}, bf16[1000,1024]{1,0:T(8,128)(2,1)}, u32[]{:S(2)}) copy-start(bf16[1000,1024]{1,0:T(8,128)(2,1)} %expression_ref.3) | copy-start | bytes 6144004
  5.6 1.1 %copy-start.7 = (bf16[384,1000]{1,0:T(8,128)(2,1)S(1)}, bf16[384,1000]{1,0:T(8,128)(2,1)}, u32[]{:S(2)}) copy-start(bf16[384,1000]{1,0:T(8,128)(2,1)} %get-tuple-element.19.low_ref) | copy-start | bytes 2304004
  6.8 3.1 %copy-start.8 = (f32[192,128]{1,0:T(8,128)S(1)}, f32[192,128]{1,0:T(8,128)}, u32[]{:S(2)}) copy-start(f32[192,128]{1,0:T(8,128)} %get-tuple-element.22) | copy-start | bytes 294916
  6.8 11.8 %copy-start.2 = (f32[64,1024]{1,0:T(8,128)S(1)}, f32[64,1024]{1,0:T(8,128)}, u32[]{:S(2)}) copy-start(f32[64,1024]{1,0:T(8,128)} %usage_ref.1) | copy-start | bytes 786436
  6.8 14.6 %copy-start.6 = (bf16[1000,1024]{1,0:T(8,128)(2,1)S(1)}, bf16[1000,1024]{1,0:T(8,128)(2,1)}, u32[]{:S(2)}) copy-start(bf16[1000,1024]{1,0:T(8,128)(2,1)} %expression_ref.3) | copy-start | bytes 6144004
  9.3 3.1 %collective-permute-start = (f32[64,512]{1,0:T(8,128)S(1)}, f32[64,512]{1,0:T(8,128)S(1)}, u32[]{:S(2)}, u32[]{:S(2)}) collective-permute-start(f32[64,512]{1,0:T(8,128)S(1)} %get-tuple-element.21), channel_id=1, source_target_pairs={{0,1},{1,0},{2,3},{3,2},{4,5},{5,4},{6,7},{7,6},{8,9},{9,8},{10,11... | collective-permute-start | bytes 393224 | tf_op jit(solution)/shard_map/ppermute | solution.py:324
  9.8 6.2 %collective-permute-start.2 = (f32[192,128]{1,0:T(8,128)S(1)}, f32[192,128]{1,0:T(8,128)S(1)}, u32[]{:S(2)}, u32[]{:S(2)}) collective-permute-start(f32[192,128]{1,0:T(8,128)S(1)} %copy-done.8), channel_id=1, source_target_pairs={{0,2},{1,3},{2,0},{3,1},{4,6},{5,7},{6,4},{7,5},{8,10},{9,11},{10,... | collective-permute-start | bytes 294920 | tf_op jit(solution)/shard_map/ppermute | solution.py:324
  12.4 6.2 %collective-permute-start.1 = (f32[64,512]{1,0:T(8,128)S(1)}, f32[64,512]{1,0:T(8,128)S(1)}, u32[]{:S(2)}, u32[]{:S(2)}) collective-permute-start(f32[64,512]{1,0:T(8,128)S(1)} %add.20.own_ref), channel_id=1, source_target_pairs={{0,2},{1,3},{2,0},{3,1},{4,6},{5,7},{6,4},{7,5},{8,10},{9,11},{10,... | collective-permute-start | bytes 393224 | tf_op jit(solution)/shard_map/ppermute | solution.py:324
  16.1 1.4 %collective-permute-start.3 = (f32[192,128]{1,0:T(8,128)S(1)}, f32[192,128]{1,0:T(8,128)S(1)}, u32[]{:S(2)}, u32[]{:S(2)}) collective-permute-start(f32[192,128]{1,0:T(8,128)S(1)} %add.21.gram_ref), channel_id=1, source_target_pairs={{0,1},{1,0},{2,3},{3,2},{4,5},{5,4},{6,7},{7,6},{8,9},{9,8},{10,11... | collective-permute-start | bytes 294920 | tf_op jit(solution)/shard_map/ppermute | solution.py:324
  20.0 1.4 %collective-permute-start.4 = (f32[64,512]{1,0:T(8,128)S(1)}, f32[64,512]{1,0:T(8,128)S(1)}, u32[]{:S(2)}, u32[]{:S(2)}) collective-permute-start(f32[64,512]{1,0:T(8,128)S(1)} %shard_map.87.own_ref), channel_id=1, source_target_pairs={{0,1},{1,0},{2,3},{3,2},{4,5},{5,4},{6,7},{7,6},{8,9},{9,8},{10,11... | collective-permute-start | bytes 393224 | tf_op jit(solution)/shard_map/ppermute | solution.py:324
  20.1 41.9 %copy-start.4 = (s32[5]{0:T(128)S(1)}, s32[5]{0:T(128)}, u32[]{:S(2)}) copy-start(s32[5]{0:T(128)} %size_ref.3) | copy-start | bytes 64
  20.1 42.6 %copy-start = (f32[5,64,1000]{2,1,0:T(8,128)S(1)}, f32[5,64,1000]{2,1,0:T(8,128)}, u32[]{:S(2)}) copy-start(f32[5,64,1000]{2,1,0:T(8,128)} %factors_ref.3) | copy-start | bytes 3840004
  20.1 42.6 %copy-start.1 = (f32[64,1000]{1,0:T(8,128)S(1)}, f32[64,1000]{1,0:T(8,128)}, u32[]{:S(2)}) copy-start(f32[64,1000]{1,0:T(8,128)} %shared_ref.5) | copy-start | bytes 768004
  25.1 6.2 %collective-permute-start.8 = (f32[96,128]{1,0:T(8,128)S(1)}, f32[96,128]{1,0:T(8,128)S(1)}, u32[]{:S(2)}, u32[]{:S(2)}) collective-permute-start(f32[96,128]{1,0:T(8,128)S(1)} %constant_dynamic-slice_fusion), channel_id=1, source_target_pairs={{0,4},{4,0},{8,12},{12,8},{1,5},{5,1},{9,13},{13,9},{2,6},{6,2},{1... | collective-permute-start | bytes 147464 | tf_op jit(solution)/shard_map/ppermute | solution.py:324
  27.0 35.7 %collective-permute-start.5 = (f32[320,256]{1,0:T(8,128)S(1)}, f32[320,256]{1,0:T(8,128)S(1)}, u32[]{:S(2)}, u32[]{:S(2)}) collective-permute-start(f32[320,256]{1,0:T(8,128)S(1)} %get-tuple-element.25), channel_id=1, source_target_pairs={{0,4},{4,0},{8,12},{12,8},{1,5},{5,1},{9,13},{13,9},{2,6},{6,2},{1... | collective-permute-start | bytes 983048 | tf_op jit(solution)/shard_map/ppermute | solution.py:324
  27.1 35.5 %collective-permute-start.6 = (f32[320,256]{1,0:T(8,128)S(1)}, f32[320,256]{1,0:T(8,128)S(1)}, u32[]{:S(2)}, u32[]{:S(2)}) collective-permute-start(f32[320,256]{1,0:T(8,128)S(1)} %get-tuple-element.26), channel_id=1, source_target_pairs={{0,8},{4,12},{8,0},{12,4},{1,9},{5,13},{9,1},{13,5},{2,10},{6,14},... | collective-permute-start | bytes 983048 | tf_op jit(solution)/shard_map/ppermute | solution.py:324
  30.0 32.7 %collective-permute-start.7 = (f32[320,256]{1,0:T(8,128)S(1)}, f32[320,256]{1,0:T(8,128)S(1)}, u32[]{:S(2)}, u32[]{:S(2)}) collective-permute-start(f32[320,256]{1,0:T(8,128)S(1)} %get-tuple-element.27), channel_id=1, source_target_pairs={{0,12},{4,8},{8,4},{12,0},{1,13},{5,9},{9,5},{13,1},{2,14},{6,10},... | collective-permute-start | bytes 983048 | tf_op jit(solution)/shard_map/ppermute | solution.py:324
  31.4 29.3 %collective-permute-start.9 = (f32[96,128]{1,0:T(8,128)S(1)}, f32[96,128]{1,0:T(8,128)S(1)}, u32[]{:S(2)}, u32[]{:S(2)}) collective-permute-start(f32[96,128]{1,0:T(8,128)S(1)} %fusion), channel_id=1, source_target_pairs={{0,8},{4,12},{8,0},{12,4},{1,9},{5,13},{9,1},{13,5},{2,10},{6,14},... | collective-permute-start | bytes 147464 | tf_op jit(solution)/shard_map/ppermute | solution.py:324
  60.7 1.3 %collective-permute-start.10 = (f32[96,128]{1,0:T(8,128)S(1)}, f32[96,128]{1,0:T(8,128)S(1)}, u32[]{:S(2)}, u32[]{:S(2)}) collective-permute-start(f32[96,128]{1,0:T(8,128)S(1)} %add.24.own_ref), channel_id=1, source_target_pairs={{0,1},{1,0},{2,3},{3,2},{4,5},{5,4},{6,7},{7,6},{8,9},{9,8},{10,11... | collective-permute-start | bytes 147464 | tf_op jit(solution)/shard_map/ppermute | solution.py:324
  64.8 38.8 %collective-permute-start.13 = (f32[320,256]{1,0:T(8,128)S(1)}, f32[320,256]{1,0:T(8,128)S(1)}, u32[]{:S(2)}, u32[]{:S(2)}) collective-permute-start(f32[320,256]{1,0:T(8,128)S(1)} %get-tuple-element.30.f0), channel_id=1, source_target_pairs={{0,12},{4,8},{8,4},{12,0},{1,13},{5,9},{9,5},{13,1},{2,14},{6,10},... | collective-permute-start | bytes 983048 | tf_op jit(solution)/shard_map/ppermute | solution.py:324
  68.5 35.1 %collective-permute-start.12 = (f32[320,256]{1,0:T(8,128)S(1)}, f32[320,256]{1,0:T(8,128)S(1)}, u32[]{:S(2)}, u32[]{:S(2)}) collective-permute-start(f32[320,256]{1,0:T(8,128)S(1)} %get-tuple-element.30.f0), channel_id=1, source_target_pairs={{0,8},{4,12},{8,0},{12,4},{1,9},{5,13},{9,1},{13,5},{2,10},{6,14},... | collective-permute-start | bytes 983048 | tf_op jit(solution)/shard_map/ppermute | solution.py:324
  68.5 35.1 %collective-permute-start.11 = (f32[320,256]{1,0:T(8,128)S(1)}, f32[320,256]{1,0:T(8,128)S(1)}, u32[]{:S(2)}, u32[]{:S(2)}) collective-permute-start(f32[320,256]{1,0:T(8,128)S(1)} %get-tuple-element.30.f0), channel_id=1, source_target_pairs={{0,4},{4,0},{8,12},{12,8},{1,5},{5,1},{9,13},{13,9},{2,6},{6,2},{1... | collective-permute-start | bytes 983048 | tf_op jit(solution)/shard_map/ppermute | solution.py:324
  69.3 5.6 %collective-permute-start.14 = (f32[128,256]{1,0:T(8,128)S(1)}, f32[128,256]{1,0:T(8,128)S(1)}, u32[]{:S(2)}, u32[]{:S(2)}) collective-permute-start(f32[128,256]{1,0:T(8,128)S(1)} %get-tuple-element.31.own_ref), channel_id=1, source_target_pairs={{0,16},{16,0},{1,17},{17,1},{2,18},{18,2},{3,19},{19,3},{4,20},{20... | collective-permute-start | bytes 393224 | tf_op jit(solution)/shard_map/ppermute | solution.py:324
  70.8 4.0 %collective-permute-start.15 = (f32[64,128]{1,0:T(8,128)S(1)}, f32[64,128]{1,0:T(8,128)S(1)}, u32[]{:S(2)}, u32[]{:S(2)}) collective-permute-start(f32[64,128]{1,0:T(8,128)S(1)} %get-tuple-element.32.gram_own), channel_id=1, source_target_pairs={{0,16},{16,0},{1,17},{17,1},{2,18},{18,2},{3,19},{19,3},{4,20},{20... | collective-permute-start | bytes 98312 | tf_op jit(solution)/shard_map/ppermute | solution.py:324
  75.9 16.9 %collective-permute-start.18 = (f32[64,256]{1,0:T(8,128)S(1)}, f32[64,256]{1,0:T(8,128)S(1)}, u32[]{:S(2)}, u32[]{:S(2)}) collective-permute-start(f32[64,256]{1,0:T(8,128)S(1)} %shard_map.91.s0), channel_id=1, source_target_pairs={{0,12},{4,8},{8,4},{12,0},{1,13},{5,9},{9,5},{13,1},{2,14},{6,10},... | collective-permute-start | bytes 196616 | tf_op jit(solution)/shard_map/ppermute | solution.py:324
  79.5 22.2 %collective-permute-start.17 = (f32[64,256]{1,0:T(8,128)S(1)}, f32[64,256]{1,0:T(8,128)S(1)}, u32[]{:S(2)}, u32[]{:S(2)}) collective-permute-start(f32[64,256]{1,0:T(8,128)S(1)} %shard_map.91.s0), channel_id=1, source_target_pairs={{0,8},{4,12},{8,0},{12,4},{1,9},{5,13},{9,1},{13,5},{2,10},{6,14},... | collective-permute-start | bytes 196616 | tf_op jit(solution)/shard_map/ppermute | solution.py:324
  92.9 10.8 %collective-permute-start.16 = (f32[64,256]{1,0:T(8,128)S(1)}, f32[64,256]{1,0:T(8,128)S(1)}, u32[]{:S(2)}, u32[]{:S(2)}) collective-permute-start(f32[64,256]{1,0:T(8,128)S(1)} %shard_map.91.s0), channel_id=1, source_target_pairs={{0,4},{4,0},{8,12},{12,8},{1,5},{5,1},{9,13},{13,9},{2,6},{6,2},{1... | collective-permute-start | bytes 196616 | tf_op jit(solution)/shard_map/ppermute | solution.py:324

commit v2 on v0

--- a/solution.py
+++ b/solution.py
@@ -1,13 +1,21 @@
+import functools
+
 import jax
 import jax.numpy as jnp
 from jax import lax
+from jax.experimental import pallas as pl
+from jax.experimental.pallas import tpu as pltpu
 from jax.sharding import PartitionSpec as P
 
 ITERS = 3
-
-
 penalty = 5.0
 precise = lax.Precision.HIGHEST
+f32 = jnp.float32
+bf16 = jnp.bfloat16
+
+GENE_TILE = 256
+SPARE = 24
+VMEM = pl.BlockSpec(memory_space=pltpu.VMEM)
 
 
 def shared_update(shared_now, total_cross, total_gram, total_pull):
@@ -20,23 +28,19 @@
     return shared_now
 
 
-def body(expression, usage_init, shared_factor, dataset_factors, cell_dataset, dataset_sizes):
+def plain_body(expression, usage_init, shared_factor, dataset_factors, cell_dataset, dataset_sizes):
     dataset_count = dataset_factors.shape[0]
     factor_rank = shared_factor.shape[0]
     gene_count = shared_factor.shape[1]
     slot_count = expression.shape[1]
-    counted = dataset_sizes.astype(jnp.float32)
-    onehot = (cell_dataset[None, :] == jnp.arange(dataset_count, dtype=jnp.int32)[:, None]).astype(
-        jnp.float32
-    )
+    counted = dataset_sizes.astype(f32)
+    onehot = (cell_dataset[None, :] == jnp.arange(dataset_count, dtype=jnp.int32)[:, None]).astype(f32)
     alive_mask = cell_dataset < dataset_count
-    stacked_low = jnp.concatenate([shared_factor[None], dataset_factors], axis=0).astype(
-        jnp.bfloat16
-    )
+    stacked_low = jnp.concatenate([shared_factor[None], dataset_factors], axis=0).astype(bf16)
     products = jnp.dot(
         stacked_low.reshape((dataset_count + 1) * factor_rank, gene_count),
         expression,
-        preferred_element_type=jnp.float32,
+        preferred_element_type=f32,
     ).reshape(dataset_count + 1, factor_rank, slot_count)
     cross_part = products[0] + jnp.sum(onehot[:, None, :] * products[1:], axis=0)
     combined = shared_factor[None] + dataset_factors
@@ -55,9 +59,9 @@
         divisor = jnp.where(alive_mask[None, :], divisor, 1.0)
         usage_now = jnp.where(alive_mask[None, :], usage_now * cross_sum / divisor, usage_now)
     masked_usage = onehot[:, None, :] * usage_now[None]
-    low_usage = masked_usage.astype(jnp.bfloat16).reshape(dataset_count * factor_rank, slot_count)
+    low_usage = masked_usage.astype(bf16).reshape(dataset_count * factor_rank, slot_count)
     cross_stat_part = lax.dot_general(
-        low_usage, expression, (((1,), (1,)), ((), ())), preferred_element_type=jnp.float32
+        low_usage, expression, (((1,), (1,)), ((), ())), preferred_element_type=f32
     ).reshape(dataset_count, factor_rank, gene_count)
     cross_stat_part = cross_stat_part / counted[:, None, None]
     gram_stat_part = (
@@ -79,9 +83,474 @@
     return (usage_now, factor_now, shared_now)
 
 
+def halves(value):
+    high = value.astype(bf16)
+    low = (value - high.astype(f32)).astype(bf16)
+    return high, low
+
+
+def nt_dot(a, b):
+    return lax.dot_general(a, b, (((1,), (1,)), ((), ())), preferred_element_type=f32)
+
+
+def left_cat(matrix):
+    high, low = halves(matrix)
+    return jnp.concatenate([high, low, high], axis=1)
+
+
+def right_cat(value):
+    high, low = halves(value)
+    return jnp.concatenate([high, high, low], axis=0)
+
+
+def flatten(block, width):
+    parts = width // block.shape[1]
+    rows = block.shape[0] // parts
+    return jnp.concatenate([block[i * rows : (i + 1) * rows] for i in range(parts)], axis=1)
+
+
+def unflatten(flat, rank):
+    parts = flat.shape[1] // rank
+    return jnp.concatenate([flat[:, i * rank : (i + 1) * rank] for i in range(parts)], axis=0)
+
+
+def start_kernel(
+    index_ref, shared_hbm, factors_hbm, expression_hbm, label_ref, send_ref, keep_ref,
+    shared_ref, factors_ref, tile_ref, low_ref, sems,
+):
+    count, rank, genes = factors_ref.shape
+    tiles, _, width = tile_ref.shape
+    core = index_ref[0]
+
+    def first_cell(t):
+        which = jnp.where(t < tiles // 2, 1 - core, core) * (tiles // 2) + t % (tiles // 2)
+        return pl.multiple_of(which * width, width)
+
+    def tile_copy(t):
+        return pltpu.make_async_copy(
+            expression_hbm.at[:, pl.ds(first_cell(t), width)], tile_ref.at[t], sems.at[1 + count + t]
+        )
+
+    def factor_copy(e):
+        return pltpu.make_async_copy(factors_hbm.at[e], factors_ref.at[e], sems.at[1 + e])
+
+    shared_copy = pltpu.make_async_copy(shared_hbm, shared_ref, sems.at[0])
+    shared_copy.start()
+    for e in range(count):
+        factor_copy(e).start()
+    tile_copy(0).start()
+    shared_copy.wait()
+    for e in range(count):
+        factor_copy(e).wait()
+    for t in range(1, tiles):
+        tile_copy(t).start()
+    shared = shared_ref[...]
+    low_ref[:rank, :] = shared.astype(bf16)
+    out_width = send_ref.shape[1]
+    rows = rank * rank // out_width
+    for e in range(count):
+        own = factors_ref[e]
+        own_high, own_low = halves(own)
+        both_high, both_low = halves(shared + own)
+        low_ref[(e + 1) * rank : (e + 2) * rank, :] = own_high
+        result = nt_dot(
+            jnp.concatenate([both_high, own_high], axis=0),
+            jnp.concatenate([both_high, both_low, own_high, own_low], axis=0),
+        )
+        mixed = result[:rank, rank : 2 * rank] + penalty * result[rank:, 3 * rank :]
+        block = result[:rank, :rank] + penalty * result[rank:, 2 * rank : 3 * rank]
+        flat = flatten(block + mixed + mixed.T, out_width)
+        send_ref[rank + e * rows : rank + (e + 1) * rows, :] = flat
+        keep_ref[rank + e * rows : rank + (e + 1) * rows, :] = flat
+
+    for t in range(tiles):
+        tile_copy(t).wait()
+        products = jnp.dot(low_ref[...], tile_ref[t], preferred_element_type=f32)
+        label = label_ref[:, pl.ds(first_cell(t), width)]
+        total = products[:rank]
+        for e in range(count):
+            total += jnp.where(label == e, products[(e + 1) * rank : (e + 2) * rank], 0.0)
+        out = send_ref if t < tiles // 2 else keep_ref
+        at = t % (tiles // 2) * width
+        out[:rank, at : at + width] = total
+
+
+def usage_kernel(index_ref, own_ref, other_ref, usage_ref, label_ref, out_ref):
+    rank = usage_ref.shape[0]
+    both = own_ref[...] + other_ref[...]
+    cross = both[:rank]
+    rows = rank * rank // both.shape[1]
+    count = both.shape[0] // rows - rank // rows
+    left = left_cat(
+        jnp.concatenate(
+            [unflatten(both[rank + e * rows : rank + (e + 1) * rows], rank) for e in range(count)],
+            axis=0,
+        )
+    )
+    label = label_ref[...]
+    alive = label < count
+    usage = usage_ref[...]
+    for sweep in range(ITERS):
+        stacked = jnp.dot(left, right_cat(usage), preferred_element_type=f32)
+        divisor = jnp.where(alive, 0.0, 1.0)
+        for e in range(count):
+            divisor += jnp.where(label == e, stacked[e * rank : (e + 1) * rank], 0.0)
+        usage = jnp.where(alive, usage * cross / divisor, usage)
+    out_ref[...] = usage
+
+
+def usage_gram_kernel(index_ref, place_ref, own_ref, other_ref, label_ref, usage_ref, gram_ref, low_ref):
+    rank, half = own_ref.shape
+    count = low_ref.shape[0] // rank
+    core = index_ref[0]
+    usage_ref[:, pl.ds(pl.multiple_of(core * half, half), half)] = own_ref[...]
+    usage_ref[:, pl.ds(pl.multiple_of((1 - core) * half, half), half)] = other_ref[...]
+    usage = usage_ref[...]
+    label = label_ref[...]
+    high, low = halves(usage)
+    right = jnp.concatenate([high, low], axis=0)
+    columns = gram_ref.shape[1]
+    for e in range(count):
+        rows = slice(e * rank, (e + 1) * rank)
+        masked = jnp.where(label == e, high, jnp.zeros_like(high))
+        low_ref[rows, :] = masked
+        both = nt_dot(masked, right)
+        mixed = both[:, rank:]
+        gram = both[:, :rank] + mixed + mixed.T
+        share = gram[:, :columns]
+        for k in range(1, rank // columns):
+            share = jnp.where(place_ref[0] == k, gram[:, k * columns : (k + 1) * columns], share)
+        gram_ref[rows, :] = share
+
+
+def stat_kernel(low_ref, gram_ref, expression_ref, *parts):
+    step = pl.program_id(0)
+    result = nt_dot(low_ref[...], expression_ref[...])
+    for t, ref in enumerate(parts):
+        @pl.when(step == t)
+        def _():
+            ref[...] = result
+            if t == 0:
+                ref[:, -SPARE : gram_ref.shape[1] - SPARE] = gram_ref[...]
+
+
+def gram_total_kernel(place_ref, size_ref, pair_ref, other_ref, left_ref, total_ref):
+    width = total_ref.shape[1]
+    rank = left_ref.shape[1] // 3
+    count = left_ref.shape[0] // rank
+    columns = pair_ref.shape[1] // 2
+    place = place_ref[0]
+    shares = [
+        pair_ref[:, :columns], pair_ref[:, columns:], other_ref[:, :columns], other_ref[:, columns:]
+    ]
+    whole_gram = []
+    for k in range(rank // columns):
+        share = shares[0]
+        for offset in range(1, rank // columns):
+            share = jnp.where(place == k ^ offset, shares[offset], share)
+        whole_gram.append(share)
+    gram = jnp.concatenate(whole_gram, axis=1)
+    total = jnp.zeros((rank, rank), f32)
+    for e in range(count):
+        rows = slice(e * rank, (e + 1) * rank)
+        scaled = gram[rows] / size_ref[e].astype(f32)
+        left_ref[rows, :] = left_cat(scaled)
+        total += scaled
+    total_ref[...] = flatten(total, width)
+
+
+def factor_kernel(size_ref, cross_ref, left_ref, gram_ref, shared_ref, factors_ref, *rest):
+    out_ref, total_ref = rest[-2:]
+    count, rank, width = factors_ref.shape
+    shared = shared_ref[...]
+    lefts = [left_ref[e * rank : (e + 1) * rank, :] for e in range(count)]
+    crosses = [
+        cross_ref[e * rank : (e + 1) * rank, :] * (1.0 / size_ref[e].astype(f32))
+        for e in range(count)
+    ]
+    factors = [factors_ref[e] for e in range(count)]
+    for sweep in range(ITERS):
+        divisors = [
+            jnp.dot(
+                lefts[e],
+                right_cat(shared + (1.0 + penalty) * factors[e]),
+                preferred_element_type=f32,
+            )
+            for e in range(count)
+        ]
+        factors = [factors[e] * crosses[e] / divisors[e] for e in range(count)]
+    total_cross = jnp.zeros((rank, width), f32)
+    total_pull = jnp.zeros((rank, width), f32)
+    for e in range(count):
+        out_ref[e] = factors[e]
+        total_cross += crosses[e]
+        total_pull += jnp.dot(lefts[e], right_cat(factors[e]), preferred_element_type=f32)
+    total_ref[:rank, :] = total_cross
+    total_ref[rank : 2 * rank, :] = total_pull
+    if total_ref.shape[0] > 2 * rank:
+        total_ref[2 * rank :, :] = gram_ref[...]
+
+
+def shared_kernel(own_ref, other_ref, gram_own, gram_other, shared_ref, *rest):
+    out_ref = rest[-1]
+    rank = out_ref.shape[0]
+    total = own_ref[...] + other_ref[...]
+    left = left_cat(unflatten(gram_own[...] + gram_other[...], rank))
+    shared = shared_ref[...]
+    for sweep in range(ITERS):
+        divisor = jnp.dot(left, right_cat(shared), preferred_element_type=f32) + total[rank : 2 * rank]
+        shared = shared * total[:rank] / divisor
+    out_ref[...] = shared
+
+
+def struct(*shape, dtype=f32):
+    return jax.ShapeDtypeStruct(shape, dtype)
+
+
+def whole(shape):
+    return pl.BlockSpec(shape, lambda *_: (0,) * len(shape))
+
+
+def call(
+    kernel, index, args, in_specs, out_shape, out_specs,
+    grid=(1,), scratch=(), cost=None, aliases={}, vmem=16,
+):
+    return pl.pallas_call(
+        kernel,
+        grid_spec=pltpu.PrefetchScalarGridSpec(
+            num_scalar_prefetch=len(index),
+            grid=grid,
+            in_specs=in_specs,
+            out_specs=out_specs,
+            scratch_shapes=list(scratch),
+        ),
+        out_shape=out_shape,
+        compiler_params=pltpu.CompilerParams(vmem_limit_bytes=int(vmem * 1024 * 1024)),
+        cost_estimate=cost,
+        input_output_aliases=aliases,
+    )(*index, *args)
+
+
+def cost(flops, moved):
+    return pl.CostEstimate(flops=int(flops), bytes_accessed=int(moved), transcendentals=0)
+
+
+def swap(value, axis, offset, size):
+    return lax.ppermute(value, axis, [(i, i ^ offset) for i in range(size)])
+
+
+INWARD = [(0, 1), (3, 2)]
+ACROSS = [(1, 2), (2, 1)]
+OUTWARD = [(1, 0), (2, 3)]
+
+
+ORDER = (
+    ("across", 0),
+    ("across", 1),
+    ("outward", 0),
+    ("across", 2),
+    ("outward", 1),
+    ("across", 3),
+    ("gram", 0),
+    ("outward", 2),
+    ("gram_total", 0),
+    ("outward", 3),
+    ("factor", 0),
+    ("factor", 1),
+    ("factor", 2),
+    ("shared", 0),
+    ("shared", 1),
+    ("factor", 3),
+    ("shared", 2),
+    ("shared", 3),
+)
+
+
+def fast_body(expression, usage_init, shared_factor, dataset_factors, cell_dataset, dataset_sizes):
+    count, rank, genes = dataset_factors.shape
+    cells = expression.shape[1]
+    half = cells // 2
+    tile = GENE_TILE
+    core = lax.axis_index("gene") % 2
+    index = core.astype(jnp.int32).reshape(1)
+    place = lax.axis_index("gene").astype(jnp.int32).reshape(1)
+    label = cell_dataset.reshape(1, cells)
+    rows = count * rank
+    flat = rank * rank // tile
+
+    hbm = pl.BlockSpec(memory_space=pltpu.HBM)
+    cell_tile = 512
+    shape = (rank + count * rank * rank // half, half)
+    send, keep = call(
+        start_kernel,
+        (index,),
+        (shared_factor, dataset_factors, expression, label),
+        [hbm, hbm, hbm, whole((1, cells))],
+        [struct(*shape), struct(*shape)],
+        [whole(shape), whole(shape)],
+        scratch=[
+            pltpu.VMEM((rank, genes), f32),
+            pltpu.VMEM((count, rank, genes), f32),
+            pltpu.VMEM((cells // cell_tile, genes, cell_tile), bf16),
+            pltpu.VMEM((rows + rank, genes), bf16),
+            pltpu.SemaphoreType.DMA((1 + count + cells // cell_tile,)),
+        ],
+        vmem=63,
+        cost=cost(2 * (count + 1) * rank * genes * cells, 2 * genes * cells),
+    )
+    both = keep + swap(send, "gene", 1, 4)
+    both_more = swap(both, "gene", 2, 4)
+    usage_half = call(
+        usage_kernel,
+        (index,),
+        (both, both_more, usage_init, label),
+        [
+            whole(shape),
+            whole(shape),
+            pl.BlockSpec((rank, half), lambda i, idx: (0, idx[0])),
+            pl.BlockSpec((1, half), lambda i, idx: (0, idx[0])),
+        ],
+        struct(rank, half),
+        whole((rank, half)),
+        cost=cost(2 * ITERS * 3 * count * rank * rank * half, 16 * rank * half),
+    )
+    usage_other = swap(usage_half, "gene", 1, 4)
+
+    pieces = pl.cdiv(genes, tile)
+    columns = rank // 4
+    usage, gram_share, low = call(
+        usage_gram_kernel,
+        (index, place),
+        (usage_half, usage_other, label),
+        [whole((rank, half)), whole((rank, half)), whole((1, cells))],
+        [struct(rank, cells), struct(rows, columns), struct(rows, cells, dtype=bf16)],
+        [whole((rank, cells)), whole((rows, columns)), whole((rows, cells))],
+        cost=cost(4 * 2 * rows * rank * cells, 6 * rows * cells),
+    )
+    own = list(
+        call(
+            stat_kernel,
+            (),
+            (low, gram_share, expression),
+            [
+                whole((rows, cells)),
+                whole((rows, columns)),
+                pl.BlockSpec((tile, cells), lambda i: ((i + pieces - 1) % pieces, 0)),
+            ],
+            [struct(rows, tile)] * pieces,
+            [whole((rows, tile))] * pieces,
+            grid=(pieces,),
+            cost=cost(2 * rows * genes * cells, 2 * genes * cells),
+        )
+    )
+
+    inward = [lax.ppermute(part, "cell", INWARD) for part in own]
+    across = [None] * pieces
+    outward = [None] * pieces
+    totals = [None] * pieces
+    token = own[1]
+
+    def after(token, *values):
+        *values, token = lax.optimization_barrier((*values, token))
+        return values
+
+    new_factors = None
+    new_shared = None
+    gram_left = None
+    grams = None
+    gram_own = None
+
+    def factor_call(j, total, into, flat_rows):
+        gene_block = pl.BlockSpec((rank, tile), lambda i, idx: (0, j))
+        set_block = pl.BlockSpec((count, rank, tile), lambda i, idx: (0, 0, j))
+        more = () if into is None else (into,)
+        shape = (2 * rank + flat_rows, tile)
+        return call(
+            factor_kernel,
+            (dataset_sizes,),
+            (total, gram_left, gram_own, shared_factor, dataset_factors) + more,
+            [whole((rows, tile)), whole((rows, 3 * rank)), whole((flat, tile))]
+            + [gene_block, set_block]
+            + [pl.BlockSpec(memory_space=pl.ANY)] * len(more),
+            [struct(count, rank, genes), struct(*shape)],
+            [set_block, whole(shape)],
+            aliases={6: 0} if more else {},
+            cost=cost(2 * 4 * 3 * rows * rank * tile, 3 * 4 * rows * tile),
+        )
+
+    def shared_call(j, own_total, other_total, into):
+        shape = (2 * rank, tile)
+        block = pl.BlockSpec((rank, tile), lambda i: (0, j))
+        more = () if into is None else (into,)
+        return call(
+            shared_kernel,
+            (),
+            (own_total, other_total, *grams, shared_factor) + more,
+            [whole(shape)] * 2
+            + [whole((flat, tile))] * 2
+            + [block]
+            + [pl.BlockSpec(memory_space=pl.ANY)] * len(more),
+            struct(rank, genes),
+            block,
+            aliases={5: 0} if more else {},
+            cost=cost(2 * 3 * 3 * rank * rank * tile, 6 * 4 * rank * tile),
+        )
+
+    def factor_step(j, token, into):
+        part, got1, got2, got3 = after(token, own[j], inward[j], across[j], outward[j])
+        total = (part + got1) + (got2 + got3)
+        into, own_total = factor_call((j + pieces - 1) % pieces, total, into, flat if j == 0 else 0)
+        totals[j] = (own_total, swap(own_total, "dp", 1, 2))
+        return into, own_total
+
+    def shared_step(j, token, into):
+        own_total, other_total = after(token, *totals[j])
+        return shared_call(
+            (j + pieces - 1) % pieces, own_total[: 2 * rank], other_total[: 2 * rank], into
+        )
+
+    for step in ORDER:
+        kind, j = step
+        if kind == "across":
+            part, got = after(token, own[j], inward[j])
+            token = part + got
+            across[j] = lax.ppermute(token, "cell", ACROSS)
+        elif kind == "outward":
+            part, got = after(token, own[j], across[j])
+            token = part + got
+            outward[j] = lax.ppermute(token, "cell", OUTWARD)
+        elif kind == "gram":
+            part, got1, got2, got3 = after(token, own[0], inward[0], across[0], outward[0])
+            lanes = slice(tile - SPARE, tile - SPARE + columns)
+            share = (part[:, lanes] + got1[:, lanes]) + (got2[:, lanes] + got3[:, lanes])
+            pair = jnp.concatenate([share, swap(share, "gene", 1, 4)], axis=1)
+            pair_got = swap(pair, "gene", 2, 4)
+            token = pair
+        elif kind == "gram_total":
+            pair, pair_got = after(token, pair, pair_got)
+            gram_left, gram_own = call(
+                gram_total_kernel,
+                (place, dataset_sizes),
+                (pair, pair_got),
+                [whole((rows, 2 * columns))] * 2,
+                [struct(rows, 3 * rank, dtype=bf16), struct(flat, tile)],
+                [whole((rows, 3 * rank)), whole((flat, tile))],
+            )
+            token = gram_own
+        elif kind == "factor":
+            new_factors, token = factor_step(j, token, new_factors)
+            if j == 0:
+                grams = [value[2 * rank :] for value in totals[0]]
+        else:
+            new_shared = shared_step(j, token, new_shared)
+            token = new_shared
+    return usage, new_factors, new_shared
+
+
 def solution(mesh):
+    sizes = (mesh.shape["dp"], mesh.shape["cell"], mesh.shape["gene"])
     return jax.shard_map(
-        body,
+        fast_body if sizes == (2, 4, 4) else plain_body,
         mesh=mesh,
         in_specs=(
             P("gene", ("dp", "cell")),

time: 176 us -> 94 us (0.53)
  waiting for transfers between devices: 121 us -> 30.8 us
  starting transfers between devices: 0.3 us -> 36.8 us
  matrix products: 26.9 us -> 0 us
  Pallas kernels: 0 us -> 23 us
  between operations: 14 us -> 1 us
  blocking collectives: 8.54 us -> 0 us
    psum x3 -> x0, waiting for transfers between devices: 121 us -> none  [the longest x1 66.2 us: body(): stat_cross, stat_gram = lax.psum((cross_stat_part, gram_stat_part), 'cell')]
    ppermute x0 -> x21, starting transfers between devices: none -> 36.8 us  [the longest x4 18.5 us: fast_body(): inward = [lax.ppermute(part, 'cell', INWARD) for part in own]]
    ppermute x0 -> x21, waiting for transfers between devices: none -> 30.8 us  [the longest x9 15.7 us: swap(): return lax.ppermute(value, axis, [(i, i ^ offset) for i in range(size)])]
    dot_general x16 -> x0, matrix products: 26.9 us -> none  [the longest x3 5.91 us: body(): jnp.dot(gram_full.reshape(dataset_count * factor_rank, factor_rank), usag...]
    pallas_call x0 -> x13, Pallas kernels: none -> 23 us  [call(): pl.pallas_call(kernel, grid_spec=pltpu.PrefetchScalarGridSpec(num_scalar_...]
    psum x1 -> x0, blocking collectives: 8.54 us -> none  [body(): lax.psum((total_cross, total_gram, total_pull), 'dp')]
  transfers between devices with their start and end apart: 3 -> 21, of which waited for: 3 -> 12; matrix products, arithmetic and copies ran while one was open for 0% -> 1% of each run, Pallas kernels for 0% -> 13%
where the time goes in v2:
time: 94 us; the launch traced here: 93.6 us
  starting transfers between devices  36.8 us (39%)
  waiting for transfers between devices  30.8 us (33%)
  Pallas kernels  23 us (24%)
  other arithmetic  1.99 us (2%)
  between operations  1 us (1%)
    pallas_call x13, Pallas kernels, call(): pl.pallas_call(kernel, grid_spec=pltpu.PrefetchScalarGridSpec(num_scalar_...  23 us
    ppermute x4, starting transfers between devices, fast_body(): inward = [lax.ppermute(part, 'cell', INWARD) for part in own]  18.5 us
    ppermute x9, waiting for transfers between devices, swap(): return lax.ppermute(value, axis, [(i, i ^ offset) for i in range(size)])  15.7 us
    ppermute x9, starting transfers between devices, swap(): return lax.ppermute(value, axis, [(i, i ^ offset) for i in range(size)])  10.2 us
    ppermute x4, waiting for transfers between devices, fast_body(): inward = [lax.ppermute(part, 'cell', INWARD) for part in own]  9.89 us
    ppermute x4, starting transfers between devices, fast_body(): outward[j] = lax.ppermute(token, 'cell', OUTWARD)  5.3 us
    ppermute x4, waiting for transfers between devices, fast_body(): outward[j] = lax.ppermute(token, 'cell', OUTWARD)  5.19 us
    ppermute x4, starting transfers between devices, fast_body(): across[j] = lax.ppermute(token, 'cell', ACROSS)  2.73 us
  transfers between devices with their start and end apart: 21, of which 12 were waited for; matrix products, arithmetic and copies ran while one was open for 1% of the time, Pallas kernels for 13%

profile of v2, /device:TPU:0, one launch (start us, length us, event | category | flops | bytes accessed | tf_op | source)
XLA Modules:
  0.0 93.6 jit_solution(5416872436190790631)
XLA Ops:
  0.7 5.5 %shard_map.85 = (f32[104,512]{1,0:T(8,128)}, f32[104,512]{1,0:T(8,128)}) custom-call(s32[1]{0:T(128)} %bitcast.index_ref, f32[64,1000]{1,0:T(8,128)} %shared_ref.15, f32[5,64,1000]{2,1,0:T(8,128)} %factors_ref.7, bf16[1000,1024]{1,0:T(8,128)(2,1)} %expression_ref.1, s32[1,1024]{1,0:T(1,128)} %bitcast.3), custom_call_target="tpu_custom_call" | custom-call | flops 786432000 | bytes 2048000 | tf_op jit(solution)/shard_map/pallas_call | solution.py:318
  6.2 0.5 collective-permute-start
  6.7 1.3 %collective-permute-done = f32[104,512]{1,0:T(8,128)S(1)} collective-permute-done((f32[104,512]{1,0:T(8,128)}, f32[104,512]{1,0:T(8,128)S(1)}, u32[]{:S(2)}, u32[]{:S(2)}) %collective-permute-start) | collective-permute-done | bytes 213024 | tf_op jit(solution)/shard_map/ppermute | solution.py:339
  8.0 1.0 %add.77.own_ref = f32[104,512]{1,0:T(8,128)S(1)} add(f32[104,512]{1,0:T(8,128)} %get-tuple-element.68, f32[104,512]{1,0:T(8,128)S(1)} %collective-permute-done) | non-fusion elementwise | flops 53248 | bytes 638976 | tf_op jit(solution)/shard_map/add | solution.py:401
  8.9 2.9 %collective-permute-start.1 = (f32[104,512]{1,0:T(8,128)S(1)}, f32[104,512]{1,0:T(8,128)S(1)}, u32[]{:S(2)}, u32[]{:S(2)}) collective-permute-start(f32[104,512]{1,0:T(8,128)S(1)} %add.77.own_ref), channel_id=1, source_target_pairs={{0,2},{1,3},{2,0},{3,1},{4,6},{5,7},{6,4},{7,5},{8,10},{9,11},{10,... | collective-permute-start | bytes 638984 | tf_op jit(solution)/shard_map/ppermute | solution.py:339
  11.9 5.6 %collective-permute-done.1.other_ref = f32[104,512]{1,0:T(8,128)S(1)} collective-permute-done((f32[104,512]{1,0:T(8,128)S(1)}, f32[104,512]{1,0:T(8,128)S(1)}, u32[]{:S(2)}, u32[]{:S(2)}) %collective-permute-start.1) | collective-permute-done | bytes 213024 | tf_op jit(solution)/shard_map/ppermute | solution.py:339
  17.4 0.9 shard_map.86.own_ref
  18.4 1.3 %collective-permute-done.2.other_ref = f32[64,512]{1,0:T(8,128)S(1)} collective-permute-done((f32[64,512]{1,0:T(8,128)S(1)}, f32[64,512]{1,0:T(8,128)S(1)}, u32[]{:S(2)}, u32[]{:S(2)}) %collective-permute-start.2) | collective-permute-done | bytes 131104 | tf_op jit(solution)/shard_map/ppermute | solution.py:339
  19.7 1.2 %shard_map.87 = (f32[64,1024]{1,0:T(8,128)}, f32[320,16]{1,0:T(8,128)S(1)}, bf16[320,1024]{1,0:T(8,128)(2,1)S(1)}) custom-call(s32[1]{0:T(128)} %bitcast.index_ref, s32[1]{0:T(128)} %bitcast.1.place_ref, f32[64,512]{1,0:T(8,128)S(1)} %shard_map.86.own_ref, f32[64,512]{1,0:T(8,128)S(1)} %collective-permute-done.2.other_ref, s32[1,1024]{1,0:T(1,128)S(1)} %bitcast.5), custom_call_target="tpu_custom_call" | custom-call | flops 167772160 | bytes 1966080 | tf_op jit(solution)/shard_map/pallas_call | solution.py:318
  20.9 1.8 %shard_map.88 = (f32[320,256]{1,0:T(8,128)S(1)}, f32[320,256]{1,0:T(8,128)S(1)}, f32[320,256]{1,0:T(8,128)S(1)}, f32[320,256]{1,0:T(8,128)S(1)}) custom-call(bf16[320,1024]{1,0:T(8,128)(2,1)S(1)} %get-tuple-element.71.low_ref, f32[320,16]{1,0:T(8,128)S(1)} %get-tuple-element.72.gram_ref, bf16[1000,1024]{1,0:T(8,128)(2,1)S(1)} %copy-done.2), custom_call_target="tpu_custom_call" | custom-call | flops 655360000 | bytes 2048000 | tf_op jit(solution)/shard_map/pallas_call | solution.py:318
  22.7 3.7 %collective-permute-start.5 = (f32[320,256]{1,0:T(8,128)S(1)}, f32[320,256]{1,0:T(8,128)S(1)}, u32[]{:S(2)}, u32[]{:S(2)}) collective-permute-start(f32[320,256]{1,0:T(8,128)S(1)} %get-tuple-element.100), channel_id=1, source_target_pairs={{0,4},{12,8},{1,5},{13,9},{2,6},{14,10},{3,7},{15,11},{16,20},{28,... | collective-permute-start | bytes 983048 | tf_op jit(solution)/shard_map/ppermute | solution.py:447
  26.4 1.3 %collective-permute-start.4 = (f32[320,256]{1,0:T(8,128)S(1)}, f32[320,256]{1,0:T(8,128)S(1)}, u32[]{:S(2)}, u32[]{:S(2)}) collective-permute-start(f32[320,256]{1,0:T(8,128)S(1)} %get-tuple-element.106), channel_id=1, source_target_pairs={{0,4},{12,8},{1,5},{13,9},{2,6},{14,10},{3,7},{15,11},{16,20},{28,... | collective-permute-start | bytes 983048 | tf_op jit(solution)/shard_map/ppermute | solution.py:447
  27.7 6.7 %collective-permute-done.5 = f32[320,256]{1,0:T(8,128)S(1)} collective-permute-done((f32[320,256]{1,0:T(8,128)S(1)}, f32[320,256]{1,0:T(8,128)S(1)}, u32[]{:S(2)}, u32[]{:S(2)}) %collective-permute-start.5) | collective-permute-done | bytes 327712 | tf_op jit(solution)/shard_map/ppermute | solution.py:447
  34.5 0.7 collective-permute-start.8
  35.2 7.2 %collective-permute-start.7 = (f32[320,256]{1,0:T(8,128)S(1)}, f32[320,256]{1,0:T(8,128)S(1)}, u32[]{:S(2)}, u32[]{:S(2)}) collective-permute-start(f32[320,256]{1,0:T(8,128)S(1)} %get-tuple-element.112), channel_id=1, source_target_pairs={{0,4},{12,8},{1,5},{13,9},{2,6},{14,10},{3,7},{15,11},{16,20},{28,... | collective-permute-start | bytes 983048 | tf_op jit(solution)/shard_map/ppermute | solution.py:447
  42.5 0.7 collective-permute-start.6
  43.1 6.3 %collective-permute-start.3 = (f32[320,256]{1,0:T(8,128)S(1)}, f32[320,256]{1,0:T(8,128)S(1)}, u32[]{:S(2)}, u32[]{:S(2)}) collective-permute-start(f32[320,256]{1,0:T(8,128)S(1)} %get-tuple-element.122), channel_id=1, source_target_pairs={{0,4},{12,8},{1,5},{13,9},{2,6},{14,10},{3,7},{15,11},{16,20},{28,... | collective-permute-start | bytes 983048 | tf_op jit(solution)/shard_map/ppermute | solution.py:447
  49.5 1.3 %collective-permute-start.10 = (f32[320,256]{1,0:T(8,128)S(1)}, f32[320,256]{1,0:T(8,128)S(1)}, u32[]{:S(2)}, u32[]{:S(2)}) collective-permute-start(f32[320,256]{1,0:T(8,128)S(1)} %add.80), channel_id=1, source_target_pairs={{4,0},{8,12},{5,1},{9,13},{6,2},{10,14},{7,3},{11,15},{20,16},{24,... | collective-permute-start | bytes 983048 | tf_op jit(solution)/shard_map/ppermute | solution.py:521
  50.8 0.7 collective-permute-start.13
  51.6 3.2 %collective-permute-done.3 = f32[320,256]{1,0:T(8,128)S(1)} collective-permute-done((f32[320,256]{1,0:T(8,128)S(1)}, f32[320,256]{1,0:T(8,128)S(1)}, u32[]{:S(2)}, u32[]{:S(2)}) %collective-permute-start.3) | collective-permute-done | bytes 327712 | tf_op jit(solution)/shard_map/ppermute | solution.py:447
  54.8 0.7 collective-permute-start.9
  55.5 3.4 %collective-permute-done.10 = f32[320,256]{1,0:T(8,128)S(1)} collective-permute-done((f32[320,256]{1,0:T(8,128)S(1)}, f32[320,256]{1,0:T(8,128)S(1)}, u32[]{:S(2)}, u32[]{:S(2)}) %collective-permute-start.10) | collective-permute-done | bytes 327712 | tf_op jit(solution)/shard_map/ppermute | solution.py:521
  59.0 0.2 add_add_fusion.4
  59.3 1.3 %collective-permute-start.15 = (f32[320,256]{1,0:T(8,128)S(1)}, f32[320,256]{1,0:T(8,128)S(1)}, u32[]{:S(2)}, u32[]{:S(2)}) collective-permute-start(f32[320,256]{1,0:T(8,128)S(1)} %add.82), channel_id=1, source_target_pairs={{4,0},{8,12},{5,1},{9,13},{6,2},{10,14},{7,3},{11,15},{20,16},{24,... | collective-permute-start | bytes 983048 | tf_op jit(solution)/shard_map/ppermute | solution.py:521
  60.7 0.1 pad_maximum_fusion.pair_ref
  60.8 1.6 %collective-permute-start.12 = (f32[320,32]{1,0:T(8,128)S(1)}, f32[320,32]{1,0:T(8,128)S(1)}, u32[]{:S(2)}, u32[]{:S(2)}) collective-permute-start(f32[320,32]{1,0:T(8,128)S(1)} %pad_maximum_fusion.pair_ref), channel_id=1, source_target_pairs={{0,2},{1,3},{2,0},{3,1},{4,6},{5,7},{6,4},{7,5},{8,10},{9,11},{10,... | collective-permute-start | bytes 122888 | tf_op jit(solution)/shard_map/ppermute | solution.py:339
  62.4 1.3 %collective-permute-start.18 = (f32[320,256]{1,0:T(8,128)S(1)}, f32[320,256]{1,0:T(8,128)S(1)}, u32[]{:S(2)}, u32[]{:S(2)}) collective-permute-start(f32[320,256]{1,0:T(8,128)S(1)} %add.87), channel_id=1, source_target_pairs={{4,0},{8,12},{5,1},{9,13},{6,2},{10,14},{7,3},{11,15},{20,16},{24,... | collective-permute-start | bytes 983048 | tf_op jit(solution)/shard_map/ppermute | solution.py:521
  63.7 3.7 %collective-permute-done.12.other_ref = f32[320,32]{1,0:T(8,128)S(1)} collective-permute-done((f32[320,32]{1,0:T(8,128)S(1)}, f32[320,32]{1,0:T(8,128)S(1)}, u32[]{:S(2)}, u32[]{:S(2)}) %collective-permute-start.12) | collective-permute-done | bytes 40992 | tf_op jit(solution)/shard_map/ppermute | solution.py:339
  67.4 1.3 %shard_map.89 = (bf16[320,192]{1,0:T(8,128)(2,1)S(1)}, f32[16,256]{1,0:T(8,128)S(1)}) custom-call(s32[1]{0:T(128)} %bitcast.1.place_ref, s32[5]{0:T(128)S(1)} %copy-done.5, f32[320,32]{1,0:T(8,128)S(1)} %pad_maximum_fusion.pair_ref, f32[320,32]{1,0:T(8,128)S(1)} %collective-permute-done.12.other_ref), custom_call_target="tpu_custom_call" | custom-call | tf_op jit(solution)/shard_map/pallas_call | solution.py:318
  68.8 1.4 %collective-permute-start.14 = (f32[320,256]{1,0:T(8,128)S(1)}, f32[320,256]{1,0:T(8,128)S(1)}, u32[]{:S(2)}, u32[]{:S(2)}) collective-permute-start(f32[320,256]{1,0:T(8,128)S(1)} %add.88), channel_id=1, source_target_pairs={{4,0},{8,12},{5,1},{9,13},{6,2},{10,14},{7,3},{11,15},{20,16},{24,... | collective-permute-start | bytes 983048 | tf_op jit(solution)/shard_map/ppermute | solution.py:521
  70.2 0.1 add_add_fusion.3.cross_ref
  70.3 1.9 %shard_map.90 = (f32[5,64,1000]{2,1,0:T(8,128)}, f32[144,256]{1,0:T(8,128)S(1)}) custom-call(s32[5]{0:T(128)S(1)} %copy-done.5, f32[320,256]{1,0:T(8,128)S(1)} %add_add_fusion.3.cross_ref, bf16[320,192]{1,0:T(8,128)(2,1)S(1)} %get-tuple-element.104.left_ref, f32[16,256]{1,0:T(8,128)S(1)} %get-tuple-element.97.gram_ref, f32[64,1000]{1,0:T(8,128)S(1)} %copy-done.1, ...), custom_call_target="tpu_custom_call" | custom-call | flops 125829120 | bytes 983040 | tf_op jit(solution)/shard_map/pallas_call | solution.py:318
  72.2 1.5 %collective-permute-start.17 = (f32[144,256]{1,0:T(8,128)S(1)}, f32[144,256]{1,0:T(8,128)S(1)}, u32[]{:S(2)}, u32[]{:S(2)}) collective-permute-start(f32[144,256]{1,0:T(8,128)S(1)} %get-tuple-element.118), channel_id=1, source_target_pairs={{0,16},{16,0},{1,17},{17,1},{2,18},{18,2},{3,19},{19,3},{4,20},{20... | collective-permute-start | bytes 442376 | tf_op jit(solution)/shard_map/ppermute | solution.py:339
  73.8 0.1 add_add_fusion.2.cross_ref
  73.9 1.9 %shard_map.91 = (f32[5,64,1000]{2,1,0:T(8,128)}, f32[128,256]{1,0:T(8,128)S(1)}) custom-call(s32[5]{0:T(128)S(1)} %copy-done.5, f32[320,256]{1,0:T(8,128)S(1)} %add_add_fusion.2.cross_ref, bf16[320,192]{1,0:T(8,128)(2,1)S(1)} %get-tuple-element.104.left_ref, f32[16,256]{1,0:T(8,128)S(1)} %get-tuple-element.97.gram_ref, ...), custom_call_target="tpu_custom_call", output_to_operand_aliasing={{0}: (6, {})} | custom-call | flops 125829120 | bytes 983040 | tf_op jit(solution)/shard_map/pallas_call | solution.py:318
  75.7 0.5 collective-permute-start.16
  76.2 1.4 %collective-permute-done.17 = f32[144,256]{1,0:T(8,128)S(1)} collective-permute-done((f32[144,256]{1,0:T(8,128)S(1)}, f32[144,256]{1,0:T(8,128)S(1)}, u32[]{:S(2)}, u32[]{:S(2)}) %collective-permute-start.17) | collective-permute-done | bytes 147488 | tf_op jit(solution)/shard_map/ppermute | solution.py:339
  77.6 1.1 %collective-permute-done.18 = f32[320,256]{1,0:T(8,128)S(1)} collective-permute-done((f32[320,256]{1,0:T(8,128)S(1)}, f32[320,256]{1,0:T(8,128)S(1)}, u32[]{:S(2)}, u32[]{:S(2)}) %collective-permute-start.18) | collective-permute-done | bytes 327712 | tf_op jit(solution)/shard_map/ppermute | solution.py:521
  78.8 1.9 %shard_map.92 = (f32[5,64,1000]{2,1,0:T(8,128)}, f32[128,256]{1,0:T(8,128)S(1)}) custom-call(s32[5]{0:T(128)S(1)} %copy-done.5, f32[320,256]{1,0:T(8,128)S(1)} %add_add_fusion.1.cross_ref, bf16[320,192]{1,0:T(8,128)(2,1)S(1)} %get-tuple-element.104.left_ref, f32[16,256]{1,0:T(8,128)S(1)} %get-tuple-element.97.gram_ref, ...), custom_call_target="tpu_custom_call", output_to_operand_aliasing={{0}: (6, {})} | custom-call | flops 125829120 | bytes 983040 | tf_op jit(solution)/shard_map/pallas_call | solution.py:318
  80.7 1.5 %collective-permute-start.20 = (f32[128,256]{1,0:T(8,128)S(1)}, f32[128,256]{1,0:T(8,128)S(1)}, u32[]{:S(2)}, u32[]{:S(2)}) collective-permute-start(f32[128,256]{1,0:T(8,128)S(1)} %get-tuple-element.129.own_ref), channel_id=1, source_target_pairs={{0,16},{16,0},{1,17},{17,1},{2,18},{18,2},{3,19},{19,3},{4,20},{20... | collective-permute-start | bytes 393224 | tf_op jit(solution)/shard_map/ppermute | solution.py:339
  82.2 1.2 %shard_map.93.rest_0_ = f32[64,1000]{1,0:T(8,128)} custom-call(f32[128,256]{1,0:T(8,128)S(1)} %slice.28.own_ref, f32[128,256]{1,0:T(8,128)S(1)} %slice.29.other_ref, f32[16,256]{1,0:T(8,128)S(1)} %slice.30.gram_own, f32[16,256]{1,0:T(8,128)S(1)} %slice.32.gram_other, f32[64,1000]{1,0:T(8,128)S(1)} %copy-done.1), custom_call_target="tpu_custom_call" | custom-call | flops 18874368 | bytes 393216 | tf_op jit(solution)/shard_map/pallas_call | solution.py:318
  83.4 1.2 %shard_map.94.rest_0_ = f32[64,1000]{1,0:T(8,128)} custom-call(f32[128,256]{1,0:T(8,128)S(1)} %get-tuple-element.120.own_ref, f32[128,256]{1,0:T(8,128)S(1)} %collective-permute-done.16.other_ref, f32[16,256]{1,0:T(8,128)S(1)} %slice.30.gram_own, f32[16,256]{1,0:T(8,128)S(1)} %slice.32.gram_other, ...), custom_call_target="tpu_custom_call", output_to_operand_aliasing={{}: (5, {})} | custom-call | flops 18874368 | bytes 393216 | tf_op jit(solution)/shard_map/pallas_call | solution.py:318
  84.6 0.7 collective-permute-done.14
  85.4 1.9 %shard_map.95 = (f32[5,64,1000]{2,1,0:T(8,128)}, f32[128,256]{1,0:T(8,128)S(1)}) custom-call(s32[5]{0:T(128)S(1)} %copy-done.5, f32[320,256]{1,0:T(8,128)S(1)} %add_add_fusion.cross_ref, bf16[320,192]{1,0:T(8,128)(2,1)S(1)} %get-tuple-element.104.left_ref, f32[16,256]{1,0:T(8,128)S(1)} %get-tuple-element.97.gram_ref, ...), custom_call_target="tpu_custom_call", output_to_operand_aliasing={{0}: (6, {})} | custom-call | flops 125829120 | bytes 983040 | tf_op jit(solution)/shard_map/pallas_call | solution.py:318
  87.3 1.5 %collective-permute-start.19 = (f32[128,256]{1,0:T(8,128)S(1)}, f32[128,256]{1,0:T(8,128)S(1)}, u32[]{:S(2)}, u32[]{:S(2)}) collective-permute-start(f32[128,256]{1,0:T(8,128)S(1)} %get-tuple-element.131.own_ref), channel_id=1, source_target_pairs={{0,16},{16,0},{1,17},{17,1},{2,18},{18,2},{3,19},{19,3},{4,20},{20... | collective-permute-start | bytes 393224 | tf_op jit(solution)/shard_map/ppermute | solution.py:339
  88.8 1.2 %shard_map.96.rest_0_ = f32[64,1000]{1,0:T(8,128)} custom-call(f32[128,256]{1,0:T(8,128)S(1)} %get-tuple-element.129.own_ref, f32[128,256]{1,0:T(8,128)S(1)} %collective-permute-done.20.other_ref, f32[16,256]{1,0:T(8,128)S(1)} %slice.30.gram_own, f32[16,256]{1,0:T(8,128)S(1)} %slice.32.gram_other, ...), custom_call_target="tpu_custom_call", output_to_operand_aliasing={{}: (5, {})} | custom-call | flops 18874368 | bytes 393216 | tf_op jit(solution)/shard_map/pallas_call | solution.py:318
  90.0 2.4 %collective-permute-done.19.other_ref = f32[128,256]{1,0:T(8,128)S(1)} collective-permute-done((f32[128,256]{1,0:T(8,128)S(1)}, f32[128,256]{1,0:T(8,128)S(1)}, u32[]{:S(2)}, u32[]{:S(2)}) %collective-permute-start.19) | collective-permute-done | bytes 131104 | tf_op jit(solution)/shard_map/ppermute | solution.py:339
  92.4 1.2 %shard_map.97 = f32[64,1000]{1,0:T(8,128)} custom-call(f32[128,256]{1,0:T(8,128)S(1)} %get-tuple-element.131.own_ref, f32[128,256]{1,0:T(8,128)S(1)} %collective-permute-done.19.other_ref, f32[16,256]{1,0:T(8,128)S(1)} %slice.30.gram_own, f32[16,256]{1,0:T(8,128)S(1)} %slice.32.gram_other, f32[64,1000]{1,0:T(8,128)S(1)} %copy-done.1, ...), custom_call_target="tpu_custom_call", output_to_operand_aliasing={{}: (5, {})} | custom-call | flops 18874368 | bytes 393216 | tf_op jit(solution)/shard_map/pallas_call | solution.py:318
  (38 shorter events, 0.8 us)
Async XLA Ops:
  0.6 16.8 %copy-start.3 = (f32[64,1024]{1,0:T(8,128)S(1)}, f32[64,1024]{1,0:T(8,128)}, u32[]{:S(2)}) copy-start(f32[64,1024]{1,0:T(8,128)} %usage_ref.1) | copy-start | bytes 786436
  0.7 16.8 %copy-start.4 = (s32[1024]{0:T(1024)S(1)}, s32[1024]{0:T(1024)}, u32[]{:S(2)}) copy-start(s32[1024]{0:T(1024)} %param.10) | copy-start | bytes 12292
  6.1 14.8 %copy-start.2 = (bf16[1000,1024]{1,0:T(8,128)(2,1)S(1)}, bf16[1000,1024]{1,0:T(8,128)(2,1)}, u32[]{:S(2)}) copy-start(bf16[1000,1024]{1,0:T(8,128)(2,1)} %expression_ref.1) | copy-start | bytes 6144004
  6.2 1.8 %collective-permute-start = (f32[104,512]{1,0:T(8,128)}, f32[104,512]{1,0:T(8,128)S(1)}, u32[]{:S(2)}, u32[]{:S(2)}) collective-permute-start(f32[104,512]{1,0:T(8,128)} %get-tuple-element.69), channel_id=1, source_target_pairs={{0,1},{1,0},{2,3},{3,2},{4,5},{5,4},{6,7},{7,6},{8,9},{9,8},{10,11... | collective-permute-start | bytes 638984 | tf_op jit(solution)/shard_map/ppermute | solution.py:339
  8.9 8.5 %collective-permute-start.1 = (f32[104,512]{1,0:T(8,128)S(1)}, f32[104,512]{1,0:T(8,128)S(1)}, u32[]{:S(2)}, u32[]{:S(2)}) collective-permute-start(f32[104,512]{1,0:T(8,128)S(1)} %add.77.own_ref), channel_id=1, source_target_pairs={{0,2},{1,3},{2,0},{3,1},{4,6},{5,7},{6,4},{7,5},{8,10},{9,11},{10,... | collective-permute-start | bytes 638984 | tf_op jit(solution)/shard_map/ppermute | solution.py:339
  18.3 1.4 %collective-permute-start.2 = (f32[64,512]{1,0:T(8,128)S(1)}, f32[64,512]{1,0:T(8,128)S(1)}, u32[]{:S(2)}, u32[]{:S(2)}) collective-permute-start(f32[64,512]{1,0:T(8,128)S(1)} %shard_map.86.own_ref), channel_id=1, source_target_pairs={{0,1},{1,0},{2,3},{3,2},{4,5},{5,4},{6,7},{7,6},{8,9},{9,8},{10,11... | collective-permute-start | bytes 393224 | tf_op jit(solution)/shard_map/ppermute | solution.py:339
  22.7 11.8 %collective-permute-start.5 = (f32[320,256]{1,0:T(8,128)S(1)}, f32[320,256]{1,0:T(8,128)S(1)}, u32[]{:S(2)}, u32[]{:S(2)}) collective-permute-start(f32[320,256]{1,0:T(8,128)S(1)} %get-tuple-element.100), channel_id=1, source_target_pairs={{0,4},{12,8},{1,5},{13,9},{2,6},{14,10},{3,7},{15,11},{16,20},{28,... | collective-permute-start | bytes 983048 | tf_op jit(solution)/shard_map/ppermute | solution.py:447
  26.4 16.0 %collective-permute-start.4 = (f32[320,256]{1,0:T(8,128)S(1)}, f32[320,256]{1,0:T(8,128)S(1)}, u32[]{:S(2)}, u32[]{:S(2)}) collective-permute-start(f32[320,256]{1,0:T(8,128)S(1)} %get-tuple-element.106), channel_id=1, source_target_pairs={{0,4},{12,8},{1,5},{13,9},{2,6},{14,10},{3,7},{15,11},{16,20},{28,... | collective-permute-start | bytes 983048 | tf_op jit(solution)/shard_map/ppermute | solution.py:447
  34.5 14.9 %collective-permute-start.8 = (f32[320,256]{1,0:T(8,128)S(1)}, f32[320,256]{1,0:T(8,128)S(1)}, u32[]{:S(2)}, u32[]{:S(2)}) collective-permute-start(f32[320,256]{1,0:T(8,128)S(1)} %add.78), channel_id=1, source_target_pairs={{4,8},{8,4},{5,9},{9,5},{6,10},{10,6},{7,11},{11,7},{20,24},{24,20... | collective-permute-start | bytes 983048 | tf_op jit(solution)/shard_map/ppermute | solution.py:517
  35.2 15.6 %collective-permute-start.7 = (f32[320,256]{1,0:T(8,128)S(1)}, f32[320,256]{1,0:T(8,128)S(1)}, u32[]{:S(2)}, u32[]{:S(2)}) collective-permute-start(f32[320,256]{1,0:T(8,128)S(1)} %get-tuple-element.112), channel_id=1, source_target_pairs={{0,4},{12,8},{1,5},{13,9},{2,6},{14,10},{3,7},{15,11},{16,20},{28,... | collective-permute-start | bytes 983048 | tf_op jit(solution)/shard_map/ppermute | solution.py:447
  42.5 9.1 %collective-permute-start.6 = (f32[320,256]{1,0:T(8,128)S(1)}, f32[320,256]{1,0:T(8,128)S(1)}, u32[]{:S(2)}, u32[]{:S(2)}) collective-permute-start(f32[320,256]{1,0:T(8,128)S(1)} %add.79), channel_id=1, source_target_pairs={{4,8},{8,4},{5,9},{9,5},{6,10},{10,6},{7,11},{11,7},{20,24},{24,20... | collective-permute-start | bytes 983048 | tf_op jit(solution)/shard_map/ppermute | solution.py:517
  43.1 11.6 %collective-permute-start.3 = (f32[320,256]{1,0:T(8,128)S(1)}, f32[320,256]{1,0:T(8,128)S(1)}, u32[]{:S(2)}, u32[]{:S(2)}) collective-permute-start(f32[320,256]{1,0:T(8,128)S(1)} %get-tuple-element.122), channel_id=1, source_target_pairs={{0,4},{12,8},{1,5},{13,9},{2,6},{14,10},{3,7},{15,11},{16,20},{28,... | collective-permute-start | bytes 983048 | tf_op jit(solution)/shard_map/ppermute | solution.py:447
  49.5 9.5 %collective-permute-start.10 = (f32[320,256]{1,0:T(8,128)S(1)}, f32[320,256]{1,0:T(8,128)S(1)}, u32[]{:S(2)}, u32[]{:S(2)}) collective-permute-start(f32[320,256]{1,0:T(8,128)S(1)} %add.80), channel_id=1, source_target_pairs={{4,0},{8,12},{5,1},{9,13},{6,2},{10,14},{7,3},{11,15},{20,16},{24,... | collective-permute-start | bytes 983048 | tf_op jit(solution)/shard_map/ppermute | solution.py:521
  50.8 11.5 %collective-permute-start.13 = (f32[320,256]{1,0:T(8,128)S(1)}, f32[320,256]{1,0:T(8,128)S(1)}, u32[]{:S(2)}, u32[]{:S(2)}) collective-permute-start(f32[320,256]{1,0:T(8,128)S(1)} %add.81), channel_id=1, source_target_pairs={{4,8},{8,4},{5,9},{9,5},{6,10},{10,6},{7,11},{11,7},{20,24},{24,20... | collective-permute-start | bytes 983048 | tf_op jit(solution)/shard_map/ppermute | solution.py:517
  54.8 12.6 %copy-start.5 = (s32[5]{0:T(128)S(1)}, s32[5]{0:T(128)}, u32[]{:S(2)}) copy-start(s32[5]{0:T(128)} %size_ref.9) | copy-start | bytes 64
  54.8 13.9 %collective-permute-start.9 = (f32[320,256]{1,0:T(8,128)S(1)}, f32[320,256]{1,0:T(8,128)S(1)}, u32[]{:S(2)}, u32[]{:S(2)}) collective-permute-start(f32[320,256]{1,0:T(8,128)S(1)} %add.83), channel_id=1, source_target_pairs={{4,8},{8,4},{5,9},{9,5},{6,10},{10,6},{7,11},{11,7},{20,24},{24,20... | collective-permute-start | bytes 983048 | tf_op jit(solution)/shard_map/ppermute | solution.py:517
  59.2 1.5 %collective-permute-start.11 = (f32[320,16]{1,0:T(8,128)S(1)}, f32[320,16]{1,0:T(8,128)S(1)}, u32[]{:S(2)}, u32[]{:S(2)}) collective-permute-start(f32[320,16]{1,0:T(8,128)S(1)} %add_add_fusion.4), channel_id=1, source_target_pairs={{0,1},{1,0},{2,3},{3,2},{4,5},{5,4},{6,7},{7,6},{8,9},{9,8},{10,11... | collective-permute-start | bytes 61448 | tf_op jit(solution)/shard_map/ppermute | solution.py:339
  59.3 14.5 %collective-permute-start.15 = (f32[320,256]{1,0:T(8,128)S(1)}, f32[320,256]{1,0:T(8,128)S(1)}, u32[]{:S(2)}, u32[]{:S(2)}) collective-permute-start(f32[320,256]{1,0:T(8,128)S(1)} %add.82), channel_id=1, source_target_pairs={{4,0},{8,12},{5,1},{9,13},{6,2},{10,14},{7,3},{11,15},{20,16},{24,... | collective-permute-start | bytes 983048 | tf_op jit(solution)/shard_map/ppermute | solution.py:521
  60.8 6.6 %collective-permute-start.12 = (f32[320,32]{1,0:T(8,128)S(1)}, f32[320,32]{1,0:T(8,128)S(1)}, u32[]{:S(2)}, u32[]{:S(2)}) collective-permute-start(f32[320,32]{1,0:T(8,128)S(1)} %pad_maximum_fusion.pair_ref), channel_id=1, source_target_pairs={{0,2},{1,3},{2,0},{3,1},{4,6},{5,7},{6,4},{7,5},{8,10},{9,11},{10,... | collective-permute-start | bytes 122888 | tf_op jit(solution)/shard_map/ppermute | solution.py:339
  62.4 16.3 %collective-permute-start.18 = (f32[320,256]{1,0:T(8,128)S(1)}, f32[320,256]{1,0:T(8,128)S(1)}, u32[]{:S(2)}, u32[]{:S(2)}) collective-permute-start(f32[320,256]{1,0:T(8,128)S(1)} %add.87), channel_id=1, source_target_pairs={{4,0},{8,12},{5,1},{9,13},{6,2},{10,14},{7,3},{11,15},{20,16},{24,... | collective-permute-start | bytes 983048 | tf_op jit(solution)/shard_map/ppermute | solution.py:521
  68.7 1.6 %copy-start = (f32[5,64,1000]{2,1,0:T(8,128)S(1)}, f32[5,64,1000]{2,1,0:T(8,128)}, u32[]{:S(2)}) copy-start(f32[5,64,1000]{2,1,0:T(8,128)} %factors_ref.7) | copy-start | bytes 3840004
  68.7 1.6 %copy-start.1 = (f32[64,1000]{1,0:T(8,128)S(1)}, f32[64,1000]{1,0:T(8,128)}, u32[]{:S(2)}) copy-start(f32[64,1000]{1,0:T(8,128)} %shared_ref.15) | copy-start | bytes 768004
  68.8 16.5 %collective-permute-start.14 = (f32[320,256]{1,0:T(8,128)S(1)}, f32[320,256]{1,0:T(8,128)S(1)}, u32[]{:S(2)}, u32[]{:S(2)}) collective-permute-start(f32[320,256]{1,0:T(8,128)S(1)} %add.88), channel_id=1, source_target_pairs={{4,0},{8,12},{5,1},{9,13},{6,2},{10,14},{7,3},{11,15},{20,16},{24,... | collective-permute-start | bytes 983048 | tf_op jit(solution)/shard_map/ppermute | solution.py:521
  72.2 5.4 %collective-permute-start.17 = (f32[144,256]{1,0:T(8,128)S(1)}, f32[144,256]{1,0:T(8,128)S(1)}, u32[]{:S(2)}, u32[]{:S(2)}) collective-permute-start(f32[144,256]{1,0:T(8,128)S(1)} %get-tuple-element.118), channel_id=1, source_target_pairs={{0,16},{16,0},{1,17},{17,1},{2,18},{18,2},{3,19},{19,3},{4,20},{20... | collective-permute-start | bytes 442376 | tf_op jit(solution)/shard_map/ppermute | solution.py:339
  75.7 7.7 %collective-permute-start.16 = (f32[128,256]{1,0:T(8,128)S(1)}, f32[128,256]{1,0:T(8,128)S(1)}, u32[]{:S(2)}, u32[]{:S(2)}) collective-permute-start(f32[128,256]{1,0:T(8,128)S(1)} %get-tuple-element.120.own_ref), channel_id=1, source_target_pairs={{0,16},{16,0},{1,17},{17,1},{2,18},{18,2},{3,19},{19,3},{4,20},{20... | collective-permute-start | bytes 393224 | tf_op jit(solution)/shard_map/ppermute | solution.py:339
  80.7 8.1 %collective-permute-start.20 = (f32[128,256]{1,0:T(8,128)S(1)}, f32[128,256]{1,0:T(8,128)S(1)}, u32[]{:S(2)}, u32[]{:S(2)}) collective-permute-start(f32[128,256]{1,0:T(8,128)S(1)} %get-tuple-element.129.own_ref), channel_id=1, source_target_pairs={{0,16},{16,0},{1,17},{17,1},{2,18},{18,2},{3,19},{19,3},{4,20},{20... | collective-permute-start | bytes 393224 | tf_op jit(solution)/shard_map/ppermute | solution.py:339
  87.3 5.1 %collective-permute-start.19 = (f32[128,256]{1,0:T(8,128)S(1)}, f32[128,256]{1,0:T(8,128)S(1)}, u32[]{:S(2)}, u32[]{:S(2)}) collective-permute-start(f32[128,256]{1,0:T(8,128)S(1)} %get-tuple-element.131.own_ref), channel_id=1, source_target_pairs={{0,16},{16,0},{1,17},{17,1},{2,18},{18,2},{3,19},{19,3},{4,20},{20... | collective-permute-start | bytes 393224 | tf_op jit(solution)/shard_map/ppermute | solution.py:339

commit v3 on v2

--- a/solution.py
+++ b/solution.py
@@ -223,15 +223,18 @@
         gram_ref[rows, :] = share
 
 
-def stat_kernel(low_ref, gram_ref, expression_ref, *parts):
+def first_stat_kernel(low_ref, gram_ref, expression_ref, part_ref):
+    part_ref[...] = nt_dot(low_ref[...], expression_ref[...])
+    part_ref[:, -SPARE : gram_ref.shape[1] - SPARE] = gram_ref[...]
+
+
+def stat_kernel(low_ref, expression_ref, *parts):
     step = pl.program_id(0)
     result = nt_dot(low_ref[...], expression_ref[...])
     for t, ref in enumerate(parts):
         @pl.when(step == t)
         def _():
             ref[...] = result
-            if t == 0:
-                ref[:, -SPARE : gram_ref.shape[1] - SPARE] = gram_ref[...]
 
 
 def gram_total_kernel(place_ref, size_ref, pair_ref, other_ref, left_ref, total_ref):
@@ -259,13 +262,15 @@
     total_ref[...] = flatten(total, width)
 
 
-def factor_kernel(size_ref, cross_ref, left_ref, gram_ref, shared_ref, factors_ref, *rest):
-    out_ref, total_ref = rest[-2:]
+def factor_kernel(tiles, size_ref, *refs):
+    crosses_ref, (left_ref, gram_ref, shared_ref, factors_ref) = refs[:tiles], refs[tiles : tiles + 4]
+    out_ref, total_ref = refs[-2:]
     count, rank, width = factors_ref.shape
     shared = shared_ref[...]
     lefts = [left_ref[e * rank : (e + 1) * rank, :] for e in range(count)]
     crosses = [
-        cross_ref[e * rank : (e + 1) * rank, :] * (1.0 / size_ref[e].astype(f32))
+        jnp.concatenate([ref[e * rank : (e + 1) * rank, :] for ref in crosses_ref], axis=1)
+        * (1.0 / size_ref[e].astype(f32))
         for e in range(count)
     ]
     factors = [factors_ref[e] for e in range(count)]
@@ -288,7 +293,8 @@
     total_ref[:rank, :] = total_cross
     total_ref[rank : 2 * rank, :] = total_pull
     if total_ref.shape[0] > 2 * rank:
-        total_ref[2 * rank :, :] = gram_ref[...]
+        total_ref[2 * rank :, : gram_ref.shape[1]] = gram_ref[...]
+        total_ref[2 * rank :, gram_ref.shape[1] :] = jnp.zeros_like(gram_ref)
 
 
 def shared_kernel(own_ref, other_ref, gram_own, gram_other, shared_ref, *rest):
@@ -339,9 +345,10 @@
     return lax.ppermute(value, axis, [(i, i ^ offset) for i in range(size)])
 
 
-INWARD = [(0, 1), (3, 2)]
-ACROSS = [(1, 2), (2, 1)]
-OUTWARD = [(1, 0), (2, 3)]
+HALF_LINE = [(0, 1), (1, 0), (2, 3), (3, 2)]
+ACROSS = [(4 * g + c, 4 * g + 3 - c) for g in (0, 1) for c in (1, 2)] + [
+    (4 * g + c, 4 * (1 - g) + c) for g in (0, 1) for c in (0, 3)
+]
 
 
 ORDER = (
@@ -353,14 +360,13 @@
     ("across", 3),
     ("gram", 0),
     ("outward", 2),
+    ("sum", 1),
     ("gram_total", 0),
     ("outward", 3),
     ("factor", 0),
-    ("factor", 1),
     ("factor", 2),
+    ("factor", 3),
     ("shared", 0),
-    ("shared", 1),
-    ("factor", 3),
     ("shared", 2),
     ("shared", 3),
 )
@@ -395,7 +401,7 @@
             pltpu.VMEM((rows + rank, genes), bf16),
             pltpu.SemaphoreType.DMA((1 + count + cells // cell_tile,)),
         ],
-        vmem=63,
+        vmem=56,
         cost=cost(2 * (count + 1) * rank * genes * cells, 2 * genes * cells),
     )
     both = keep + swap(send, "gene", 1, 4)
@@ -427,24 +433,36 @@
         [whole((rank, cells)), whole((rows, columns)), whole((rows, cells))],
         cost=cost(4 * 2 * rows * rank * cells, 6 * rows * cells),
     )
-    own = list(
+    first = call(
+        first_stat_kernel,
+        (),
+        (low, gram_share, expression),
+        [
+            whole((rows, cells)),
+            whole((rows, columns)),
+            pl.BlockSpec((tile, cells), lambda i: (pieces - 1, 0)),
+        ],
+        struct(rows, tile),
+        whole((rows, tile)),
+        cost=cost(2 * rows * tile * cells, 2 * tile * cells),
+    )
+    own = [first] + list(
         call(
             stat_kernel,
             (),
-            (low, gram_share, expression),
-            [
-                whole((rows, cells)),
-                whole((rows, columns)),
-                pl.BlockSpec((tile, cells), lambda i: ((i + pieces - 1) % pieces, 0)),
-            ],
-            [struct(rows, tile)] * pieces,
-            [whole((rows, tile))] * pieces,
-            grid=(pieces,),
+            (low, expression),
+            [whole((rows, cells)), pl.BlockSpec((tile, cells), lambda i: (pieces - 2 - i, 0))],
+            [struct(rows, tile)] * (pieces - 1),
+            [whole((rows, tile))] * (pieces - 1),
+            grid=(pieces - 1,),
             cost=cost(2 * rows * genes * cells, 2 * genes * cells),
         )
     )
 
-    inward = [lax.ppermute(part, "cell", INWARD) for part in own]
+    depth = lax.axis_index("cell")
+    inner = (depth == 1) | (depth == 2)
+    last = pieces - 1
+    inward = [lax.ppermute(part, "cell", HALF_LINE) for part in own[:last]] + [None]
     across = [None] * pieces
     outward = [None] * pieces
     totals = [None] * pieces
@@ -460,27 +478,9 @@
     grams = None
     gram_own = None
 
-    def factor_call(j, total, into, flat_rows):
-        gene_block = pl.BlockSpec((rank, tile), lambda i, idx: (0, j))
-        set_block = pl.BlockSpec((count, rank, tile), lambda i, idx: (0, 0, j))
-        more = () if into is None else (into,)
-        shape = (2 * rank + flat_rows, tile)
-        return call(
-            factor_kernel,
-            (dataset_sizes,),
-            (total, gram_left, gram_own, shared_factor, dataset_factors) + more,
-            [whole((rows, tile)), whole((rows, 3 * rank)), whole((flat, tile))]
-            + [gene_block, set_block]
-            + [pl.BlockSpec(memory_space=pl.ANY)] * len(more),
-            [struct(count, rank, genes), struct(*shape)],
-            [set_block, whole(shape)],
-            aliases={6: 0} if more else {},
-            cost=cost(2 * 4 * 3 * rows * rank * tile, 3 * 4 * rows * tile),
-        )
-
-    def shared_call(j, own_total, other_total, into):
-        shape = (2 * rank, tile)
-        block = pl.BlockSpec((rank, tile), lambda i: (0, j))
+    def shared_call(block_at, width, own_total, other_total, into):
+        shape = (2 * rank, width)
+        block = pl.BlockSpec((rank, width), lambda i: (0, block_at))
         more = () if into is None else (into,)
         return call(
             shared_kernel,
@@ -493,20 +493,47 @@
             struct(rank, genes),
             block,
             aliases={5: 0} if more else {},
-            cost=cost(2 * 3 * 3 * rank * rank * tile, 6 * 4 * rank * tile),
-        )
-
-    def factor_step(j, token, into):
+            cost=cost(2 * 3 * 3 * rank * rank * width, 6 * 4 * rank * width),
+        )
+
+    sums = [None] * pieces
+
+    def sum_step(j, token):
         part, got1, got2, got3 = after(token, own[j], inward[j], across[j], outward[j])
-        total = (part + got1) + (got2 + got3)
-        into, own_total = factor_call((j + pieces - 1) % pieces, total, into, flat if j == 0 else 0)
-        totals[j] = (own_total, swap(own_total, "dp", 1, 2))
+        sums[j] = part + jnp.where(inner, got1 + got2, got3)
+        return sums[j]
+
+    def factor_step(first, number, token, into):
+        width = number * tile
+        block_at = (pieces - first - number) // number
+        gene_block = pl.BlockSpec((rank, width), lambda i, idx: (0, block_at))
+        set_block = pl.BlockSpec((count, rank, width), lambda i, idx: (0, 0, block_at))
+        more = () if into is None else (into,)
+        shape = (2 * rank + (flat if first == 0 else 0), width)
+        *crosses, _ = lax.optimization_barrier((*sums[first : first + number][::-1], token))
+        into, own_total = call(
+            functools.partial(factor_kernel, number),
+            (dataset_sizes,),
+            (*crosses, gram_left, gram_own, shared_factor, dataset_factors) + more,
+            [whole((rows, tile))] * number
+            + [whole((rows, 3 * rank)), whole((flat, tile)), gene_block, set_block]
+            + [pl.BlockSpec(memory_space=pl.ANY)] * len(more),
+            [struct(count, rank, genes), struct(*shape)],
+            [set_block, whole(shape)],
+            aliases={5 + number: 0} if more else {},
+            cost=cost(2 * 4 * 3 * rows * rank * width, 3 * 4 * rows * width),
+        )
+        totals[first] = (own_total, swap(own_total, "dp", 1, 2))
         return into, own_total
 
-    def shared_step(j, token, into):
-        own_total, other_total = after(token, *totals[j])
+    def shared_step(first, number, token, into):
+        own_total, other_total = after(token, *totals[first])
         return shared_call(
-            (j + pieces - 1) % pieces, own_total[: 2 * rank], other_total[: 2 * rank], into
+            (pieces - first - number) // number,
+            number * tile,
+            own_total[: 2 * rank],
+            other_total[: 2 * rank],
+            into,
         )
 
     for step in ORDER:
@@ -514,15 +541,21 @@
         if kind == "across":
             part, got = after(token, own[j], inward[j])
             token = part + got
-            across[j] = lax.ppermute(token, "cell", ACROSS)
+            across[j] = lax.ppermute(token, ("dp", "cell"), ACROSS)
         elif kind == "outward":
             part, got = after(token, own[j], across[j])
             token = part + got
-            outward[j] = lax.ppermute(token, "cell", OUTWARD)
+            if j == 0:
+                mixed = jnp.where(inner, token, own[last])
+                inward[last] = outward[0] = lax.ppermute(mixed, "cell", HALF_LINE)
+            else:
+                outward[j] = lax.ppermute(token, "cell", HALF_LINE)
         elif kind == "gram":
             part, got1, got2, got3 = after(token, own[0], inward[0], across[0], outward[0])
             lanes = slice(tile - SPARE, tile - SPARE + columns)
-            share = (part[:, lanes] + got1[:, lanes]) + (got2[:, lanes] + got3[:, lanes])
+            share = part[:, lanes] + jnp.where(
+                inner, got1[:, lanes] + got2[:, lanes], got3[:, lanes]
+            )
             pair = jnp.concatenate([share, swap(share, "gene", 1, 4)], axis=1)
             pair_got = swap(pair, "gene", 2, 4)
             token = pair
@@ -537,12 +570,18 @@
                 [whole((rows, 3 * rank)), whole((flat, tile))],
             )
             token = gram_own
+        elif kind == "sum":
+            token = sum_step(j, token)
         elif kind == "factor":
-            new_factors, token = factor_step(j, token, new_factors)
+            number = 2 if j == 0 else 1
+            for k in range(j, j + number):
+                if sums[k] is None:
+                    sum_step(k, token)
+            new_factors, token = factor_step(j, number, token, new_factors)
             if j == 0:
-                grams = [value[2 * rank :] for value in totals[0]]
+                grams = [value[2 * rank :, :tile] for value in totals[0]]
         else:
-            new_shared = shared_step(j, token, new_shared)
+            new_shared = shared_step(j, 2 if j == 0 else 1, token, new_shared)
             token = new_shared
     return usage, new_factors, new_shared
 

time: 94 us -> 83.2 us (0.89)
  starting transfers between devices: 36.8 us -> 26.8 us
  Pallas kernels: 23 us -> 20.3 us
  waiting for transfers between devices: 30.8 us -> 33 us
    ppermute x12 -> x11, starting transfers between devices: 26.5 us -> 18.1 us  [the longest x4 7.34 us: fast_body(): across[j] = lax.ppermute(token, ('dp', 'cell'), ACROSS)]
    ppermute x12 -> x11, waiting for transfers between devices: 15.1 us -> 20.3 us  [the longest x3 14.1 us: fast_body(): lax.ppermute(part, 'cell', HALF_LINE)]
    ppermute x9 -> x8, waiting for transfers between devices: 15.7 us -> 12.7 us  [swap(): return lax.ppermute(value, axis, [(i, i ^ offset) for i in range(size)])]
    pallas_call x13 -> x12, Pallas kernels: 23 us -> 20.3 us  [call(): pl.pallas_call(kernel, grid_spec=pltpu.PrefetchScalarGridSpec(num_scalar_...]
    ppermute x9 -> x8, starting transfers between devices: 10.2 us -> 8.69 us  [swap(): return lax.ppermute(value, axis, [(i, i ^ offset) for i in range(size)])]
  transfers between devices with their start and end apart: 21 -> 19, of which waited for: 12 -> 14; matrix products, arithmetic and copies ran while one was open for 1% -> 1% of each run, Pallas kernels for 13% -> 13%
where the time goes in v3:
time: 83.2 us; the launch traced here: 83 us
  waiting for transfers between devices  33 us (40%)
  starting transfers between devices  26.8 us (32%)
  Pallas kernels  20.3 us (24%)
  other arithmetic  2.03 us (2%)
    pallas_call x12, Pallas kernels, call(): pl.pallas_call(kernel, grid_spec=pltpu.PrefetchScalarGridSpec(num_scalar_...  20.3 us
    ppermute x3, waiting for transfers between devices, fast_body(): lax.ppermute(part, 'cell', HALF_LINE)  14.1 us
    ppermute x8, waiting for transfers between devices, swap(): return lax.ppermute(value, axis, [(i, i ^ offset) for i in range(size)])  12.7 us
    ppermute x8, starting transfers between devices, swap(): return lax.ppermute(value, axis, [(i, i ^ offset) for i in range(size)])  8.69 us
    ppermute x4, starting transfers between devices, fast_body(): across[j] = lax.ppermute(token, ('dp', 'cell'), ACROSS)  7.34 us
    ppermute x3, starting transfers between devices, fast_body(): outward[j] = lax.ppermute(token, 'cell', HALF_LINE)  5.28 us
    ppermute x3, starting transfers between devices, fast_body(): lax.ppermute(part, 'cell', HALF_LINE)  3.79 us
    ppermute x1, waiting for transfers between devices, fast_body(): inward[last] = outward[0] = lax.ppermute(mixed, 'cell', HALF_LINE)  3.39 us
  transfers between devices with their start and end apart: 19, of which 14 were waited for; matrix products, arithmetic and copies ran while one was open for 1% of the time, Pallas kernels for 13%

profile of v3, /device:TPU:0, one launch (start us, length us, event | category | flops | bytes accessed | tf_op | source)
XLA Modules:
  0.0 83.0 jit_solution(1349678364594920696)
XLA Ops:
  0.7 5.5 %shard_map.85 = (f32[104,512]{1,0:T(8,128)}, f32[104,512]{1,0:T(8,128)}) custom-call(s32[1]{0:T(128)} %bitcast.index_ref, f32[64,1000]{1,0:T(8,128)} %shared_ref.5, f32[5,64,1000]{2,1,0:T(8,128)} %refs_4_.5, bf16[1000,1024]{1,0:T(8,128)(2,1)} %expression_ref.3, s32[1,1024]{1,0:T(1,128)} %bitcast.3), custom_call_target="tpu_custom_call" | custom-call | flops 786432000 | bytes 2048000 | tf_op jit(solution)/shard_map/pallas_call | solution.py:324
  6.2 0.5 collective-permute-start
  6.7 1.3 %collective-permute-done = f32[104,512]{1,0:T(8,128)S(1)} collective-permute-done((f32[104,512]{1,0:T(8,128)}, f32[104,512]{1,0:T(8,128)S(1)}, u32[]{:S(2)}, u32[]{:S(2)}) %collective-permute-start) | collective-permute-done | bytes 213024 | tf_op jit(solution)/shard_map/ppermute | solution.py:345
  8.0 1.0 %add.62.own_ref = f32[104,512]{1,0:T(8,128)S(1)} add(f32[104,512]{1,0:T(8,128)} %get-tuple-element.67, f32[104,512]{1,0:T(8,128)S(1)} %collective-permute-done) | non-fusion elementwise | flops 53248 | bytes 638976 | tf_op jit(solution)/shard_map/add | solution.py:407
  8.9 2.9 %collective-permute-start.1 = (f32[104,512]{1,0:T(8,128)S(1)}, f32[104,512]{1,0:T(8,128)S(1)}, u32[]{:S(2)}, u32[]{:S(2)}) collective-permute-start(f32[104,512]{1,0:T(8,128)S(1)} %add.62.own_ref), channel_id=1, source_target_pairs={{0,2},{1,3},{2,0},{3,1},{4,6},{5,7},{6,4},{7,5},{8,10},{9,11},{10,... | collective-permute-start | bytes 638984 | tf_op jit(solution)/shard_map/ppermute | solution.py:345
  11.9 5.6 %collective-permute-done.1.other_ref = f32[104,512]{1,0:T(8,128)S(1)} collective-permute-done((f32[104,512]{1,0:T(8,128)S(1)}, f32[104,512]{1,0:T(8,128)S(1)}, u32[]{:S(2)}, u32[]{:S(2)}) %collective-permute-start.1) | collective-permute-done | bytes 213024 | tf_op jit(solution)/shard_map/ppermute | solution.py:345
  17.4 0.9 %shard_map.86.own_ref = f32[64,512]{1,0:T(8,128)S(1)} custom-call(s32[1]{0:T(128)} %bitcast.index_ref, f32[104,512]{1,0:T(8,128)S(1)} %add.62.own_ref, f32[104,512]{1,0:T(8,128)S(1)} %collective-permute-done.1.other_ref, f32[64,1024]{1,0:T(8,128)S(1)} %copy-done.3, s32[1,1024]{1,0:T(1,128)S(1)} %bitcast.4), custom_call_target="tpu_custom_call" | custom-call | flops 188743680 | bytes 524288 | tf_op jit(solution)/shard_map/pallas_call | solution.py:324
  18.4 1.3 %collective-permute-done.2.other_ref = f32[64,512]{1,0:T(8,128)S(1)} collective-permute-done((f32[64,512]{1,0:T(8,128)S(1)}, f32[64,512]{1,0:T(8,128)S(1)}, u32[]{:S(2)}, u32[]{:S(2)}) %collective-permute-start.2) | collective-permute-done | bytes 131104 | tf_op jit(solution)/shard_map/ppermute | solution.py:345
  19.7 1.2 %shard_map.87 = (f32[64,1024]{1,0:T(8,128)}, f32[320,16]{1,0:T(8,128)S(1)}, bf16[320,1024]{1,0:T(8,128)(2,1)S(1)}) custom-call(s32[1]{0:T(128)} %bitcast.index_ref, s32[1]{0:T(128)} %bitcast.1.place_ref, f32[64,512]{1,0:T(8,128)S(1)} %shard_map.86.own_ref, f32[64,512]{1,0:T(8,128)S(1)} %collective-permute-done.2.other_ref, s32[1,1024]{1,0:T(1,128)S(1)} %bitcast.5), custom_call_target="tpu_custom_call" | custom-call | flops 167772160 | bytes 1966080 | tf_op jit(solution)/shard_map/pallas_call | solution.py:324
  20.9 0.4 shard_map.89
  21.3 1.9 %collective-permute-start.3 = (f32[320,256]{1,0:T(8,128)S(1)}, f32[320,256]{1,0:T(8,128)S(1)}, u32[]{:S(2)}, u32[]{:S(2)}) collective-permute-start(f32[320,256]{1,0:T(8,128)S(1)} %shard_map.89), channel_id=1, source_target_pairs={{0,4},{4,0},{8,12},{12,8},{1,5},{5,1},{9,13},{13,9},{2,6},{6,2},{1... | collective-permute-start | bytes 983048 | tf_op jit(solution)/shard_map/ppermute | solution.py:465
  23.2 1.2 %shard_map.88 = (f32[320,256]{1,0:T(8,128)S(1)}, f32[320,256]{1,0:T(8,128)S(1)}, f32[320,256]{1,0:T(8,128)S(1)}) custom-call(bf16[320,1024]{1,0:T(8,128)(2,1)S(1)} %get-tuple-element.70.low_ref, bf16[1000,1024]{1,0:T(8,128)(2,1)S(1)} %copy-done.1), custom_call_target="tpu_custom_call" | custom-call | flops 655360000 | bytes 2048000 | tf_op jit(solution)/shard_map/pallas_call | solution.py:324
  24.4 0.3 collective-permute-start.5
  24.7 7.2 %collective-permute-done.3 = f32[320,256]{1,0:T(8,128)S(1)} collective-permute-done((f32[320,256]{1,0:T(8,128)S(1)}, f32[320,256]{1,0:T(8,128)S(1)}, u32[]{:S(2)}, u32[]{:S(2)}) %collective-permute-start.3) | collective-permute-done | bytes 327712 | tf_op jit(solution)/shard_map/ppermute | solution.py:465
  32.0 1.8 %collective-permute-start.4 = (f32[320,256]{1,0:T(8,128)S(1)}, f32[320,256]{1,0:T(8,128)S(1)}, u32[]{:S(2)}, u32[]{:S(2)}) collective-permute-start(f32[320,256]{1,0:T(8,128)S(1)} %add.63), channel_id=1, source_target_pairs={{4,8},{8,4},{20,24},{24,20},{0,16},{12,28},{16,0},{28,12},{5,9},{9... | collective-permute-start | bytes 983048 | tf_op jit(solution)/shard_map/ppermute | solution.py:544
  33.8 1.6 %collective-permute-start.8 = (f32[320,256]{1,0:T(8,128)S(1)}, f32[320,256]{1,0:T(8,128)S(1)}, u32[]{:S(2)}, u32[]{:S(2)}) collective-permute-start(f32[320,256]{1,0:T(8,128)S(1)} %get-tuple-element.110), channel_id=1, source_target_pairs={{0,4},{4,0},{8,12},{12,8},{1,5},{5,1},{9,13},{13,9},{2,6},{6,2},{1... | collective-permute-start | bytes 983048 | tf_op jit(solution)/shard_map/ppermute | solution.py:465
  35.4 3.5 %collective-permute-done.5 = f32[320,256]{1,0:T(8,128)S(1)} collective-permute-done((f32[320,256]{1,0:T(8,128)S(1)}, f32[320,256]{1,0:T(8,128)S(1)}, u32[]{:S(2)}, u32[]{:S(2)}) %collective-permute-start.5) | collective-permute-done | bytes 327712 | tf_op jit(solution)/shard_map/ppermute | solution.py:465
  39.0 1.8 %collective-permute-start.7 = (f32[320,256]{1,0:T(8,128)S(1)}, f32[320,256]{1,0:T(8,128)S(1)}, u32[]{:S(2)}, u32[]{:S(2)}) collective-permute-start(f32[320,256]{1,0:T(8,128)S(1)} %add.64), channel_id=1, source_target_pairs={{4,8},{8,4},{20,24},{24,20},{0,16},{12,28},{16,0},{28,12},{5,9},{9... | collective-permute-start | bytes 983048 | tf_op jit(solution)/shard_map/ppermute | solution.py:544
  40.9 1.7 %collective-permute-start.6 = (f32[320,256]{1,0:T(8,128)S(1)}, f32[320,256]{1,0:T(8,128)S(1)}, u32[]{:S(2)}, u32[]{:S(2)}) collective-permute-start(f32[320,256]{1,0:T(8,128)S(1)} %broadcast_select_fusion), channel_id=1, source_target_pairs={{0,4},{4,0},{8,12},{12,8},{1,5},{5,1},{9,13},{13,9},{2,6},{6,2},{1... | collective-permute-start | bytes 983048 | tf_op jit(solution)/shard_map/ppermute | solution.py:550
  42.6 3.4 %collective-permute-done.8 = f32[320,256]{1,0:T(8,128)S(1)} collective-permute-done((f32[320,256]{1,0:T(8,128)S(1)}, f32[320,256]{1,0:T(8,128)S(1)}, u32[]{:S(2)}, u32[]{:S(2)}) %collective-permute-start.8) | collective-permute-done | bytes 327712 | tf_op jit(solution)/shard_map/ppermute | solution.py:465
  46.0 1.8 %collective-permute-start.13 = (f32[320,256]{1,0:T(8,128)S(1)}, f32[320,256]{1,0:T(8,128)S(1)}, u32[]{:S(2)}, u32[]{:S(2)}) collective-permute-start(f32[320,256]{1,0:T(8,128)S(1)} %add.66), channel_id=1, source_target_pairs={{4,8},{8,4},{20,24},{24,20},{0,16},{12,28},{16,0},{28,12},{5,9},{9... | collective-permute-start | bytes 983048 | tf_op jit(solution)/shard_map/ppermute | solution.py:544
  47.9 1.7 %collective-permute-start.12 = (f32[320,256]{1,0:T(8,128)S(1)}, f32[320,256]{1,0:T(8,128)S(1)}, u32[]{:S(2)}, u32[]{:S(2)}) collective-permute-start(f32[320,256]{1,0:T(8,128)S(1)} %add.67), channel_id=1, source_target_pairs={{0,4},{4,0},{8,12},{12,8},{1,5},{5,1},{9,13},{13,9},{2,6},{6,2},{1... | collective-permute-start | bytes 983048 | tf_op jit(solution)/shard_map/ppermute | solution.py:552
  49.6 3.4 %collective-permute-done.6 = f32[320,256]{1,0:T(8,128)S(1)} collective-permute-done((f32[320,256]{1,0:T(8,128)S(1)}, f32[320,256]{1,0:T(8,128)S(1)}, u32[]{:S(2)}, u32[]{:S(2)}) %collective-permute-start.6) | collective-permute-done | bytes 327712 | tf_op jit(solution)/shard_map/ppermute | solution.py:550
  53.0 0.2 select_add_fusion.4
  53.3 1.8 %collective-permute-start.9 = (f32[320,256]{1,0:T(8,128)S(1)}, f32[320,256]{1,0:T(8,128)S(1)}, u32[]{:S(2)}, u32[]{:S(2)}) collective-permute-start(f32[320,256]{1,0:T(8,128)S(1)} %add.68), channel_id=1, source_target_pairs={{4,8},{8,4},{20,24},{24,20},{0,16},{12,28},{16,0},{28,12},{5,9},{9... | collective-permute-start | bytes 983048 | tf_op jit(solution)/shard_map/ppermute | solution.py:544
  55.2 0.1 pad_maximum_fusion.pair_ref
  55.3 1.6 %collective-permute-start.11 = (f32[320,32]{1,0:T(8,128)S(1)}, f32[320,32]{1,0:T(8,128)S(1)}, u32[]{:S(2)}, u32[]{:S(2)}) collective-permute-start(f32[320,32]{1,0:T(8,128)S(1)} %pad_maximum_fusion.pair_ref), channel_id=1, source_target_pairs={{0,2},{1,3},{2,0},{3,1},{4,6},{5,7},{6,4},{7,5},{8,10},{9,11},{10,... | collective-permute-start | bytes 122888 | tf_op jit(solution)/shard_map/ppermute | solution.py:345
  56.9 1.7 %collective-permute-start.15 = (f32[320,256]{1,0:T(8,128)S(1)}, f32[320,256]{1,0:T(8,128)S(1)}, u32[]{:S(2)}, u32[]{:S(2)}) collective-permute-start(f32[320,256]{1,0:T(8,128)S(1)} %add.71), channel_id=1, source_target_pairs={{0,4},{4,0},{8,12},{12,8},{1,5},{5,1},{9,13},{13,9},{2,6},{6,2},{1... | collective-permute-start | bytes 983048 | tf_op jit(solution)/shard_map/ppermute | solution.py:552
  58.6 0.7 collective-permute-done.12
  59.3 0.1 select_add_fusion.3.refs_0_
  59.4 2.2 %collective-permute-done.11.other_ref = f32[320,32]{1,0:T(8,128)S(1)} collective-permute-done((f32[320,32]{1,0:T(8,128)S(1)}, f32[320,32]{1,0:T(8,128)S(1)}, u32[]{:S(2)}, u32[]{:S(2)}) %collective-permute-start.11) | collective-permute-done | bytes 40992 | tf_op jit(solution)/shard_map/ppermute | solution.py:345
  61.6 1.3 %shard_map.90 = (bf16[320,192]{1,0:T(8,128)(2,1)S(1)}, f32[16,256]{1,0:T(8,128)S(1)}) custom-call(s32[1]{0:T(128)} %bitcast.1.place_ref, s32[5]{0:T(128)S(1)} %copy-done.5, f32[320,32]{1,0:T(8,128)S(1)} %pad_maximum_fusion.pair_ref, f32[320,32]{1,0:T(8,128)S(1)} %collective-permute-done.11.other_ref), custom_call_target="tpu_custom_call" | custom-call | tf_op jit(solution)/shard_map/pallas_call | solution.py:324
  63.0 0.5 collective-permute-done.9
  63.5 1.9 %collective-permute-start.14 = (f32[320,256]{1,0:T(8,128)S(1)}, f32[320,256]{1,0:T(8,128)S(1)}, u32[]{:S(2)}, u32[]{:S(2)}) collective-permute-start(f32[320,256]{1,0:T(8,128)S(1)} %add.74), channel_id=1, source_target_pairs={{0,4},{4,0},{8,12},{12,8},{1,5},{5,1},{9,13},{13,9},{2,6},{6,2},{1... | collective-permute-start | bytes 983048 | tf_op jit(solution)/shard_map/ppermute | solution.py:552
  65.5 2.4 %shard_map.91 = (f32[5,64,1000]{2,1,0:T(8,128)}, f32[144,512]{1,0:T(8,128)S(1)}) custom-call(s32[5]{0:T(128)S(1)} %copy-done.5, f32[320,256]{1,0:T(8,128)S(1)} %select_add_fusion.3.refs_0_, f32[320,256]{1,0:T(8,128)S(1)} %select_add_fusion.2.refs_1_, bf16[320,192]{1,0:T(8,128)(2,1)S(1)} %get-tuple-element.108.refs_2_.refs_1_, ...), custom_call_target="tpu_custom_call" | custom-call | flops 251658240 | bytes 1966080 | tf_op jit(solution)/shard_map/pallas_call | solution.py:324
  67.9 1.5 %collective-permute-start.18 = (f32[144,512]{1,0:T(8,128)S(1)}, f32[144,512]{1,0:T(8,128)S(1)}, u32[]{:S(2)}, u32[]{:S(2)}) collective-permute-start(f32[144,512]{1,0:T(8,128)S(1)} %get-tuple-element.125), channel_id=1, source_target_pairs={{0,16},{16,0},{1,17},{17,1},{2,18},{18,2},{3,19},{19,3},{4,20},{20... | collective-permute-start | bytes 884744 | tf_op jit(solution)/shard_map/ppermute | solution.py:345
  69.5 1.9 %shard_map.92 = (f32[5,64,1000]{2,1,0:T(8,128)}, f32[128,256]{1,0:T(8,128)S(1)}) custom-call(s32[5]{0:T(128)S(1)} %copy-done.5, f32[320,256]{1,0:T(8,128)S(1)} %select_add_fusion.1.refs_0_, bf16[320,192]{1,0:T(8,128)(2,1)S(1)} %get-tuple-element.108.refs_2_.refs_1_, ...), custom_call_target="tpu_custom_call", output_to_operand_aliasing={{0}: (6, {})} | custom-call | flops 125829120 | bytes 983040 | tf_op jit(solution)/shard_map/pallas_call | solution.py:324
  71.4 0.5 collective-permute-start.17
  71.9 1.6 %collective-permute-done.14 = f32[320,256]{1,0:T(8,128)S(1)} collective-permute-done((f32[320,256]{1,0:T(8,128)S(1)}, f32[320,256]{1,0:T(8,128)S(1)}, u32[]{:S(2)}, u32[]{:S(2)}) %collective-permute-start.14) | collective-permute-done | bytes 327712 | tf_op jit(solution)/shard_map/ppermute | solution.py:552
  73.5 0.1 select_add_fusion.refs_0_
  73.6 1.9 %shard_map.93 = (f32[5,64,1000]{2,1,0:T(8,128)}, f32[128,256]{1,0:T(8,128)S(1)}) custom-call(s32[5]{0:T(128)S(1)} %copy-done.5, f32[320,256]{1,0:T(8,128)S(1)} %select_add_fusion.refs_0_, bf16[320,192]{1,0:T(8,128)(2,1)S(1)} %get-tuple-element.108.refs_2_.refs_1_, f32[16,256]{1,0:T(8,128)S(1)} %get-tuple-element.99.refs_3_.refs_2_, ...), custom_call_target="tpu_custom_call", output_to_operand_aliasing={{0}: (6, {})} | custom-call | flops 125829120 | bytes 983040 | tf_op jit(solution)/shard_map/pallas_call | solution.py:324
  75.5 1.5 %collective-permute-start.16 = (f32[128,256]{1,0:T(8,128)S(1)}, f32[128,256]{1,0:T(8,128)S(1)}, u32[]{:S(2)}, u32[]{:S(2)}) collective-permute-start(f32[128,256]{1,0:T(8,128)S(1)} %get-tuple-element.129.own_ref), channel_id=1, source_target_pairs={{0,16},{16,0},{1,17},{17,1},{2,18},{18,2},{3,19},{19,3},{4,20},{20... | collective-permute-start | bytes 393224 | tf_op jit(solution)/shard_map/ppermute | solution.py:345
  77.0 0.5 collective-permute-done.18
  77.6 1.3 %shard_map.94.rest_0_ = f32[64,1000]{1,0:T(8,128)} custom-call(f32[128,512]{1,0:T(8,128)S(1)} %slice.28.own_ref, f32[128,512]{1,0:T(8,128)S(1)} %slice.29.other_ref, f32[16,256]{1,0:T(8,128)S(1)} %slice.30.gram_own, f32[16,256]{1,0:T(8,128)S(1)} %slice.32.gram_other, f32[64,1000]{1,0:T(8,128)S(1)} %copy-done.2), custom_call_target="tpu_custom_call" | custom-call | flops 37748736 | bytes 786432 | tf_op jit(solution)/shard_map/pallas_call | solution.py:324
  78.9 1.5 %collective-permute-done.17.other_ref = f32[128,256]{1,0:T(8,128)S(1)} collective-permute-done((f32[128,256]{1,0:T(8,128)S(1)}, f32[128,256]{1,0:T(8,128)S(1)}, u32[]{:S(2)}, u32[]{:S(2)}) %collective-permute-start.17) | collective-permute-done | bytes 131104 | tf_op jit(solution)/shard_map/ppermute | solution.py:345
  80.4 1.2 %shard_map.95.rest_0_ = f32[64,1000]{1,0:T(8,128)} custom-call(f32[128,256]{1,0:T(8,128)S(1)} %get-tuple-element.127.own_ref, f32[128,256]{1,0:T(8,128)S(1)} %collective-permute-done.17.other_ref, f32[16,256]{1,0:T(8,128)S(1)} %slice.30.gram_own, f32[16,256]{1,0:T(8,128)S(1)} %slice.32.gram_other, ...), custom_call_target="tpu_custom_call", output_to_operand_aliasing={{}: (5, {})} | custom-call | flops 18874368 | bytes 393216 | tf_op jit(solution)/shard_map/pallas_call | solution.py:324
  81.6 0.2 collective-permute-done.16.other_ref
  81.8 1.2 %shard_map.96 = f32[64,1000]{1,0:T(8,128)} custom-call(f32[128,256]{1,0:T(8,128)S(1)} %get-tuple-element.129.own_ref, f32[128,256]{1,0:T(8,128)S(1)} %collective-permute-done.16.other_ref, f32[16,256]{1,0:T(8,128)S(1)} %slice.30.gram_own, f32[16,256]{1,0:T(8,128)S(1)} %slice.32.gram_other, f32[64,1000]{1,0:T(8,128)S(1)} %copy-done.2, ...), custom_call_target="tpu_custom_call", output_to_operand_aliasing={{}: (5, {})} | custom-call | flops 18874368 | bytes 393216 | tf_op jit(solution)/shard_map/pallas_call | solution.py:324
  (33 shorter events, 0.8 us)
Async XLA Ops:
  0.6 16.8 %copy-start.3 = (f32[64,1024]{1,0:T(8,128)S(1)}, f32[64,1024]{1,0:T(8,128)}, u32[]{:S(2)}) copy-start(f32[64,1024]{1,0:T(8,128)} %usage_ref.1) | copy-start | bytes 786436
  0.7 16.8 %copy-start.4 = (s32[1024]{0:T(1024)S(1)}, s32[1024]{0:T(1024)}, u32[]{:S(2)}) copy-start(s32[1024]{0:T(1024)} %param.10) | copy-start | bytes 12292
  6.1 14.8 %copy-start.1 = (bf16[1000,1024]{1,0:T(8,128)(2,1)S(1)}, bf16[1000,1024]{1,0:T(8,128)(2,1)}, u32[]{:S(2)}) copy-start(bf16[1000,1024]{1,0:T(8,128)(2,1)} %expression_ref.3) | copy-start | bytes 6144004
  6.2 1.8 %collective-permute-start = (f32[104,512]{1,0:T(8,128)}, f32[104,512]{1,0:T(8,128)S(1)}, u32[]{:S(2)}, u32[]{:S(2)}) collective-permute-start(f32[104,512]{1,0:T(8,128)} %get-tuple-element.68), channel_id=1, source_target_pairs={{0,1},{1,0},{2,3},{3,2},{4,5},{5,4},{6,7},{7,6},{8,9},{9,8},{10,11... | collective-permute-start | bytes 638984 | tf_op jit(solution)/shard_map/ppermute | solution.py:345
  8.9 8.5 %collective-permute-start.1 = (f32[104,512]{1,0:T(8,128)S(1)}, f32[104,512]{1,0:T(8,128)S(1)}, u32[]{:S(2)}, u32[]{:S(2)}) collective-permute-start(f32[104,512]{1,0:T(8,128)S(1)} %add.62.own_ref), channel_id=1, source_target_pairs={{0,2},{1,3},{2,0},{3,1},{4,6},{5,7},{6,4},{7,5},{8,10},{9,11},{10,... | collective-permute-start | bytes 638984 | tf_op jit(solution)/shard_map/ppermute | solution.py:345
  18.3 1.4 %collective-permute-start.2 = (f32[64,512]{1,0:T(8,128)S(1)}, f32[64,512]{1,0:T(8,128)S(1)}, u32[]{:S(2)}, u32[]{:S(2)}) collective-permute-start(f32[64,512]{1,0:T(8,128)S(1)} %shard_map.86.own_ref), channel_id=1, source_target_pairs={{0,1},{1,0},{2,3},{3,2},{4,5},{5,4},{6,7},{7,6},{8,9},{9,8},{10,11... | collective-permute-start | bytes 393224 | tf_op jit(solution)/shard_map/ppermute | solution.py:345
  21.3 10.6 %collective-permute-start.3 = (f32[320,256]{1,0:T(8,128)S(1)}, f32[320,256]{1,0:T(8,128)S(1)}, u32[]{:S(2)}, u32[]{:S(2)}) collective-permute-start(f32[320,256]{1,0:T(8,128)S(1)} %shard_map.89), channel_id=1, source_target_pairs={{0,4},{4,0},{8,12},{12,8},{1,5},{5,1},{9,13},{13,9},{2,6},{6,2},{1... | collective-permute-start | bytes 983048 | tf_op jit(solution)/shard_map/ppermute | solution.py:465
  24.4 14.5 %collective-permute-start.5 = (f32[320,256]{1,0:T(8,128)S(1)}, f32[320,256]{1,0:T(8,128)S(1)}, u32[]{:S(2)}, u32[]{:S(2)}) collective-permute-start(f32[320,256]{1,0:T(8,128)S(1)} %get-tuple-element.93), channel_id=1, source_target_pairs={{0,4},{4,0},{8,12},{12,8},{1,5},{5,1},{9,13},{13,9},{2,6},{6,2},{1... | collective-permute-start | bytes 983048 | tf_op jit(solution)/shard_map/ppermute | solution.py:465
  32.0 8.9 %collective-permute-start.4 = (f32[320,256]{1,0:T(8,128)S(1)}, f32[320,256]{1,0:T(8,128)S(1)}, u32[]{:S(2)}, u32[]{:S(2)}) collective-permute-start(f32[320,256]{1,0:T(8,128)S(1)} %add.63), channel_id=1, source_target_pairs={{4,8},{8,4},{20,24},{24,20},{0,16},{12,28},{16,0},{28,12},{5,9},{9... | collective-permute-start | bytes 983048 | tf_op jit(solution)/shard_map/ppermute | solution.py:544
  33.8 12.2 %collective-permute-start.8 = (f32[320,256]{1,0:T(8,128)S(1)}, f32[320,256]{1,0:T(8,128)S(1)}, u32[]{:S(2)}, u32[]{:S(2)}) collective-permute-start(f32[320,256]{1,0:T(8,128)S(1)} %get-tuple-element.110), channel_id=1, source_target_pairs={{0,4},{4,0},{8,12},{12,8},{1,5},{5,1},{9,13},{13,9},{2,6},{6,2},{1... | collective-permute-start | bytes 983048 | tf_op jit(solution)/shard_map/ppermute | solution.py:465
  39.0 8.9 %collective-permute-start.7 = (f32[320,256]{1,0:T(8,128)S(1)}, f32[320,256]{1,0:T(8,128)S(1)}, u32[]{:S(2)}, u32[]{:S(2)}) collective-permute-start(f32[320,256]{1,0:T(8,128)S(1)} %add.64), channel_id=1, source_target_pairs={{4,8},{8,4},{20,24},{24,20},{0,16},{12,28},{16,0},{28,12},{5,9},{9... | collective-permute-start | bytes 983048 | tf_op jit(solution)/shard_map/ppermute | solution.py:544
  40.9 12.1 %collective-permute-start.6 = (f32[320,256]{1,0:T(8,128)S(1)}, f32[320,256]{1,0:T(8,128)S(1)}, u32[]{:S(2)}, u32[]{:S(2)}) collective-permute-start(f32[320,256]{1,0:T(8,128)S(1)} %broadcast_select_fusion), channel_id=1, source_target_pairs={{0,4},{4,0},{8,12},{12,8},{1,5},{5,1},{9,13},{13,9},{2,6},{6,2},{1... | collective-permute-start | bytes 983048 | tf_op jit(solution)/shard_map/ppermute | solution.py:550
  46.0 10.9 %collective-permute-start.13 = (f32[320,256]{1,0:T(8,128)S(1)}, f32[320,256]{1,0:T(8,128)S(1)}, u32[]{:S(2)}, u32[]{:S(2)}) collective-permute-start(f32[320,256]{1,0:T(8,128)S(1)} %add.66), channel_id=1, source_target_pairs={{4,8},{8,4},{20,24},{24,20},{0,16},{12,28},{16,0},{28,12},{5,9},{9... | collective-permute-start | bytes 983048 | tf_op jit(solution)/shard_map/ppermute | solution.py:544
  47.9 11.4 %collective-permute-start.12 = (f32[320,256]{1,0:T(8,128)S(1)}, f32[320,256]{1,0:T(8,128)S(1)}, u32[]{:S(2)}, u32[]{:S(2)}) collective-permute-start(f32[320,256]{1,0:T(8,128)S(1)} %add.67), channel_id=1, source_target_pairs={{0,4},{4,0},{8,12},{12,8},{1,5},{5,1},{9,13},{13,9},{2,6},{6,2},{1... | collective-permute-start | bytes 983048 | tf_op jit(solution)/shard_map/ppermute | solution.py:552
  53.3 1.9 %collective-permute-start.10 = (f32[320,16]{1,0:T(8,128)S(1)}, f32[320,16]{1,0:T(8,128)S(1)}, u32[]{:S(2)}, u32[]{:S(2)}) collective-permute-start(f32[320,16]{1,0:T(8,128)S(1)} %select_add_fusion.4), channel_id=1, source_target_pairs={{0,1},{1,0},{2,3},{3,2},{4,5},{5,4},{6,7},{7,6},{8,9},{9,8},{10,11... | collective-permute-start | bytes 61448 | tf_op jit(solution)/shard_map/ppermute | solution.py:345
  53.3 10.1 %collective-permute-start.9 = (f32[320,256]{1,0:T(8,128)S(1)}, f32[320,256]{1,0:T(8,128)S(1)}, u32[]{:S(2)}, u32[]{:S(2)}) collective-permute-start(f32[320,256]{1,0:T(8,128)S(1)} %add.68), channel_id=1, source_target_pairs={{4,8},{8,4},{20,24},{24,20},{0,16},{12,28},{16,0},{28,12},{5,9},{9... | collective-permute-start | bytes 983048 | tf_op jit(solution)/shard_map/ppermute | solution.py:544
  55.3 6.4 %copy-start.5 = (s32[5]{0:T(128)S(1)}, s32[5]{0:T(128)}, u32[]{:S(2)}) copy-start(s32[5]{0:T(128)} %size_ref.7) | copy-start | bytes 64
  55.3 6.3 %collective-permute-start.11 = (f32[320,32]{1,0:T(8,128)S(1)}, f32[320,32]{1,0:T(8,128)S(1)}, u32[]{:S(2)}, u32[]{:S(2)}) collective-permute-start(f32[320,32]{1,0:T(8,128)S(1)} %pad_maximum_fusion.pair_ref), channel_id=1, source_target_pairs={{0,2},{1,3},{2,0},{3,1},{4,6},{5,7},{6,4},{7,5},{8,10},{9,11},{10,... | collective-permute-start | bytes 122888 | tf_op jit(solution)/shard_map/ppermute | solution.py:345
  56.9 12.5 %collective-permute-start.15 = (f32[320,256]{1,0:T(8,128)S(1)}, f32[320,256]{1,0:T(8,128)S(1)}, u32[]{:S(2)}, u32[]{:S(2)}) collective-permute-start(f32[320,256]{1,0:T(8,128)S(1)} %add.71), channel_id=1, source_target_pairs={{0,4},{4,0},{8,12},{12,8},{1,5},{5,1},{9,13},{13,9},{2,6},{6,2},{1... | collective-permute-start | bytes 983048 | tf_op jit(solution)/shard_map/ppermute | solution.py:552
  63.5 2.0 %copy-start = (f32[5,64,1000]{2,1,0:T(8,128)S(1)}, f32[5,64,1000]{2,1,0:T(8,128)}, u32[]{:S(2)}) copy-start(f32[5,64,1000]{2,1,0:T(8,128)} %refs_4_.5) | copy-start | bytes 3840004
  63.5 2.0 %copy-start.2 = (f32[64,1000]{1,0:T(8,128)S(1)}, f32[64,1000]{1,0:T(8,128)}, u32[]{:S(2)}) copy-start(f32[64,1000]{1,0:T(8,128)} %shared_ref.5) | copy-start | bytes 768004
  63.5 10.0 %collective-permute-start.14 = (f32[320,256]{1,0:T(8,128)S(1)}, f32[320,256]{1,0:T(8,128)S(1)}, u32[]{:S(2)}, u32[]{:S(2)}) collective-permute-start(f32[320,256]{1,0:T(8,128)S(1)} %add.74), channel_id=1, source_target_pairs={{0,4},{4,0},{8,12},{12,8},{1,5},{5,1},{9,13},{13,9},{2,6},{6,2},{1... | collective-permute-start | bytes 983048 | tf_op jit(solution)/shard_map/ppermute | solution.py:552
  67.9 9.7 %collective-permute-start.18 = (f32[144,512]{1,0:T(8,128)S(1)}, f32[144,512]{1,0:T(8,128)S(1)}, u32[]{:S(2)}, u32[]{:S(2)}) collective-permute-start(f32[144,512]{1,0:T(8,128)S(1)} %get-tuple-element.125), channel_id=1, source_target_pairs={{0,16},{16,0},{1,17},{17,1},{2,18},{18,2},{3,19},{19,3},{4,20},{20... | collective-permute-start | bytes 884744 | tf_op jit(solution)/shard_map/ppermute | solution.py:345
  71.4 9.0 %collective-permute-start.17 = (f32[128,256]{1,0:T(8,128)S(1)}, f32[128,256]{1,0:T(8,128)S(1)}, u32[]{:S(2)}, u32[]{:S(2)}) collective-permute-start(f32[128,256]{1,0:T(8,128)S(1)} %get-tuple-element.127.own_ref), channel_id=1, source_target_pairs={{0,16},{16,0},{1,17},{17,1},{2,18},{18,2},{3,19},{19,3},{4,20},{20... | collective-permute-start | bytes 393224 | tf_op jit(solution)/shard_map/ppermute | solution.py:345
  75.5 6.3 %collective-permute-start.16 = (f32[128,256]{1,0:T(8,128)S(1)}, f32[128,256]{1,0:T(8,128)S(1)}, u32[]{:S(2)}, u32[]{:S(2)}) collective-permute-start(f32[128,256]{1,0:T(8,128)S(1)} %get-tuple-element.129.own_ref), channel_id=1, source_target_pairs={{0,16},{16,0},{1,17},{17,1},{2,18},{18,2},{3,19},{19,3},{4,20},{20... | collective-permute-start | bytes 393224 | tf_op jit(solution)/shard_map/ppermute | solution.py:345

commit v4 on v3

--- a/solution.py
+++ b/solution.py
@@ -145,20 +145,23 @@
     for t in range(1, tiles):
         tile_copy(t).start()
     shared = shared_ref[...]
-    low_ref[:rank, :] = shared.astype(bf16)
+    shared_high, shared_low = halves(shared)
+    low_ref[:rank, :] = shared_high
+    pair = nt_dot(shared_high, jnp.concatenate([shared_high, shared_low], axis=0))
+    shared_gram = pair[:, :rank] + pair[:, rank:] + pair[:, rank:].T
     out_width = send_ref.shape[1]
     rows = rank * rank // out_width
     for e in range(count):
         own = factors_ref[e]
         own_high, own_low = halves(own)
-        both_high, both_low = halves(shared + own)
         low_ref[(e + 1) * rank : (e + 2) * rank, :] = own_high
         result = nt_dot(
-            jnp.concatenate([both_high, own_high], axis=0),
-            jnp.concatenate([both_high, both_low, own_high, own_low], axis=0),
-        )
-        mixed = result[:rank, rank : 2 * rank] + penalty * result[rank:, 3 * rank :]
-        block = result[:rank, :rank] + penalty * result[rank:, 2 * rank : 3 * rank]
+            jnp.concatenate([shared_high, own_high], axis=0),
+            jnp.concatenate([own_high, own_low, shared_low], axis=0),
+        )
+        cross = result[:rank, :rank] + result[:rank, rank : 2 * rank] + result[rank:, 2 * rank :].T
+        mixed = cross + (1.0 + penalty) * result[rank:, rank : 2 * rank]
+        block = shared_gram + (1.0 + penalty) * result[rank:, :rank]
         flat = flatten(block + mixed + mixed.T, out_width)
         send_ref[rank + e * rows : rank + (e + 1) * rows, :] = flat
         keep_ref[rank + e * rows : rank + (e + 1) * rows, :] = flat
@@ -199,38 +202,62 @@
     out_ref[...] = usage
 
 
-def usage_gram_kernel(index_ref, place_ref, own_ref, other_ref, label_ref, usage_ref, gram_ref, low_ref):
-    rank, half = own_ref.shape
+def half_statistics(usage, label, expression, low_ref):
+    rank, half = usage.shape
     count = low_ref.shape[0] // rank
-    core = index_ref[0]
-    usage_ref[:, pl.ds(pl.multiple_of(core * half, half), half)] = own_ref[...]
-    usage_ref[:, pl.ds(pl.multiple_of((1 - core) * half, half), half)] = other_ref[...]
-    usage = usage_ref[...]
-    label = label_ref[...]
     high, low = halves(usage)
     right = jnp.concatenate([high, low], axis=0)
-    columns = gram_ref.shape[1]
+    grams = []
+    for e in range(count):
+        masked = jnp.where(label == e, high, jnp.zeros_like(high))
+        low_ref[e * rank : (e + 1) * rank, :] = masked
+        grams.append(nt_dot(masked, right))
+    return nt_dot(low_ref[...], expression), grams
+
+
+def own_half_kernel(index_ref, own_ref, label_ref, expression_ref, low_ref, part_ref, gram_ref):
+    rank = own_ref.shape[0]
+    part, grams = half_statistics(own_ref[...], label_ref[...], expression_ref[...], low_ref)
+    part_ref[...] = part
+    for e, gram in enumerate(grams):
+        gram_ref[e * rank : (e + 1) * rank, :] = gram
+
+
+def first_stat_kernel(
+    index_ref, place_ref, other_ref, own_part_ref, own_gram_ref, label_ref, expression_ref,
+    low_ref, part_ref,
+):
+    rank, half = other_ref.shape
+    count = low_ref.shape[0] // rank
+    part, grams = half_statistics(other_ref[...], label_ref[...], expression_ref[...], low_ref)
+    part_ref[...] = part + own_part_ref[...]
+    columns = rank // 4
     for e in range(count):
         rows = slice(e * rank, (e + 1) * rank)
-        masked = jnp.where(label == e, high, jnp.zeros_like(high))
-        low_ref[rows, :] = masked
-        both = nt_dot(masked, right)
+        both = grams[e] + own_gram_ref[rows, :]
         mixed = both[:, rank:]
         gram = both[:, :rank] + mixed + mixed.T
         share = gram[:, :columns]
         for k in range(1, rank // columns):
             share = jnp.where(place_ref[0] == k, gram[:, k * columns : (k + 1) * columns], share)
-        gram_ref[rows, :] = share
-
-
-def first_stat_kernel(low_ref, gram_ref, expression_ref, part_ref):
-    part_ref[...] = nt_dot(low_ref[...], expression_ref[...])
-    part_ref[:, -SPARE : gram_ref.shape[1] - SPARE] = gram_ref[...]
-
-
-def stat_kernel(low_ref, expression_ref, *parts):
+        part_ref[rows, -SPARE : columns - SPARE] = share
+
+
+def stat_kernel(
+    index_ref, own_ref, other_ref, low_ref, other_low_ref, expression_ref, other_expression_ref,
+    usage_ref, *parts,
+):
     step = pl.program_id(0)
+    half = own_ref.shape[1]
+
+    @pl.when(step == 0)
+    def _():
+        core = index_ref[0]
+        usage_ref[:, pl.ds(pl.multiple_of(core * half, half), half)] = own_ref[...]
+        usage_ref[:, pl.ds(pl.multiple_of((1 - core) * half, half), half)] = other_ref[...]
+
     result = nt_dot(low_ref[...], expression_ref[...])
+    result += nt_dot(other_low_ref[...], other_expression_ref[...])
     for t, ref in enumerate(parts):
         @pl.when(step == t)
         def _():
@@ -241,10 +268,19 @@
     width = total_ref.shape[1]
     rank = left_ref.shape[1] // 3
     count = left_ref.shape[0] // rank
-    columns = pair_ref.shape[1] // 2
+    columns = pair_ref.shape[1] // 8
+    packed = pair_ref.shape[0] // 2
     place = place_ref[0]
     shares = [
-        pair_ref[:, :columns], pair_ref[:, columns:], other_ref[:, :columns], other_ref[:, columns:]
+        jnp.concatenate(
+            [
+                ref[at : at + packed, i * columns : (i + 1) * columns]
+                for i in range(8)
+            ],
+            axis=0,
+        )
+        for ref in (pair_ref, other_ref)
+        for at in (0, packed)
     ]
     whole_gram = []
     for k in range(rank // columns):
@@ -362,8 +398,8 @@
     ("outward", 2),
     ("sum", 1),
     ("gram_total", 0),
+    ("factor", 0),
     ("outward", 3),
-    ("factor", 0),
     ("factor", 2),
     ("factor", 3),
     ("shared", 0),
@@ -424,40 +460,52 @@
 
     pieces = pl.cdiv(genes, tile)
     columns = rank // 4
-    usage, gram_share, low = call(
-        usage_gram_kernel,
+    low_half, part_half, gram_half = call(
+        own_half_kernel,
+        (index,),
+        (usage_half, label, expression),
+        [
+            whole((rank, half)),
+            pl.BlockSpec((1, half), lambda i, idx: (0, idx[0])),
+            pl.BlockSpec((tile, half), lambda i, idx: (pieces - 1, idx[0])),
+        ],
+        [struct(rows, half, dtype=bf16), struct(rows, tile), struct(rows, 2 * rank)],
+        [whole((rows, half)), whole((rows, tile)), whole((rows, 2 * rank))],
+        cost=cost(2 * rows * (tile + 2 * rank) * half, 2 * tile * half),
+    )
+    other_low, first = call(
+        first_stat_kernel,
         (index, place),
-        (usage_half, usage_other, label),
-        [whole((rank, half)), whole((rank, half)), whole((1, cells))],
-        [struct(rank, cells), struct(rows, columns), struct(rows, cells, dtype=bf16)],
-        [whole((rank, cells)), whole((rows, columns)), whole((rows, cells))],
-        cost=cost(4 * 2 * rows * rank * cells, 6 * rows * cells),
-    )
-    first = call(
-        first_stat_kernel,
-        (),
-        (low, gram_share, expression),
+        (usage_other, part_half, gram_half, label, expression),
         [
-            whole((rows, cells)),
-            whole((rows, columns)),
-            pl.BlockSpec((tile, cells), lambda i: (pieces - 1, 0)),
+            whole((rank, half)),
+            whole((rows, tile)),
+            whole((rows, 2 * rank)),
+            pl.BlockSpec((1, half), lambda i, idx, _: (0, 1 - idx[0])),
+            pl.BlockSpec((tile, half), lambda i, idx, _: (pieces - 1, 1 - idx[0])),
         ],
-        struct(rows, tile),
-        whole((rows, tile)),
-        cost=cost(2 * rows * tile * cells, 2 * tile * cells),
-    )
-    own = [first] + list(
-        call(
-            stat_kernel,
-            (),
-            (low, expression),
-            [whole((rows, cells)), pl.BlockSpec((tile, cells), lambda i: (pieces - 2 - i, 0))],
-            [struct(rows, tile)] * (pieces - 1),
-            [whole((rows, tile))] * (pieces - 1),
-            grid=(pieces - 1,),
-            cost=cost(2 * rows * genes * cells, 2 * genes * cells),
-        )
-    )
+        [struct(rows, half, dtype=bf16), struct(rows, tile)],
+        [whole((rows, half)), whole((rows, tile))],
+        cost=cost(2 * rows * (tile + 2 * rank) * half, 2 * tile * half),
+    )
+    usage, *others = call(
+        stat_kernel,
+        (index,),
+        (usage_half, usage_other, low_half, other_low, expression, expression),
+        [
+            whole((rank, half)),
+            whole((rank, half)),
+            whole((rows, half)),
+            whole((rows, half)),
+            pl.BlockSpec((tile, half), lambda i, idx: (pieces - 2 - i, idx[0])),
+            pl.BlockSpec((tile, half), lambda i, idx: (pieces - 2 - i, 1 - idx[0])),
+        ],
+        [struct(rank, cells)] + [struct(rows, tile)] * (pieces - 1),
+        [whole((rank, cells))] + [whole((rows, tile))] * (pieces - 1),
+        grid=(pieces - 1,),
+        cost=cost(2 * rows * genes * cells, 2 * genes * cells),
+    )
+    own = [first] + others
 
     depth = lax.axis_index("cell")
     inner = (depth == 1) | (depth == 2)
@@ -556,7 +604,11 @@
             share = part[:, lanes] + jnp.where(
                 inner, got1[:, lanes] + got2[:, lanes], got3[:, lanes]
             )
-            pair = jnp.concatenate([share, swap(share, "gene", 1, 4)], axis=1)
+            packed = rows // 8
+            share = jnp.concatenate(
+                [share[i * packed : (i + 1) * packed] for i in range(8)], axis=1
+            )
+            pair = jnp.concatenate([share, swap(share, "gene", 1, 4)], axis=0)
             pair_got = swap(pair, "gene", 2, 4)
             token = pair
         elif kind == "gram_total":
@@ -565,9 +617,10 @@
                 gram_total_kernel,
                 (place, dataset_sizes),
                 (pair, pair_got),
-                [whole((rows, 2 * columns))] * 2,
+                [whole((2 * packed, 8 * columns))] * 2,
                 [struct(rows, 3 * rank, dtype=bf16), struct(flat, tile)],
                 [whole((rows, 3 * rank)), whole((flat, tile))],
+                cost=cost(1000000, 200000),
             )
             token = gram_own
         elif kind == "sum":

time: 83.2 us -> 81.8 us (0.983)
  waiting for transfers between devices: 33 us -> 28.1 us
  other arithmetic: 2.03 us -> 5.21 us
    ppermute x8, waiting for transfers between devices: 12.7 us -> 8.68 us  [swap(): return lax.ppermute(value, axis, [(i, i ^ offset) for i in range(size)])]
    add x7, other arithmetic: 0.3 us -> 2.53 us  [fast_body(): token = part + got]
    ppermute x1, waiting for transfers between devices: 3.39 us -> 2.01 us  [fast_body(): inward[last] = outward[0] = lax.ppermute(mixed, 'cell', HALF_LINE)]
    ppermute x3, waiting for transfers between devices: 2.31 us -> 3.64 us  [fast_body(): outward[j] = lax.ppermute(token, 'cell', HALF_LINE)]
    add x4, other arithmetic: 0.37 us -> 1.42 us  [sum_step(): sums[j] = part + jnp.where(inner, got1 + got2, got3)]
    ppermute x3, waiting for transfers between devices: 14.1 us -> 13.2 us  [fast_body(): lax.ppermute(part, 'cell', HALF_LINE)]
  transfers between devices with their start and end apart: 19 -> 19, of which waited for: 14 -> 10; matrix products, arithmetic and copies ran while one was open for 1% -> 5% of each run, Pallas kernels for 13% -> 15%
where the time goes in v4:
time: 81.8 us; the launch traced here: 81.6 us
  waiting for transfers between devices  28.1 us (34%)
  starting transfers between devices  26.7 us (33%)
  Pallas kernels  20.5 us (25%)
  other arithmetic  5.21 us (6%)
  between operations  0.88 us (1%)
    pallas_call x12, Pallas kernels, call(): pl.pallas_call(kernel, grid_spec=pltpu.PrefetchScalarGridSpec(num_scalar_...  20.5 us
    ppermute x3, waiting for transfers between devices, fast_body(): lax.ppermute(part, 'cell', HALF_LINE)  13.2 us
    ppermute x8, starting transfers between devices, swap(): return lax.ppermute(value, axis, [(i, i ^ offset) for i in range(size)])  8.76 us
    ppermute x8, waiting for transfers between devices, swap(): return lax.ppermute(value, axis, [(i, i ^ offset) for i in range(size)])  8.68 us
    ppermute x4, starting transfers between devices, fast_body(): across[j] = lax.ppermute(token, ('dp', 'cell'), ACROSS)  7.3 us
    ppermute x3, starting transfers between devices, fast_body(): outward[j] = lax.ppermute(token, 'cell', HALF_LINE)  5.2 us
    ppermute x3, starting transfers between devices, fast_body(): lax.ppermute(part, 'cell', HALF_LINE)  3.72 us
    ppermute x3, waiting for transfers between devices, fast_body(): outward[j] = lax.ppermute(token, 'cell', HALF_LINE)  3.64 us
  transfers between devices with their start and end apart: 19, of which 10 were waited for; matrix products, arithmetic and copies ran while one was open for 5% of the time, Pallas kernels for 15%

profile of v4, /device:TPU:0, one launch (start us, length us, event | category | flops | bytes accessed | tf_op | source)
XLA Modules:
  0.0 81.6 jit_solution(17664129042732223013)
XLA Ops:
  0.7 5.2 %shard_map.85 = (f32[104,512]{1,0:T(8,128)}, f32[104,512]{1,0:T(8,128)}) custom-call(s32[1]{0:T(128)} %bitcast.index_ref, f32[64,1000]{1,0:T(8,128)} %shared_ref.5, f32[5,64,1000]{2,1,0:T(8,128)} %refs_4_.5, bf16[1000,1024]{1,0:T(8,128)(2,1)} %other_expression_ref.1, s32[1,1024]{1,0:T(1,128)} %bitcast.3), custom_call_target="tpu_custom_call" | custom-call | flops 786432000 | bytes 2048000 | tf_op jit(solution)/shard_map/pallas_call | solution.py:360
  5.9 0.5 collective-permute-start
  6.4 1.3 %collective-permute-done = f32[104,512]{1,0:T(8,128)S(1)} collective-permute-done((f32[104,512]{1,0:T(8,128)}, f32[104,512]{1,0:T(8,128)S(1)}, u32[]{:S(2)}, u32[]{:S(2)}) %collective-permute-start) | collective-permute-done | bytes 213024 | tf_op jit(solution)/shard_map/ppermute | solution.py:381
  7.7 1.0 %add.62.own_ref = f32[104,512]{1,0:T(8,128)S(1)} add(f32[104,512]{1,0:T(8,128)} %get-tuple-element.70, f32[104,512]{1,0:T(8,128)S(1)} %collective-permute-done) | non-fusion elementwise | flops 53248 | bytes 638976 | tf_op jit(solution)/shard_map/add | solution.py:443
  8.7 2.9 %collective-permute-start.1 = (f32[104,512]{1,0:T(8,128)S(1)}, f32[104,512]{1,0:T(8,128)S(1)}, u32[]{:S(2)}, u32[]{:S(2)}) collective-permute-start(f32[104,512]{1,0:T(8,128)S(1)} %add.62.own_ref), channel_id=1, source_target_pairs={{0,2},{1,3},{2,0},{3,1},{4,6},{5,7},{6,4},{7,5},{8,10},{9,11},{10,... | collective-permute-start | bytes 638984 | tf_op jit(solution)/shard_map/ppermute | solution.py:381
  11.6 5.6 %collective-permute-done.1.other_ref = f32[104,512]{1,0:T(8,128)S(1)} collective-permute-done((f32[104,512]{1,0:T(8,128)S(1)}, f32[104,512]{1,0:T(8,128)S(1)}, u32[]{:S(2)}, u32[]{:S(2)}) %collective-permute-start.1) | collective-permute-done | bytes 213024 | tf_op jit(solution)/shard_map/ppermute | solution.py:381
  17.1 0.9 %shard_map.86.own_ref = f32[64,512]{1,0:T(8,128)S(1)} custom-call(s32[1]{0:T(128)} %bitcast.index_ref, f32[104,512]{1,0:T(8,128)S(1)} %add.62.own_ref, f32[104,512]{1,0:T(8,128)S(1)} %collective-permute-done.1.other_ref, f32[64,1024]{1,0:T(8,128)S(1)} %copy-done.3, s32[1,1024]{1,0:T(1,128)S(1)} %bitcast.4), custom_call_target="tpu_custom_call" | custom-call | flops 188743680 | bytes 524288 | tf_op jit(solution)/shard_map/pallas_call | solution.py:360
  18.1 0.5 shard_map.87
  18.6 0.8 %collective-permute-done.2.other_ref = f32[64,512]{1,0:T(8,128)S(1)} collective-permute-done((f32[64,512]{1,0:T(8,128)S(1)}, f32[64,512]{1,0:T(8,128)S(1)}, u32[]{:S(2)}, u32[]{:S(2)}) %collective-permute-start.2) | collective-permute-done | bytes 131104 | tf_op jit(solution)/shard_map/ppermute | solution.py:381
  19.4 1.0 %shard_map.88 = (bf16[320,512]{1,0:T(8,128)(2,1)S(1)}, f32[320,256]{1,0:T(8,128)S(1)}) custom-call(s32[1]{0:T(128)} %bitcast.index_ref, s32[1]{0:T(128)} %bitcast.2.place_ref, f32[64,512]{1,0:T(8,128)S(1)} %collective-permute-done.2.other_ref, f32[320,256]{1,0:T(8,128)S(1)} %get-tuple-element.73.own_part_ref, f32[320,128]{1,0:T(8,128)S(1)} %get-tuple-element.74.own_gram_ref, ...), custom_call_target="tpu_custom_call" | custom-call | flops 125829120 | bytes 262144 | tf_op jit(solution)/shard_map/pallas_call | solution.py:360
  20.5 1.9 %collective-permute-start.3 = (f32[320,256]{1,0:T(8,128)S(1)}, f32[320,256]{1,0:T(8,128)S(1)}, u32[]{:S(2)}, u32[]{:S(2)}) collective-permute-start(f32[320,256]{1,0:T(8,128)S(1)} %get-tuple-element.106), channel_id=1, source_target_pairs={{0,4},{4,0},{8,12},{12,8},{1,5},{5,1},{9,13},{13,9},{2,6},{6,2},{1... | collective-permute-start | bytes 983048 | tf_op jit(solution)/shard_map/ppermute | solution.py:513
  22.4 2.2 %shard_map.89 = (f32[64,1024]{1,0:T(8,128)}, f32[320,256]{1,0:T(8,128)S(1)}, f32[320,256]{1,0:T(8,128)S(1)}, f32[320,256]{1,0:T(8,128)S(1)}) custom-call(s32[1]{0:T(128)} %bitcast.index_ref, f32[64,512]{1,0:T(8,128)S(1)} %shard_map.86.own_ref, f32[64,512]{1,0:T(8,128)S(1)} %collective-permute-done.2.other_ref, ...), custom_call_target="tpu_custom_call" | custom-call | flops 655360000 | bytes 2048000 | tf_op jit(solution)/shard_map/pallas_call | solution.py:360
  24.5 0.2 collective-permute-start.5
  24.7 6.4 %collective-permute-done.3 = f32[320,256]{1,0:T(8,128)S(1)} collective-permute-done((f32[320,256]{1,0:T(8,128)S(1)}, f32[320,256]{1,0:T(8,128)S(1)}, u32[]{:S(2)}, u32[]{:S(2)}) %collective-permute-start.3) | collective-permute-done | bytes 327712 | tf_op jit(solution)/shard_map/ppermute | solution.py:513
  31.1 1.8 %collective-permute-start.4 = (f32[320,256]{1,0:T(8,128)S(1)}, f32[320,256]{1,0:T(8,128)S(1)}, u32[]{:S(2)}, u32[]{:S(2)}) collective-permute-start(f32[320,256]{1,0:T(8,128)S(1)} %add.63), channel_id=1, source_target_pairs={{4,8},{8,4},{20,24},{24,20},{0,16},{12,28},{16,0},{28,12},{5,9},{9... | collective-permute-start | bytes 983048 | tf_op jit(solution)/shard_map/ppermute | solution.py:592
  33.0 1.6 %collective-permute-start.8 = (f32[320,256]{1,0:T(8,128)S(1)}, f32[320,256]{1,0:T(8,128)S(1)}, u32[]{:S(2)}, u32[]{:S(2)}) collective-permute-start(f32[320,256]{1,0:T(8,128)S(1)} %get-tuple-element.116), channel_id=1, source_target_pairs={{0,4},{4,0},{8,12},{12,8},{1,5},{5,1},{9,13},{13,9},{2,6},{6,2},{1... | collective-permute-start | bytes 983048 | tf_op jit(solution)/shard_map/ppermute | solution.py:513
  34.6 3.5 %collective-permute-done.5 = f32[320,256]{1,0:T(8,128)S(1)} collective-permute-done((f32[320,256]{1,0:T(8,128)S(1)}, f32[320,256]{1,0:T(8,128)S(1)}, u32[]{:S(2)}, u32[]{:S(2)}) %collective-permute-start.5) | collective-permute-done | bytes 327712 | tf_op jit(solution)/shard_map/ppermute | solution.py:513
  38.2 1.8 %collective-permute-start.7 = (f32[320,256]{1,0:T(8,128)S(1)}, f32[320,256]{1,0:T(8,128)S(1)}, u32[]{:S(2)}, u32[]{:S(2)}) collective-permute-start(f32[320,256]{1,0:T(8,128)S(1)} %add.64), channel_id=1, source_target_pairs={{4,8},{8,4},{20,24},{24,20},{0,16},{12,28},{16,0},{28,12},{5,9},{9... | collective-permute-start | bytes 983048 | tf_op jit(solution)/shard_map/ppermute | solution.py:592
  40.1 1.7 %collective-permute-start.6 = (f32[320,256]{1,0:T(8,128)S(1)}, f32[320,256]{1,0:T(8,128)S(1)}, u32[]{:S(2)}, u32[]{:S(2)}) collective-permute-start(f32[320,256]{1,0:T(8,128)S(1)} %broadcast_select_fusion), channel_id=1, source_target_pairs={{0,4},{4,0},{8,12},{12,8},{1,5},{5,1},{9,13},{13,9},{2,6},{6,2},{1... | collective-permute-start | bytes 983048 | tf_op jit(solution)/shard_map/ppermute | solution.py:598
  41.8 3.4 %collective-permute-done.8 = f32[320,256]{1,0:T(8,128)S(1)} collective-permute-done((f32[320,256]{1,0:T(8,128)S(1)}, f32[320,256]{1,0:T(8,128)S(1)}, u32[]{:S(2)}, u32[]{:S(2)}) %collective-permute-start.8) | collective-permute-done | bytes 327712 | tf_op jit(solution)/shard_map/ppermute | solution.py:513
  45.1 0.8 add.66
  45.9 1.8 %collective-permute-start.11 = (f32[320,256]{1,0:T(8,128)}, f32[320,256]{1,0:T(8,128)S(1)}, u32[]{:S(2)}, u32[]{:S(2)}) collective-permute-start(f32[320,256]{1,0:T(8,128)} %add.66), channel_id=1, source_target_pairs={{4,8},{8,4},{20,24},{24,20},{0,16},{12,28},{16,0},{28,12},{5,9},{9... | collective-permute-start | bytes 983048 | tf_op jit(solution)/shard_map/ppermute | solution.py:592
  47.7 0.8 %add.67 = f32[320,256]{1,0:T(8,128)} add(f32[320,256]{1,0:T(8,128)S(1)} %get-tuple-element.99, f32[320,256]{1,0:T(8,128)S(1)} %collective-permute-done.7) | non-fusion elementwise | flops 81920 | bytes 983040 | tf_op jit(solution)/shard_map/add | solution.py:595
  48.5 1.6 %collective-permute-start.10 = (f32[320,256]{1,0:T(8,128)}, f32[320,256]{1,0:T(8,128)}, u32[]{:S(2)}, u32[]{:S(2)}) collective-permute-start(f32[320,256]{1,0:T(8,128)} %add.67), channel_id=1, source_target_pairs={{0,4},{4,0},{8,12},{12,8},{1,5},{5,1},{9,13},{13,9},{2,6},{6,2},{1... | collective-permute-start | bytes 983048 | tf_op jit(solution)/shard_map/ppermute | solution.py:600
  50.1 2.0 %collective-permute-done.6 = f32[320,256]{1,0:T(8,128)S(1)} collective-permute-done((f32[320,256]{1,0:T(8,128)S(1)}, f32[320,256]{1,0:T(8,128)S(1)}, u32[]{:S(2)}, u32[]{:S(2)}) %collective-permute-start.6) | collective-permute-done | bytes 327712 | tf_op jit(solution)/shard_map/ppermute | solution.py:598
  52.2 0.8 add.68
  52.9 0.2 select_add_fusion.4
  53.2 0.1 concatenate.6
  53.4 1.8 %collective-permute-start.9 = (f32[320,256]{1,0:T(8,128)}, f32[320,256]{1,0:T(8,128)S(1)}, u32[]{:S(2)}, u32[]{:S(2)}) collective-permute-start(f32[320,256]{1,0:T(8,128)} %add.68), channel_id=1, source_target_pairs={{4,8},{8,4},{20,24},{24,20},{0,16},{12,28},{16,0},{28,12},{5,9},{9... | collective-permute-start | bytes 983048 | tf_op jit(solution)/shard_map/ppermute | solution.py:592
  55.2 1.6 %collective-permute-start.13 = (f32[80,128]{1,0:T(8,128)S(1)}, f32[80,128]{1,0:T(8,128)S(1)}, u32[]{:S(2)}, u32[]{:S(2)}) collective-permute-start(f32[80,128]{1,0:T(8,128)S(1)} %pad_maximum_fusion.pair_ref), channel_id=1, source_target_pairs={{0,2},{1,3},{2,0},{3,1},{4,6},{5,7},{6,4},{7,5},{8,10},{9,11},{10,... | collective-permute-start | bytes 122888 | tf_op jit(solution)/shard_map/ppermute | solution.py:381
  56.9 1.7 %collective-permute-start.15 = (f32[320,256]{1,0:T(8,128)S(1)}, f32[320,256]{1,0:T(8,128)S(1)}, u32[]{:S(2)}, u32[]{:S(2)}) collective-permute-start(f32[320,256]{1,0:T(8,128)S(1)} %add.71), channel_id=1, source_target_pairs={{0,4},{4,0},{8,12},{12,8},{1,5},{5,1},{9,13},{13,9},{2,6},{6,2},{1... | collective-permute-start | bytes 983048 | tf_op jit(solution)/shard_map/ppermute | solution.py:600
  58.6 1.2 %select_add_fusion.3.refs_0_ = f32[320,256]{1,0:T(8,128)S(1)} fusion(f32[320,256]{1,0:T(8,128)S(1)} %get-tuple-element.99, f32[320,256]{1,0:T(8,128)} %collective-permute-done.10, f32[320,256]{1,0:T(8,128)S(1)} %collective-permute-done.5, f32[320,256]{1,0:T(8,128)} %copy-done.6, pred[]{:T(512)S(6)} %or.3), kind=kLoop, calls=%fused_computation.3 | loop fusion | flops 245760 | bytes 1638401 | tf_op jit(solution)/shard_map/add | solution.py:551
  59.8 1.0 %shard_map.90 = (bf16[320,192]{1,0:T(8,128)(2,1)S(1)}, f32[16,256]{1,0:T(8,128)S(1)}) custom-call(s32[1]{0:T(128)} %bitcast.2.place_ref, s32[5]{0:T(128)S(1)} %copy-done.5, f32[80,128]{1,0:T(8,128)S(1)} %pad_maximum_fusion.pair_ref, f32[80,128]{1,0:T(8,128)S(1)} %collective-permute-done.13.other_ref), custom_call_target="tpu_custom_call" | custom-call | flops 1000000 | bytes 200000 | tf_op jit(solution)/shard_map/pallas_call | solution.py:360
  60.8 0.1 select_add_fusion.2.refs_1_
  60.9 2.3 %shard_map.91 = (f32[5,64,1000]{2,1,0:T(8,128)}, f32[144,512]{1,0:T(8,128)S(1)}) custom-call(s32[5]{0:T(128)S(1)} %copy-done.5, f32[320,256]{1,0:T(8,128)S(1)} %select_add_fusion.3.refs_0_, f32[320,256]{1,0:T(8,128)S(1)} %select_add_fusion.2.refs_1_, bf16[320,192]{1,0:T(8,128)(2,1)S(1)} %get-tuple-element.112.refs_2_.refs_1_, ...), custom_call_target="tpu_custom_call" | custom-call | flops 251658240 | bytes 1966080 | tf_op jit(solution)/shard_map/pallas_call | solution.py:360
  63.2 0.5 collective-permute-done.9
  63.8 1.9 %collective-permute-start.14 = (f32[320,256]{1,0:T(8,128)S(1)}, f32[320,256]{1,0:T(8,128)S(1)}, u32[]{:S(2)}, u32[]{:S(2)}) collective-permute-start(f32[320,256]{1,0:T(8,128)S(1)} %add.76), channel_id=1, source_target_pairs={{0,4},{4,0},{8,12},{12,8},{1,5},{5,1},{9,13},{13,9},{2,6},{6,2},{1... | collective-permute-start | bytes 983048 | tf_op jit(solution)/shard_map/ppermute | solution.py:600
  65.7 1.5 %collective-permute-start.18 = (f32[144,512]{1,0:T(8,128)S(1)}, f32[144,512]{1,0:T(8,128)S(1)}, u32[]{:S(2)}, u32[]{:S(2)}) collective-permute-start(f32[144,512]{1,0:T(8,128)S(1)} %get-tuple-element.131), channel_id=1, source_target_pairs={{0,16},{16,0},{1,17},{17,1},{2,18},{18,2},{3,19},{19,3},{4,20},{20... | collective-permute-start | bytes 884744 | tf_op jit(solution)/shard_map/ppermute | solution.py:381
  67.2 0.1 select_add_fusion.1.refs_0_
  67.3 1.9 %shard_map.92 = (f32[5,64,1000]{2,1,0:T(8,128)}, f32[128,256]{1,0:T(8,128)S(1)}) custom-call(s32[5]{0:T(128)S(1)} %copy-done.5, f32[320,256]{1,0:T(8,128)S(1)} %select_add_fusion.1.refs_0_, bf16[320,192]{1,0:T(8,128)(2,1)S(1)} %get-tuple-element.112.refs_2_.refs_1_, ...), custom_call_target="tpu_custom_call", output_to_operand_aliasing={{0}: (6, {})} | custom-call | flops 125829120 | bytes 983040 | tf_op jit(solution)/shard_map/pallas_call | solution.py:360
  69.2 0.7 collective-permute-start.17
  69.8 3.6 %collective-permute-done.14 = f32[320,256]{1,0:T(8,128)S(1)} collective-permute-done((f32[320,256]{1,0:T(8,128)S(1)}, f32[320,256]{1,0:T(8,128)S(1)}, u32[]{:S(2)}, u32[]{:S(2)}) %collective-permute-start.14) | collective-permute-done | bytes 327712 | tf_op jit(solution)/shard_map/ppermute | solution.py:600
  73.6 1.9 %shard_map.93 = (f32[5,64,1000]{2,1,0:T(8,128)}, f32[128,256]{1,0:T(8,128)S(1)}) custom-call(s32[5]{0:T(128)S(1)} %copy-done.5, f32[320,256]{1,0:T(8,128)S(1)} %select_add_fusion.refs_0_, bf16[320,192]{1,0:T(8,128)(2,1)S(1)} %get-tuple-element.112.refs_2_.refs_1_, f32[16,256]{1,0:T(8,128)S(1)} %get-tuple-element.105.refs_3_.refs_2_, ...), custom_call_target="tpu_custom_call", output_to_operand_aliasing={{0}: (6, {})} | custom-call | flops 125829120 | bytes 983040 | tf_op jit(solution)/shard_map/pallas_call | solution.py:360
  75.4 1.4 %collective-permute-start.16 = (f32[128,256]{1,0:T(8,128)S(1)}, f32[128,256]{1,0:T(8,128)S(1)}, u32[]{:S(2)}, u32[]{:S(2)}) collective-permute-start(f32[128,256]{1,0:T(8,128)S(1)} %get-tuple-element.135.own_ref), channel_id=1, source_target_pairs={{0,16},{16,0},{1,17},{17,1},{2,18},{18,2},{3,19},{19,3},{4,20},{20... | collective-permute-start | bytes 393224 | tf_op jit(solution)/shard_map/ppermute | solution.py:381
  76.9 1.3 %shard_map.94.rest_0_ = f32[64,1000]{1,0:T(8,128)} custom-call(f32[128,512]{1,0:T(8,128)S(1)} %slice.60.own_ref, f32[128,512]{1,0:T(8,128)S(1)} %slice.61.other_ref, f32[16,256]{1,0:T(8,128)S(1)} %slice.62.gram_own, f32[16,256]{1,0:T(8,128)S(1)} %slice.72.gram_other, f32[64,1000]{1,0:T(8,128)S(1)} %copy-done.2), custom_call_target="tpu_custom_call" | custom-call | flops 37748736 | bytes 786432 | tf_op jit(solution)/shard_map/pallas_call | solution.py:360
  78.2 1.2 %shard_map.95.rest_0_ = f32[64,1000]{1,0:T(8,128)} custom-call(f32[128,256]{1,0:T(8,128)S(1)} %get-tuple-element.133.own_ref, f32[128,256]{1,0:T(8,128)S(1)} %collective-permute-done.17.other_ref, f32[16,256]{1,0:T(8,128)S(1)} %slice.62.gram_own, f32[16,256]{1,0:T(8,128)S(1)} %slice.72.gram_other, ...), custom_call_target="tpu_custom_call", output_to_operand_aliasing={{}: (5, {})} | custom-call | flops 18874368 | bytes 393216 | tf_op jit(solution)/shard_map/pallas_call | solution.py:360
  79.4 1.0 %collective-permute-done.16.other_ref = f32[128,256]{1,0:T(8,128)S(1)} collective-permute-done((f32[128,256]{1,0:T(8,128)S(1)}, f32[128,256]{1,0:T(8,128)S(1)}, u32[]{:S(2)}, u32[]{:S(2)}) %collective-permute-start.16) | collective-permute-done | bytes 131104 | tf_op jit(solution)/shard_map/ppermute | solution.py:381
  80.4 1.2 %shard_map.96 = f32[64,1000]{1,0:T(8,128)} custom-call(f32[128,256]{1,0:T(8,128)S(1)} %get-tuple-element.135.own_ref, f32[128,256]{1,0:T(8,128)S(1)} %collective-permute-done.16.other_ref, f32[16,256]{1,0:T(8,128)S(1)} %slice.62.gram_own, f32[16,256]{1,0:T(8,128)S(1)} %slice.72.gram_other, f32[64,1000]{1,0:T(8,128)S(1)} %copy-done.2, ...), custom_call_target="tpu_custom_call", output_to_operand_aliasing={{}: (5, {})} | custom-call | flops 18874368 | bytes 393216 | tf_op jit(solution)/shard_map/pallas_call | solution.py:360
  (37 shorter events, 0.6 us)
Async XLA Ops:
  0.6 16.5 %copy-start.3 = (f32[64,1024]{1,0:T(8,128)S(1)}, f32[64,1024]{1,0:T(8,128)}, u32[]{:S(2)}) copy-start(f32[64,1024]{1,0:T(8,128)} %usage_ref.1) | copy-start | bytes 786436
  0.7 16.5 %copy-start.4 = (s32[1024]{0:T(1024)S(1)}, s32[1024]{0:T(1024)}, u32[]{:S(2)}) copy-start(s32[1024]{0:T(1024)} %param.10) | copy-start | bytes 12292
  0.7 17.4 %copy-start = (bf16[1000,1024]{1,0:T(8,128)(2,1)S(1)}, bf16[1000,1024]{1,0:T(8,128)(2,1)}, u32[]{:S(2)}) copy-start(bf16[1000,1024]{1,0:T(8,128)(2,1)} %other_expression_ref.1) | copy-start | bytes 6144004
  5.9 1.8 %collective-permute-start = (f32[104,512]{1,0:T(8,128)}, f32[104,512]{1,0:T(8,128)S(1)}, u32[]{:S(2)}, u32[]{:S(2)}) collective-permute-start(f32[104,512]{1,0:T(8,128)} %get-tuple-element.71), channel_id=1, source_target_pairs={{0,1},{1,0},{2,3},{3,2},{4,5},{5,4},{6,7},{7,6},{8,9},{9,8},{10,11... | collective-permute-start | bytes 638984 | tf_op jit(solution)/shard_map/ppermute | solution.py:381
  8.7 8.5 %collective-permute-start.1 = (f32[104,512]{1,0:T(8,128)S(1)}, f32[104,512]{1,0:T(8,128)S(1)}, u32[]{:S(2)}, u32[]{:S(2)}) collective-permute-start(f32[104,512]{1,0:T(8,128)S(1)} %add.62.own_ref), channel_id=1, source_target_pairs={{0,2},{1,3},{2,0},{3,1},{4,6},{5,7},{6,4},{7,5},{8,10},{9,11},{10,... | collective-permute-start | bytes 638984 | tf_op jit(solution)/shard_map/ppermute | solution.py:381
  18.0 1.4 %collective-permute-start.2 = (f32[64,512]{1,0:T(8,128)S(1)}, f32[64,512]{1,0:T(8,128)S(1)}, u32[]{:S(2)}, u32[]{:S(2)}) collective-permute-start(f32[64,512]{1,0:T(8,128)S(1)} %shard_map.86.own_ref), channel_id=1, source_target_pairs={{0,1},{1,0},{2,3},{3,2},{4,5},{5,4},{6,7},{7,6},{8,9},{9,8},{10,11... | collective-permute-start | bytes 393224 | tf_op jit(solution)/shard_map/ppermute | solution.py:381
  20.5 10.6 %collective-permute-start.3 = (f32[320,256]{1,0:T(8,128)S(1)}, f32[320,256]{1,0:T(8,128)S(1)}, u32[]{:S(2)}, u32[]{:S(2)}) collective-permute-start(f32[320,256]{1,0:T(8,128)S(1)} %get-tuple-element.106), channel_id=1, source_target_pairs={{0,4},{4,0},{8,12},{12,8},{1,5},{5,1},{9,13},{13,9},{2,6},{6,2},{1... | collective-permute-start | bytes 983048 | tf_op jit(solution)/shard_map/ppermute | solution.py:513
  24.5 13.6 %collective-permute-start.5 = (f32[320,256]{1,0:T(8,128)S(1)}, f32[320,256]{1,0:T(8,128)S(1)}, u32[]{:S(2)}, u32[]{:S(2)}) collective-permute-start(f32[320,256]{1,0:T(8,128)S(1)} %get-tuple-element.99), channel_id=1, source_target_pairs={{0,4},{4,0},{8,12},{12,8},{1,5},{5,1},{9,13},{13,9},{2,6},{6,2},{1... | collective-permute-start | bytes 983048 | tf_op jit(solution)/shard_map/ppermute | solution.py:513
  31.1 8.9 %collective-permute-start.4 = (f32[320,256]{1,0:T(8,128)S(1)}, f32[320,256]{1,0:T(8,128)S(1)}, u32[]{:S(2)}, u32[]{:S(2)}) collective-permute-start(f32[320,256]{1,0:T(8,128)S(1)} %add.63), channel_id=1, source_target_pairs={{4,8},{8,4},{20,24},{24,20},{0,16},{12,28},{16,0},{28,12},{5,9},{9... | collective-permute-start | bytes 983048 | tf_op jit(solution)/shard_map/ppermute | solution.py:592
  33.0 12.2 %collective-permute-start.8 = (f32[320,256]{1,0:T(8,128)S(1)}, f32[320,256]{1,0:T(8,128)S(1)}, u32[]{:S(2)}, u32[]{:S(2)}) collective-permute-start(f32[320,256]{1,0:T(8,128)S(1)} %get-tuple-element.116), channel_id=1, source_target_pairs={{0,4},{4,0},{8,12},{12,8},{1,5},{5,1},{9,13},{13,9},{2,6},{6,2},{1... | collective-permute-start | bytes 983048 | tf_op jit(solution)/shard_map/ppermute | solution.py:513
  38.2 9.5 %collective-permute-start.7 = (f32[320,256]{1,0:T(8,128)S(1)}, f32[320,256]{1,0:T(8,128)S(1)}, u32[]{:S(2)}, u32[]{:S(2)}) collective-permute-start(f32[320,256]{1,0:T(8,128)S(1)} %add.64), channel_id=1, source_target_pairs={{4,8},{8,4},{20,24},{24,20},{0,16},{12,28},{16,0},{28,12},{5,9},{9... | collective-permute-start | bytes 983048 | tf_op jit(solution)/shard_map/ppermute | solution.py:592
  40.1 12.1 %collective-permute-start.6 = (f32[320,256]{1,0:T(8,128)S(1)}, f32[320,256]{1,0:T(8,128)S(1)}, u32[]{:S(2)}, u32[]{:S(2)}) collective-permute-start(f32[320,256]{1,0:T(8,128)S(1)} %broadcast_select_fusion), channel_id=1, source_target_pairs={{0,4},{4,0},{8,12},{12,8},{1,5},{5,1},{9,13},{13,9},{2,6},{6,2},{1... | collective-permute-start | bytes 983048 | tf_op jit(solution)/shard_map/ppermute | solution.py:598
  45.9 10.9 %collective-permute-start.11 = (f32[320,256]{1,0:T(8,128)}, f32[320,256]{1,0:T(8,128)S(1)}, u32[]{:S(2)}, u32[]{:S(2)}) collective-permute-start(f32[320,256]{1,0:T(8,128)} %add.66), channel_id=1, source_target_pairs={{4,8},{8,4},{20,24},{24,20},{0,16},{12,28},{16,0},{28,12},{5,9},{9... | collective-permute-start | bytes 983048 | tf_op jit(solution)/shard_map/ppermute | solution.py:592
  47.7 5.5 %copy-start.6 = (f32[320,256]{1,0:T(8,128)}, f32[320,256]{1,0:T(8,128)S(1)}, u32[]{:S(2)}) copy-start(f32[320,256]{1,0:T(8,128)S(1)} %collective-permute-done.7) | copy-start | bytes 983044
  48.5 10.1 %collective-permute-start.10 = (f32[320,256]{1,0:T(8,128)}, f32[320,256]{1,0:T(8,128)}, u32[]{:S(2)}, u32[]{:S(2)}) collective-permute-start(f32[320,256]{1,0:T(8,128)} %add.67), channel_id=1, source_target_pairs={{0,4},{4,0},{8,12},{12,8},{1,5},{5,1},{9,13},{13,9},{2,6},{6,2},{1... | collective-permute-start | bytes 983048 | tf_op jit(solution)/shard_map/ppermute | solution.py:600
  53.3 1.9 %collective-permute-start.12 = (f32[40,128]{1,0:T(8,128)S(1)}, f32[40,128]{1,0:T(8,128)S(1)}, u32[]{:S(2)}, u32[]{:S(2)}) collective-permute-start(f32[40,128]{1,0:T(8,128)S(1)} %concatenate.6), channel_id=1, source_target_pairs={{0,1},{1,0},{2,3},{3,2},{4,5},{5,4},{6,7},{7,6},{8,9},{9,8},{10,11... | collective-permute-start | bytes 61448 | tf_op jit(solution)/shard_map/ppermute | solution.py:381
  53.4 10.4 %collective-permute-start.9 = (f32[320,256]{1,0:T(8,128)}, f32[320,256]{1,0:T(8,128)S(1)}, u32[]{:S(2)}, u32[]{:S(2)}) collective-permute-start(f32[320,256]{1,0:T(8,128)} %add.68), channel_id=1, source_target_pairs={{4,8},{8,4},{20,24},{24,20},{0,16},{12,28},{16,0},{28,12},{5,9},{9... | collective-permute-start | bytes 983048 | tf_op jit(solution)/shard_map/ppermute | solution.py:592
  55.2 4.5 %copy-start.5 = (s32[5]{0:T(128)S(1)}, s32[5]{0:T(128)}, u32[]{:S(2)}) copy-start(s32[5]{0:T(128)} %size_ref.7) | copy-start | bytes 64
  55.2 4.5 %collective-permute-start.13 = (f32[80,128]{1,0:T(8,128)S(1)}, f32[80,128]{1,0:T(8,128)S(1)}, u32[]{:S(2)}, u32[]{:S(2)}) collective-permute-start(f32[80,128]{1,0:T(8,128)S(1)} %pad_maximum_fusion.pair_ref), channel_id=1, source_target_pairs={{0,2},{1,3},{2,0},{3,1},{4,6},{5,7},{6,4},{7,5},{8,10},{9,11},{10,... | collective-permute-start | bytes 122888 | tf_op jit(solution)/shard_map/ppermute | solution.py:381
  56.9 4.0 %copy-start.1 = (f32[5,64,1000]{2,1,0:T(8,128)S(1)}, f32[5,64,1000]{2,1,0:T(8,128)}, u32[]{:S(2)}) copy-start(f32[5,64,1000]{2,1,0:T(8,128)} %refs_4_.5) | copy-start | bytes 3840004
  56.9 4.0 %copy-start.2 = (f32[64,1000]{1,0:T(8,128)S(1)}, f32[64,1000]{1,0:T(8,128)}, u32[]{:S(2)}) copy-start(f32[64,1000]{1,0:T(8,128)} %shared_ref.5) | copy-start | bytes 768004
  56.9 10.3 %collective-permute-start.15 = (f32[320,256]{1,0:T(8,128)S(1)}, f32[320,256]{1,0:T(8,128)S(1)}, u32[]{:S(2)}, u32[]{:S(2)}) collective-permute-start(f32[320,256]{1,0:T(8,128)S(1)} %add.71), channel_id=1, source_target_pairs={{0,4},{4,0},{8,12},{12,8},{1,5},{5,1},{9,13},{13,9},{2,6},{6,2},{1... | collective-permute-start | bytes 983048 | tf_op jit(solution)/shard_map/ppermute | solution.py:600
  63.8 9.7 %collective-permute-start.14 = (f32[320,256]{1,0:T(8,128)S(1)}, f32[320,256]{1,0:T(8,128)S(1)}, u32[]{:S(2)}, u32[]{:S(2)}) collective-permute-start(f32[320,256]{1,0:T(8,128)S(1)} %add.76), channel_id=1, source_target_pairs={{0,4},{4,0},{8,12},{12,8},{1,5},{5,1},{9,13},{13,9},{2,6},{6,2},{1... | collective-permute-start | bytes 983048 | tf_op jit(solution)/shard_map/ppermute | solution.py:600
  65.7 11.2 %collective-permute-start.18 = (f32[144,512]{1,0:T(8,128)S(1)}, f32[144,512]{1,0:T(8,128)S(1)}, u32[]{:S(2)}, u32[]{:S(2)}) collective-permute-start(f32[144,512]{1,0:T(8,128)S(1)} %get-tuple-element.131), channel_id=1, source_target_pairs={{0,16},{16,0},{1,17},{17,1},{2,18},{18,2},{3,19},{19,3},{4,20},{20... | collective-permute-start | bytes 884744 | tf_op jit(solution)/shard_map/ppermute | solution.py:381
  69.2 9.0 %collective-permute-start.17 = (f32[128,256]{1,0:T(8,128)S(1)}, f32[128,256]{1,0:T(8,128)S(1)}, u32[]{:S(2)}, u32[]{:S(2)}) collective-permute-start(f32[128,256]{1,0:T(8,128)S(1)} %get-tuple-element.133.own_ref), channel_id=1, source_target_pairs={{0,16},{16,0},{1,17},{17,1},{2,18},{18,2},{3,19},{19,3},{4,20},{20... | collective-permute-start | bytes 393224 | tf_op jit(solution)/shard_map/ppermute | solution.py:381
  75.4 5.0 %collective-permute-start.16 = (f32[128,256]{1,0:T(8,128)S(1)}, f32[128,256]{1,0:T(8,128)S(1)}, u32[]{:S(2)}, u32[]{:S(2)}) collective-permute-start(f32[128,256]{1,0:T(8,128)S(1)} %get-tuple-element.135.own_ref), channel_id=1, source_target_pairs={{0,16},{16,0},{1,17},{17,1},{2,18},{18,2},{3,19},{19,3},{4,20},{20... | collective-permute-start | bytes 393224 | tf_op jit(solution)/shard_map/ppermute | solution.py:381

commit v5 on v4

--- a/solution.py
+++ b/solution.py
@@ -103,6 +103,24 @@
     return jnp.concatenate([high, high, low], axis=0)
 
 
+def thirds(value):
+    high, rest = value.astype(bf16), value
+    rest = rest - high.astype(f32)
+    middle = rest.astype(bf16)
+    low = (rest - middle.astype(f32)).astype(bf16)
+    return high, middle, low
+
+
+def fine_left(matrix):
+    high, middle, low = thirds(matrix)
+    return jnp.concatenate([high, high, middle, middle, high, low], axis=1)
+
+
+def fine_right(value):
+    high, middle, low = thirds(value)
+    return jnp.concatenate([high, middle, high, middle, low, high], axis=0)
+
+
 def flatten(block, width):
     parts = width // block.shape[1]
     rows = block.shape[0] // parts
@@ -184,7 +202,7 @@
     cross = both[:rank]
     rows = rank * rank // both.shape[1]
     count = both.shape[0] // rows - rank // rows
-    left = left_cat(
+    left = fine_left(
         jnp.concatenate(
             [unflatten(both[rank + e * rows : rank + (e + 1) * rows], rank) for e in range(count)],
             axis=0,
@@ -194,7 +212,7 @@
     alive = label < count
     usage = usage_ref[...]
     for sweep in range(ITERS):
-        stacked = jnp.dot(left, right_cat(usage), preferred_element_type=f32)
+        stacked = jnp.dot(left, fine_right(usage), preferred_element_type=f32)
         divisor = jnp.where(alive, 0.0, 1.0)
         for e in range(count):
             divisor += jnp.where(label == e, stacked[e * rank : (e + 1) * rank], 0.0)
@@ -437,7 +455,7 @@
             pltpu.VMEM((rows + rank, genes), bf16),
             pltpu.SemaphoreType.DMA((1 + count + cells // cell_tile,)),
         ],
-        vmem=56,
+        vmem=53.5,
         cost=cost(2 * (count + 1) * rank * genes * cells, 2 * genes * cells),
     )
     both = keep + swap(send, "gene", 1, 4)
@@ -588,16 +606,17 @@
         kind, j = step
         if kind == "across":
             part, got = after(token, own[j], inward[j])
-            token = part + got
-            across[j] = lax.ppermute(token, ("dp", "cell"), ACROSS)
+            both = part + got
+            across[j] = lax.ppermute(both, ("dp", "cell"), ACROSS)
+            token = both if j == 2 else got
         elif kind == "outward":
             part, got = after(token, own[j], across[j])
-            token = part + got
+            both, token = part + got, got
             if j == 0:
-                mixed = jnp.where(inner, token, own[last])
+                mixed = jnp.where(inner, both, own[last])
                 inward[last] = outward[0] = lax.ppermute(mixed, "cell", HALF_LINE)
             else:
-                outward[j] = lax.ppermute(token, "cell", HALF_LINE)
+                outward[j] = lax.ppermute(both, "cell", HALF_LINE)
         elif kind == "gram":
             part, got1, got2, got3 = after(token, own[0], inward[0], across[0], outward[0])
             lanes = slice(tile - SPARE, tile - SPARE + columns)

time: 81.8 us -> 79.6 us (0.973)
  other arithmetic: 5.21 us -> 3.45 us
  Pallas kernels: 20.5 us -> 19.5 us
    pallas_call x12, Pallas kernels: 20.5 us -> 19.5 us  [call(): pl.pallas_call(kernel, grid_spec=pltpu.PrefetchScalarGridSpec(num_scalar_...]
    add x1, other arithmetic: 0.96 us -> 0.03 us  [fast_body(): both = keep + swap(send, 'gene', 1, 4)]
where the time goes in v5:
time: 79.6 us; the launch traced here: 79.4 us
  waiting for transfers between devices  28 us (35%)
  starting transfers between devices  26.7 us (34%)
  Pallas kernels  19.5 us (24%)
  other arithmetic  3.45 us (4%)
  local copies, waits for them, and re-layouts  0.88 us (1%)
  between operations  0.87 us (1%)
    pallas_call x12, Pallas kernels, call(): pl.pallas_call(kernel, grid_spec=pltpu.PrefetchScalarGridSpec(num_scalar_...  19.5 us
    ppermute x3, waiting for transfers between devices, fast_body(): lax.ppermute(part, 'cell', HALF_LINE)  13.2 us
    ppermute x8, starting transfers between devices, swap(): return lax.ppermute(value, axis, [(i, i ^ offset) for i in range(size)])  9.04 us
    ppermute x8, waiting for transfers between devices, swap(): return lax.ppermute(value, axis, [(i, i ^ offset) for i in range(size)])  8.48 us
    ppermute x4, starting transfers between devices, fast_body(): across[j] = lax.ppermute(both, ('dp', 'cell'), ACROSS)  7.36 us
    ppermute x3, starting transfers between devices, fast_body(): outward[j] = lax.ppermute(both, 'cell', HALF_LINE)  4.93 us
    ppermute x3, waiting for transfers between devices, fast_body(): outward[j] = lax.ppermute(both, 'cell', HALF_LINE)  4.27 us
    ppermute x3, starting transfers between devices, fast_body(): lax.ppermute(part, 'cell', HALF_LINE)  3.73 us
  transfers between devices with their start and end apart: 19, of which 10 were waited for; matrix products, arithmetic and copies ran while one was open for 5% of the time, Pallas kernels for 15%

profile of v5, /device:TPU:0, one launch (start us, length us, event | category | flops | bytes accessed | tf_op | source)
XLA Modules:
  0.0 79.4 jit_solution(15884598115527805719)
XLA Ops:
  0.7 0.7 copy-done.4
  1.3 3.8 %shard_map.85 = (f32[104,512]{1,0:T(8,128)S(1)}, f32[104,512]{1,0:T(8,128)S(1)}) custom-call(s32[1]{0:T(128)} %bitcast.index_ref, f32[64,1000]{1,0:T(8,128)} %shared_ref.5, f32[5,64,1000]{2,1,0:T(8,128)} %refs_4_.5, bf16[1000,1024]{1,0:T(8,128)(2,1)} %other_expression_ref.1, s32[1,1024]{1,0:T(1,128)S(1)} %bitcast.3), custom_call_target="tpu_custom_call" | custom-call | flops 786432000 | bytes 2048000 | tf_op jit(solution)/shard_map/pallas_call | solution.py:378
  5.2 0.5 collective-permute-start
  5.7 1.1 %collective-permute-done = f32[104,512]{1,0:T(8,128)S(1)} collective-permute-done((f32[104,512]{1,0:T(8,128)S(1)}, f32[104,512]{1,0:T(8,128)S(1)}, u32[]{:S(2)}, u32[]{:S(2)}) %collective-permute-start) | collective-permute-done | bytes 213024 | tf_op jit(solution)/shard_map/ppermute | solution.py:399
  6.8 2.9 %collective-permute-start.1 = (f32[104,512]{1,0:T(8,128)S(1)}, f32[104,512]{1,0:T(8,128)S(1)}, u32[]{:S(2)}, u32[]{:S(2)}) collective-permute-start(f32[104,512]{1,0:T(8,128)S(1)} %add.62.own_ref), channel_id=1, source_target_pairs={{0,2},{1,3},{2,0},{3,1},{4,6},{5,7},{6,4},{7,5},{8,10},{9,11},{10,... | collective-permute-start | bytes 638984 | tf_op jit(solution)/shard_map/ppermute | solution.py:399
  9.7 5.6 %collective-permute-done.1.other_ref = f32[104,512]{1,0:T(8,128)S(1)} collective-permute-done((f32[104,512]{1,0:T(8,128)S(1)}, f32[104,512]{1,0:T(8,128)S(1)}, u32[]{:S(2)}, u32[]{:S(2)}) %collective-permute-start.1) | collective-permute-done | bytes 213024 | tf_op jit(solution)/shard_map/ppermute | solution.py:399
  15.3 1.2 %shard_map.86.own_ref = f32[64,512]{1,0:T(8,128)S(1)} custom-call(s32[1]{0:T(128)} %bitcast.index_ref, f32[104,512]{1,0:T(8,128)S(1)} %add.62.own_ref, f32[104,512]{1,0:T(8,128)S(1)} %collective-permute-done.1.other_ref, f32[64,1024]{1,0:T(8,128)S(1)} %copy-done.3, s32[1,1024]{1,0:T(1,128)S(1)} %bitcast.4), custom_call_target="tpu_custom_call" | custom-call | flops 188743680 | bytes 524288 | tf_op jit(solution)/shard_map/pallas_call | solution.py:378
  16.6 0.5 shard_map.87
  17.1 0.8 %collective-permute-done.2.other_ref = f32[64,512]{1,0:T(8,128)S(1)} collective-permute-done((f32[64,512]{1,0:T(8,128)S(1)}, f32[64,512]{1,0:T(8,128)S(1)}, u32[]{:S(2)}, u32[]{:S(2)}) %collective-permute-start.2) | collective-permute-done | bytes 131104 | tf_op jit(solution)/shard_map/ppermute | solution.py:399
  17.9 1.0 %shard_map.88 = (bf16[320,512]{1,0:T(8,128)(2,1)S(1)}, f32[320,256]{1,0:T(8,128)S(1)}) custom-call(s32[1]{0:T(128)} %bitcast.index_ref, s32[1]{0:T(128)} %bitcast.2.place_ref, f32[64,512]{1,0:T(8,128)S(1)} %collective-permute-done.2.other_ref, f32[320,256]{1,0:T(8,128)S(1)} %get-tuple-element.73.own_part_ref, f32[320,128]{1,0:T(8,128)S(1)} %get-tuple-element.74.own_gram_ref, ...), custom_call_target="tpu_custom_call" | custom-call | flops 125829120 | bytes 262144 | tf_op jit(solution)/shard_map/pallas_call | solution.py:378
  18.9 1.9 %collective-permute-start.3 = (f32[320,256]{1,0:T(8,128)S(1)}, f32[320,256]{1,0:T(8,128)S(1)}, u32[]{:S(2)}, u32[]{:S(2)}) collective-permute-start(f32[320,256]{1,0:T(8,128)S(1)} %get-tuple-element.105), channel_id=1, source_target_pairs={{0,4},{4,0},{8,12},{12,8},{1,5},{5,1},{9,13},{13,9},{2,6},{6,2},{1... | collective-permute-start | bytes 983048 | tf_op jit(solution)/shard_map/ppermute | solution.py:531
  20.8 2.2 %shard_map.89 = (f32[64,1024]{1,0:T(8,128)}, f32[320,256]{1,0:T(8,128)S(1)}, f32[320,256]{1,0:T(8,128)S(1)}, f32[320,256]{1,0:T(8,128)S(1)}) custom-call(s32[1]{0:T(128)} %bitcast.index_ref, f32[64,512]{1,0:T(8,128)S(1)} %shard_map.86.own_ref, f32[64,512]{1,0:T(8,128)S(1)} %collective-permute-done.2.other_ref, ...), custom_call_target="tpu_custom_call" | custom-call | flops 655360000 | bytes 2048000 | tf_op jit(solution)/shard_map/pallas_call | solution.py:378
  23.0 0.2 collective-permute-start.5
  23.2 6.4 %collective-permute-done.3 = f32[320,256]{1,0:T(8,128)S(1)} collective-permute-done((f32[320,256]{1,0:T(8,128)S(1)}, f32[320,256]{1,0:T(8,128)S(1)}, u32[]{:S(2)}, u32[]{:S(2)}) %collective-permute-start.3) | collective-permute-done | bytes 327712 | tf_op jit(solution)/shard_map/ppermute | solution.py:531
  29.6 1.9 %collective-permute-start.4 = (f32[320,256]{1,0:T(8,128)S(1)}, f32[320,256]{1,0:T(8,128)S(1)}, u32[]{:S(2)}, u32[]{:S(2)}) collective-permute-start(f32[320,256]{1,0:T(8,128)S(1)} %add.63), channel_id=1, source_target_pairs={{4,8},{8,4},{20,24},{24,20},{0,16},{12,28},{16,0},{28,12},{5,9},{9... | collective-permute-start | bytes 983048 | tf_op jit(solution)/shard_map/ppermute | solution.py:610
  31.4 1.6 %collective-permute-start.8 = (f32[320,256]{1,0:T(8,128)S(1)}, f32[320,256]{1,0:T(8,128)S(1)}, u32[]{:S(2)}, u32[]{:S(2)}) collective-permute-start(f32[320,256]{1,0:T(8,128)S(1)} %get-tuple-element.116), channel_id=1, source_target_pairs={{0,4},{4,0},{8,12},{12,8},{1,5},{5,1},{9,13},{13,9},{2,6},{6,2},{1... | collective-permute-start | bytes 983048 | tf_op jit(solution)/shard_map/ppermute | solution.py:531
  33.1 3.5 %collective-permute-done.5 = f32[320,256]{1,0:T(8,128)S(1)} collective-permute-done((f32[320,256]{1,0:T(8,128)S(1)}, f32[320,256]{1,0:T(8,128)S(1)}, u32[]{:S(2)}, u32[]{:S(2)}) %collective-permute-start.5) | collective-permute-done | bytes 327712 | tf_op jit(solution)/shard_map/ppermute | solution.py:531
  36.6 1.9 %collective-permute-start.7 = (f32[320,256]{1,0:T(8,128)S(1)}, f32[320,256]{1,0:T(8,128)S(1)}, u32[]{:S(2)}, u32[]{:S(2)}) collective-permute-start(f32[320,256]{1,0:T(8,128)S(1)} %add.65), channel_id=1, source_target_pairs={{4,8},{8,4},{20,24},{24,20},{0,16},{12,28},{16,0},{28,12},{5,9},{9... | collective-permute-start | bytes 983048 | tf_op jit(solution)/shard_map/ppermute | solution.py:610
  38.5 1.7 %collective-permute-start.6 = (f32[320,256]{1,0:T(8,128)S(1)}, f32[320,256]{1,0:T(8,128)S(1)}, u32[]{:S(2)}, u32[]{:S(2)}) collective-permute-start(f32[320,256]{1,0:T(8,128)S(1)} %add_select_fusion), channel_id=1, source_target_pairs={{0,4},{4,0},{8,12},{12,8},{1,5},{5,1},{9,13},{13,9},{2,6},{6,2},{1... | collective-permute-start | bytes 983048 | tf_op jit(solution)/shard_map/ppermute | solution.py:617
  40.2 3.4 %collective-permute-done.8 = f32[320,256]{1,0:T(8,128)S(1)} collective-permute-done((f32[320,256]{1,0:T(8,128)S(1)}, f32[320,256]{1,0:T(8,128)S(1)}, u32[]{:S(2)}, u32[]{:S(2)}) %collective-permute-start.8) | collective-permute-done | bytes 327712 | tf_op jit(solution)/shard_map/ppermute | solution.py:531
  43.6 0.8 add.66
  44.3 1.8 %collective-permute-start.11 = (f32[320,256]{1,0:T(8,128)}, f32[320,256]{1,0:T(8,128)S(1)}, u32[]{:S(2)}, u32[]{:S(2)}) collective-permute-start(f32[320,256]{1,0:T(8,128)} %add.66), channel_id=1, source_target_pairs={{4,8},{8,4},{20,24},{24,20},{0,16},{12,28},{16,0},{28,12},{5,9},{9... | collective-permute-start | bytes 983048 | tf_op jit(solution)/shard_map/ppermute | solution.py:610
  46.1 0.8 %add.68 = f32[320,256]{1,0:T(8,128)} add(f32[320,256]{1,0:T(8,128)S(1)} %get-tuple-element.98, f32[320,256]{1,0:T(8,128)S(1)} %collective-permute-done.7) | non-fusion elementwise | flops 81920 | bytes 983040 | tf_op jit(solution)/shard_map/add | solution.py:614
  47.0 1.6 %collective-permute-start.10 = (f32[320,256]{1,0:T(8,128)}, f32[320,256]{1,0:T(8,128)}, u32[]{:S(2)}, u32[]{:S(2)}) collective-permute-start(f32[320,256]{1,0:T(8,128)} %add.68), channel_id=1, source_target_pairs={{0,4},{4,0},{8,12},{12,8},{1,5},{5,1},{9,13},{13,9},{2,6},{6,2},{1... | collective-permute-start | bytes 983048 | tf_op jit(solution)/shard_map/ppermute | solution.py:619
  48.6 2.0 %collective-permute-done.6 = f32[320,256]{1,0:T(8,128)S(1)} collective-permute-done((f32[320,256]{1,0:T(8,128)S(1)}, f32[320,256]{1,0:T(8,128)S(1)}, u32[]{:S(2)}, u32[]{:S(2)}) %collective-permute-start.6) | collective-permute-done | bytes 327712 | tf_op jit(solution)/shard_map/ppermute | solution.py:617
  50.6 0.2 select_add_fusion.4
  50.9 0.1 concatenate.6
  51.1 1.9 %collective-permute-start.9 = (f32[320,256]{1,0:T(8,128)S(1)}, f32[320,256]{1,0:T(8,128)S(1)}, u32[]{:S(2)}, u32[]{:S(2)}) collective-permute-start(f32[320,256]{1,0:T(8,128)S(1)} %add.67), channel_id=1, source_target_pairs={{4,8},{8,4},{20,24},{24,20},{0,16},{12,28},{16,0},{28,12},{5,9},{9... | collective-permute-start | bytes 983048 | tf_op jit(solution)/shard_map/ppermute | solution.py:610
  53.0 1.6 %collective-permute-start.13 = (f32[80,128]{1,0:T(8,128)S(1)}, f32[80,128]{1,0:T(8,128)S(1)}, u32[]{:S(2)}, u32[]{:S(2)}) collective-permute-start(f32[80,128]{1,0:T(8,128)S(1)} %pad_maximum_fusion.pair_ref), channel_id=1, source_target_pairs={{0,2},{1,3},{2,0},{3,1},{4,6},{5,7},{6,4},{7,5},{8,10},{9,11},{10,... | collective-permute-start | bytes 122888 | tf_op jit(solution)/shard_map/ppermute | solution.py:399
  54.6 1.7 %collective-permute-start.15 = (f32[320,256]{1,0:T(8,128)S(1)}, f32[320,256]{1,0:T(8,128)S(1)}, u32[]{:S(2)}, u32[]{:S(2)}) collective-permute-start(f32[320,256]{1,0:T(8,128)S(1)} %add.76), channel_id=1, source_target_pairs={{0,4},{4,0},{8,12},{12,8},{1,5},{5,1},{9,13},{13,9},{2,6},{6,2},{1... | collective-permute-start | bytes 983048 | tf_op jit(solution)/shard_map/ppermute | solution.py:619
  56.3 0.7 collective-permute-done.10
  57.1 1.1 %select_add_fusion.3.refs_0_ = f32[320,256]{1,0:T(8,128)S(1)} fusion(f32[320,256]{1,0:T(8,128)S(1)} %get-tuple-element.98, f32[320,256]{1,0:T(8,128)} %collective-permute-done.10, f32[320,256]{1,0:T(8,128)S(1)} %collective-permute-done.5, f32[320,256]{1,0:T(8,128)S(1)} %copy-done.7, pred[]{:T(512)S(6)} %or.3), kind=kLoop, calls=%fused_computation.3 | loop fusion | flops 245760 | bytes 1638401 | tf_op jit(solution)/shard_map/add | solution.py:569
  58.1 1.0 %shard_map.90 = (bf16[320,192]{1,0:T(8,128)(2,1)S(1)}, f32[16,256]{1,0:T(8,128)S(1)}) custom-call(s32[1]{0:T(128)} %bitcast.2.place_ref, s32[5]{0:T(128)S(1)} %copy-done.5, f32[80,128]{1,0:T(8,128)S(1)} %pad_maximum_fusion.pair_ref, f32[80,128]{1,0:T(8,128)S(1)} %collective-permute-done.13.other_ref), custom_call_target="tpu_custom_call" | custom-call | flops 1000000 | bytes 200000 | tf_op jit(solution)/shard_map/pallas_call | solution.py:378
  59.1 0.1 select_add_fusion.2.refs_1_
  59.2 2.4 %shard_map.91 = (f32[5,64,1000]{2,1,0:T(8,128)}, f32[144,512]{1,0:T(8,128)S(1)}) custom-call(s32[5]{0:T(128)S(1)} %copy-done.5, f32[320,256]{1,0:T(8,128)S(1)} %select_add_fusion.3.refs_0_, f32[320,256]{1,0:T(8,128)S(1)} %select_add_fusion.2.refs_1_, bf16[320,192]{1,0:T(8,128)(2,1)S(1)} %get-tuple-element.111.refs_2_.refs_1_, ...), custom_call_target="tpu_custom_call" | custom-call | flops 251658240 | bytes 1966080 | tf_op jit(solution)/shard_map/pallas_call | solution.py:378
  61.6 1.6 %collective-permute-start.14 = (f32[320,256]{1,0:T(8,128)S(1)}, f32[320,256]{1,0:T(8,128)S(1)}, u32[]{:S(2)}, u32[]{:S(2)}) collective-permute-start(f32[320,256]{1,0:T(8,128)S(1)} %add.75), channel_id=1, source_target_pairs={{0,4},{4,0},{8,12},{12,8},{1,5},{5,1},{9,13},{13,9},{2,6},{6,2},{1... | collective-permute-start | bytes 983048 | tf_op jit(solution)/shard_map/ppermute | solution.py:619
  63.2 1.5 %collective-permute-start.18 = (f32[144,512]{1,0:T(8,128)S(1)}, f32[144,512]{1,0:T(8,128)S(1)}, u32[]{:S(2)}, u32[]{:S(2)}) collective-permute-start(f32[144,512]{1,0:T(8,128)S(1)} %get-tuple-element.131), channel_id=1, source_target_pairs={{0,16},{16,0},{1,17},{17,1},{2,18},{18,2},{3,19},{19,3},{4,20},{20... | collective-permute-start | bytes 884744 | tf_op jit(solution)/shard_map/ppermute | solution.py:399
  64.8 0.1 select_add_fusion.1.refs_0_
  64.9 1.9 %shard_map.92 = (f32[5,64,1000]{2,1,0:T(8,128)}, f32[128,256]{1,0:T(8,128)S(1)}) custom-call(s32[5]{0:T(128)S(1)} %copy-done.5, f32[320,256]{1,0:T(8,128)S(1)} %select_add_fusion.1.refs_0_, bf16[320,192]{1,0:T(8,128)(2,1)S(1)} %get-tuple-element.111.refs_2_.refs_1_, ...), custom_call_target="tpu_custom_call", output_to_operand_aliasing={{0}: (6, {})} | custom-call | flops 125829120 | bytes 983040 | tf_op jit(solution)/shard_map/pallas_call | solution.py:378
  66.7 1.0 %collective-permute-start.17 = (f32[128,256]{1,0:T(8,128)S(1)}, f32[128,256]{1,0:T(8,128)S(1)}, u32[]{:S(2)}, u32[]{:S(2)}) collective-permute-start(f32[128,256]{1,0:T(8,128)S(1)} %get-tuple-element.133.own_ref), channel_id=1, source_target_pairs={{0,16},{16,0},{1,17},{17,1},{2,18},{18,2},{3,19},{19,3},{4,20},{20... | collective-permute-start | bytes 393224 | tf_op jit(solution)/shard_map/ppermute | solution.py:399
  67.7 3.5 %collective-permute-done.14 = f32[320,256]{1,0:T(8,128)S(1)} collective-permute-done((f32[320,256]{1,0:T(8,128)S(1)}, f32[320,256]{1,0:T(8,128)S(1)}, u32[]{:S(2)}, u32[]{:S(2)}) %collective-permute-start.14) | collective-permute-done | bytes 327712 | tf_op jit(solution)/shard_map/ppermute | solution.py:619
  71.2 0.1 select_add_fusion.refs_0_
  71.3 1.9 %shard_map.93 = (f32[5,64,1000]{2,1,0:T(8,128)}, f32[128,256]{1,0:T(8,128)S(1)}) custom-call(s32[5]{0:T(128)S(1)} %copy-done.5, f32[320,256]{1,0:T(8,128)S(1)} %select_add_fusion.refs_0_, bf16[320,192]{1,0:T(8,128)(2,1)S(1)} %get-tuple-element.111.refs_2_.refs_1_, f32[16,256]{1,0:T(8,128)S(1)} %get-tuple-element.104.refs_3_.refs_2_, ...), custom_call_target="tpu_custom_call", output_to_operand_aliasing={{0}: (6, {})} | custom-call | flops 125829120 | bytes 983040 | tf_op jit(solution)/shard_map/pallas_call | solution.py:378
  73.2 1.4 %collective-permute-start.16 = (f32[128,256]{1,0:T(8,128)S(1)}, f32[128,256]{1,0:T(8,128)S(1)}, u32[]{:S(2)}, u32[]{:S(2)}) collective-permute-start(f32[128,256]{1,0:T(8,128)S(1)} %get-tuple-element.135.own_ref), channel_id=1, source_target_pairs={{0,16},{16,0},{1,17},{17,1},{2,18},{18,2},{3,19},{19,3},{4,20},{20... | collective-permute-start | bytes 393224 | tf_op jit(solution)/shard_map/ppermute | solution.py:399
  74.7 1.3 %shard_map.94.rest_0_ = f32[64,1000]{1,0:T(8,128)} custom-call(f32[128,512]{1,0:T(8,128)S(1)} %slice.60.own_ref, f32[128,512]{1,0:T(8,128)S(1)} %slice.61.other_ref, f32[16,256]{1,0:T(8,128)S(1)} %slice.62.gram_own, f32[16,256]{1,0:T(8,128)S(1)} %slice.72.gram_other, f32[64,1000]{1,0:T(8,128)S(1)} %copy-done.2), custom_call_target="tpu_custom_call" | custom-call | flops 37748736 | bytes 786432 | tf_op jit(solution)/shard_map/pallas_call | solution.py:378
  76.0 1.2 %shard_map.95.rest_0_ = f32[64,1000]{1,0:T(8,128)} custom-call(f32[128,256]{1,0:T(8,128)S(1)} %get-tuple-element.133.own_ref, f32[128,256]{1,0:T(8,128)S(1)} %collective-permute-done.17.other_ref, f32[16,256]{1,0:T(8,128)S(1)} %slice.62.gram_own, f32[16,256]{1,0:T(8,128)S(1)} %slice.72.gram_other, ...), custom_call_target="tpu_custom_call", output_to_operand_aliasing={{}: (5, {})} | custom-call | flops 18874368 | bytes 393216 | tf_op jit(solution)/shard_map/pallas_call | solution.py:378
  77.2 1.0 %collective-permute-done.16.other_ref = f32[128,256]{1,0:T(8,128)S(1)} collective-permute-done((f32[128,256]{1,0:T(8,128)S(1)}, f32[128,256]{1,0:T(8,128)S(1)}, u32[]{:S(2)}, u32[]{:S(2)}) %collective-permute-start.16) | collective-permute-done | bytes 131104 | tf_op jit(solution)/shard_map/ppermute | solution.py:399
  78.2 1.2 %shard_map.96 = f32[64,1000]{1,0:T(8,128)} custom-call(f32[128,256]{1,0:T(8,128)S(1)} %get-tuple-element.135.own_ref, f32[128,256]{1,0:T(8,128)S(1)} %collective-permute-done.16.other_ref, f32[16,256]{1,0:T(8,128)S(1)} %slice.62.gram_own, f32[16,256]{1,0:T(8,128)S(1)} %slice.72.gram_other, f32[64,1000]{1,0:T(8,128)S(1)} %copy-done.2, ...), custom_call_target="tpu_custom_call", output_to_operand_aliasing={{}: (5, {})} | custom-call | flops 18874368 | bytes 393216 | tf_op jit(solution)/shard_map/pallas_call | solution.py:378
  (39 shorter events, 0.6 us)
Async XLA Ops:
  0.6 0.7 copy-start.4
  1.3 14.0 %copy-start.3 = (f32[64,1024]{1,0:T(8,128)S(1)}, f32[64,1024]{1,0:T(8,128)}, u32[]{:S(2)}) copy-start(f32[64,1024]{1,0:T(8,128)} %usage_ref.1) | copy-start | bytes 786436
  1.3 15.2 %copy-start = (bf16[1000,1024]{1,0:T(8,128)(2,1)S(1)}, bf16[1000,1024]{1,0:T(8,128)(2,1)}, u32[]{:S(2)}) copy-start(bf16[1000,1024]{1,0:T(8,128)(2,1)} %other_expression_ref.1) | copy-start | bytes 6144004
  5.2 1.6 %collective-permute-start = (f32[104,512]{1,0:T(8,128)S(1)}, f32[104,512]{1,0:T(8,128)S(1)}, u32[]{:S(2)}, u32[]{:S(2)}) collective-permute-start(f32[104,512]{1,0:T(8,128)S(1)} %get-tuple-element.71), channel_id=1, source_target_pairs={{0,1},{1,0},{2,3},{3,2},{4,5},{5,4},{6,7},{7,6},{8,9},{9,8},{10,11... | collective-permute-start | bytes 638984 | tf_op jit(solution)/shard_map/ppermute | solution.py:399
  6.8 8.5 %collective-permute-start.1 = (f32[104,512]{1,0:T(8,128)S(1)}, f32[104,512]{1,0:T(8,128)S(1)}, u32[]{:S(2)}, u32[]{:S(2)}) collective-permute-start(f32[104,512]{1,0:T(8,128)S(1)} %add.62.own_ref), channel_id=1, source_target_pairs={{0,2},{1,3},{2,0},{3,1},{4,6},{5,7},{6,4},{7,5},{8,10},{9,11},{10,... | collective-permute-start | bytes 638984 | tf_op jit(solution)/shard_map/ppermute | solution.py:399
  16.5 1.4 %collective-permute-start.2 = (f32[64,512]{1,0:T(8,128)S(1)}, f32[64,512]{1,0:T(8,128)S(1)}, u32[]{:S(2)}, u32[]{:S(2)}) collective-permute-start(f32[64,512]{1,0:T(8,128)S(1)} %shard_map.86.own_ref), channel_id=1, source_target_pairs={{0,1},{1,0},{2,3},{3,2},{4,5},{5,4},{6,7},{7,6},{8,9},{9,8},{10,11... | collective-permute-start | bytes 393224 | tf_op jit(solution)/shard_map/ppermute | solution.py:399
  18.9 10.6 %collective-permute-start.3 = (f32[320,256]{1,0:T(8,128)S(1)}, f32[320,256]{1,0:T(8,128)S(1)}, u32[]{:S(2)}, u32[]{:S(2)}) collective-permute-start(f32[320,256]{1,0:T(8,128)S(1)} %get-tuple-element.105), channel_id=1, source_target_pairs={{0,4},{4,0},{8,12},{12,8},{1,5},{5,1},{9,13},{13,9},{2,6},{6,2},{1... | collective-permute-start | bytes 983048 | tf_op jit(solution)/shard_map/ppermute | solution.py:531
  23.0 13.6 %collective-permute-start.5 = (f32[320,256]{1,0:T(8,128)S(1)}, f32[320,256]{1,0:T(8,128)S(1)}, u32[]{:S(2)}, u32[]{:S(2)}) collective-permute-start(f32[320,256]{1,0:T(8,128)S(1)} %get-tuple-element.98), channel_id=1, source_target_pairs={{0,4},{4,0},{8,12},{12,8},{1,5},{5,1},{9,13},{13,9},{2,6},{6,2},{1... | collective-permute-start | bytes 983048 | tf_op jit(solution)/shard_map/ppermute | solution.py:531
  29.6 8.9 %collective-permute-start.4 = (f32[320,256]{1,0:T(8,128)S(1)}, f32[320,256]{1,0:T(8,128)S(1)}, u32[]{:S(2)}, u32[]{:S(2)}) collective-permute-start(f32[320,256]{1,0:T(8,128)S(1)} %add.63), channel_id=1, source_target_pairs={{4,8},{8,4},{20,24},{24,20},{0,16},{12,28},{16,0},{28,12},{5,9},{9... | collective-permute-start | bytes 983048 | tf_op jit(solution)/shard_map/ppermute | solution.py:610
  31.4 12.1 %collective-permute-start.8 = (f32[320,256]{1,0:T(8,128)S(1)}, f32[320,256]{1,0:T(8,128)S(1)}, u32[]{:S(2)}, u32[]{:S(2)}) collective-permute-start(f32[320,256]{1,0:T(8,128)S(1)} %get-tuple-element.116), channel_id=1, source_target_pairs={{0,4},{4,0},{8,12},{12,8},{1,5},{5,1},{9,13},{13,9},{2,6},{6,2},{1... | collective-permute-start | bytes 983048 | tf_op jit(solution)/shard_map/ppermute | solution.py:531
  36.6 9.5 %collective-permute-start.7 = (f32[320,256]{1,0:T(8,128)S(1)}, f32[320,256]{1,0:T(8,128)S(1)}, u32[]{:S(2)}, u32[]{:S(2)}) collective-permute-start(f32[320,256]{1,0:T(8,128)S(1)} %add.65), channel_id=1, source_target_pairs={{4,8},{8,4},{20,24},{24,20},{0,16},{12,28},{16,0},{28,12},{5,9},{9... | collective-permute-start | bytes 983048 | tf_op jit(solution)/shard_map/ppermute | solution.py:610
  38.5 12.1 %collective-permute-start.6 = (f32[320,256]{1,0:T(8,128)S(1)}, f32[320,256]{1,0:T(8,128)S(1)}, u32[]{:S(2)}, u32[]{:S(2)}) collective-permute-start(f32[320,256]{1,0:T(8,128)S(1)} %add_select_fusion), channel_id=1, source_target_pairs={{0,4},{4,0},{8,12},{12,8},{1,5},{5,1},{9,13},{13,9},{2,6},{6,2},{1... | collective-permute-start | bytes 983048 | tf_op jit(solution)/shard_map/ppermute | solution.py:617
  44.3 10.2 %collective-permute-start.11 = (f32[320,256]{1,0:T(8,128)}, f32[320,256]{1,0:T(8,128)S(1)}, u32[]{:S(2)}, u32[]{:S(2)}) collective-permute-start(f32[320,256]{1,0:T(8,128)} %add.66), channel_id=1, source_target_pairs={{4,8},{8,4},{20,24},{24,20},{0,16},{12,28},{16,0},{28,12},{5,9},{9... | collective-permute-start | bytes 983048 | tf_op jit(solution)/shard_map/ppermute | solution.py:610
  46.1 4.5 %copy-start.6 = (f32[320,256]{1,0:T(8,128)}, f32[320,256]{1,0:T(8,128)S(1)}, u32[]{:S(2)}) copy-start(f32[320,256]{1,0:T(8,128)S(1)} %collective-permute-done.7) | copy-start | bytes 983044
  47.0 10.1 %collective-permute-start.10 = (f32[320,256]{1,0:T(8,128)}, f32[320,256]{1,0:T(8,128)}, u32[]{:S(2)}, u32[]{:S(2)}) collective-permute-start(f32[320,256]{1,0:T(8,128)} %add.68), channel_id=1, source_target_pairs={{0,4},{4,0},{8,12},{12,8},{1,5},{5,1},{9,13},{13,9},{2,6},{6,2},{1... | collective-permute-start | bytes 983048 | tf_op jit(solution)/shard_map/ppermute | solution.py:619
  51.0 6.1 %copy-start.7 = (f32[320,256]{1,0:T(8,128)S(1)}, f32[320,256]{1,0:T(8,128)}, u32[]{:S(2)}) copy-start(f32[320,256]{1,0:T(8,128)} %copy-done.6) | copy-start | bytes 983044
  51.0 2.0 %collective-permute-start.12 = (f32[40,128]{1,0:T(8,128)S(1)}, f32[40,128]{1,0:T(8,128)S(1)}, u32[]{:S(2)}, u32[]{:S(2)}) collective-permute-start(f32[40,128]{1,0:T(8,128)S(1)} %concatenate.6), channel_id=1, source_target_pairs={{0,1},{1,0},{2,3},{3,2},{4,5},{5,4},{6,7},{7,6},{8,9},{9,8},{10,11... | collective-permute-start | bytes 61448 | tf_op jit(solution)/shard_map/ppermute | solution.py:399
  51.1 10.5 %collective-permute-start.9 = (f32[320,256]{1,0:T(8,128)S(1)}, f32[320,256]{1,0:T(8,128)S(1)}, u32[]{:S(2)}, u32[]{:S(2)}) collective-permute-start(f32[320,256]{1,0:T(8,128)S(1)} %add.67), channel_id=1, source_target_pairs={{4,8},{8,4},{20,24},{24,20},{0,16},{12,28},{16,0},{28,12},{5,9},{9... | collective-permute-start | bytes 983048 | tf_op jit(solution)/shard_map/ppermute | solution.py:610
  53.0 5.1 %copy-start.5 = (s32[5]{0:T(128)S(1)}, s32[5]{0:T(128)}, u32[]{:S(2)}) copy-start(s32[5]{0:T(128)} %size_ref.7) | copy-start | bytes 64
  53.0 5.1 %collective-permute-start.13 = (f32[80,128]{1,0:T(8,128)S(1)}, f32[80,128]{1,0:T(8,128)S(1)}, u32[]{:S(2)}, u32[]{:S(2)}) collective-permute-start(f32[80,128]{1,0:T(8,128)S(1)} %pad_maximum_fusion.pair_ref), channel_id=1, source_target_pairs={{0,2},{1,3},{2,0},{3,1},{4,6},{5,7},{6,4},{7,5},{8,10},{9,11},{10,... | collective-permute-start | bytes 122888 | tf_op jit(solution)/shard_map/ppermute | solution.py:399
  54.6 4.6 %copy-start.1 = (f32[5,64,1000]{2,1,0:T(8,128)S(1)}, f32[5,64,1000]{2,1,0:T(8,128)}, u32[]{:S(2)}) copy-start(f32[5,64,1000]{2,1,0:T(8,128)} %refs_4_.5) | copy-start | bytes 3840004
  54.6 4.6 %copy-start.2 = (f32[64,1000]{1,0:T(8,128)S(1)}, f32[64,1000]{1,0:T(8,128)}, u32[]{:S(2)}) copy-start(f32[64,1000]{1,0:T(8,128)} %shared_ref.5) | copy-start | bytes 768004
  54.6 10.2 %collective-permute-start.15 = (f32[320,256]{1,0:T(8,128)S(1)}, f32[320,256]{1,0:T(8,128)S(1)}, u32[]{:S(2)}, u32[]{:S(2)}) collective-permute-start(f32[320,256]{1,0:T(8,128)S(1)} %add.76), channel_id=1, source_target_pairs={{0,4},{4,0},{8,12},{12,8},{1,5},{5,1},{9,13},{13,9},{2,6},{6,2},{1... | collective-permute-start | bytes 983048 | tf_op jit(solution)/shard_map/ppermute | solution.py:619
  61.6 9.6 %collective-permute-start.14 = (f32[320,256]{1,0:T(8,128)S(1)}, f32[320,256]{1,0:T(8,128)S(1)}, u32[]{:S(2)}, u32[]{:S(2)}) collective-permute-start(f32[320,256]{1,0:T(8,128)S(1)} %add.75), channel_id=1, source_target_pairs={{0,4},{4,0},{8,12},{12,8},{1,5},{5,1},{9,13},{13,9},{2,6},{6,2},{1... | collective-permute-start | bytes 983048 | tf_op jit(solution)/shard_map/ppermute | solution.py:619
  63.2 11.4 %collective-permute-start.18 = (f32[144,512]{1,0:T(8,128)S(1)}, f32[144,512]{1,0:T(8,128)S(1)}, u32[]{:S(2)}, u32[]{:S(2)}) collective-permute-start(f32[144,512]{1,0:T(8,128)S(1)} %get-tuple-element.131), channel_id=1, source_target_pairs={{0,16},{16,0},{1,17},{17,1},{2,18},{18,2},{3,19},{19,3},{4,20},{20... | collective-permute-start | bytes 884744 | tf_op jit(solution)/shard_map/ppermute | solution.py:399
  66.7 9.2 %collective-permute-start.17 = (f32[128,256]{1,0:T(8,128)S(1)}, f32[128,256]{1,0:T(8,128)S(1)}, u32[]{:S(2)}, u32[]{:S(2)}) collective-permute-start(f32[128,256]{1,0:T(8,128)S(1)} %get-tuple-element.133.own_ref), channel_id=1, source_target_pairs={{0,16},{16,0},{1,17},{17,1},{2,18},{18,2},{3,19},{19,3},{4,20},{20... | collective-permute-start | bytes 393224 | tf_op jit(solution)/shard_map/ppermute | solution.py:399
  73.2 5.0 %collective-permute-start.16 = (f32[128,256]{1,0:T(8,128)S(1)}, f32[128,256]{1,0:T(8,128)S(1)}, u32[]{:S(2)}, u32[]{:S(2)}) collective-permute-start(f32[128,256]{1,0:T(8,128)S(1)} %get-tuple-element.135.own_ref), channel_id=1, source_target_pairs={{0,16},{16,0},{1,17},{17,1},{2,18},{18,2},{3,19},{19,3},{4,20},{20... | collective-permute-start | bytes 393224 | tf_op jit(solution)/shard_map/ppermute | solution.py:399

commit v6 on v5

--- a/solution.py
+++ b/solution.py
@@ -618,11 +618,7 @@
             else:
                 outward[j] = lax.ppermute(both, "cell", HALF_LINE)
         elif kind == "gram":
-            part, got1, got2, got3 = after(token, own[0], inward[0], across[0], outward[0])
-            lanes = slice(tile - SPARE, tile - SPARE + columns)
-            share = part[:, lanes] + jnp.where(
-                inner, got1[:, lanes] + got2[:, lanes], got3[:, lanes]
-            )
+            share = sum_step(0, token)[:, tile - SPARE : tile - SPARE + columns]
             packed = rows // 8
             share = jnp.concatenate(
                 [share[i * packed : (i + 1) * packed] for i in range(8)], axis=1

time: 79.6 us -> 79.6 us (level)
  local copies, waits for them, and re-layouts: 0.88 us -> 2.41 us
  waiting for transfers between devices: 28 us -> 27 us
    ppermute x3, waiting for transfers between devices: 13.2 us -> 10.8 us  [fast_body(): lax.ppermute(part, 'cell', HALF_LINE)]
    unnamed x16 -> x20, local copies, waits for them, and re-layouts: 0.71 us -> 2.16 us
    ppermute x4, waiting for transfers between devices: 0.01 us -> 1.02 us  [fast_body(): across[j] = lax.ppermute(both, ('dp', 'cell'), ACROSS)]
  transfers between devices with their start and end apart: 19 -> 19, of which waited for: 10 -> 12; matrix products, arithmetic and copies ran while one was open for 5% -> 4% of each run, Pallas kernels for 15% -> 15%
where the time goes in v6:
time: 79.6 us; the launch traced here: 79.4 us
  waiting for transfers between devices  27 us (34%)
  starting transfers between devices  26.6 us (33%)
  Pallas kernels  19.4 us (24%)
  other arithmetic  3.18 us (4%)
  local copies, waits for them, and re-layouts  2.41 us (3%)
  between operations  0.87 us (1%)
    pallas_call x12, Pallas kernels, call(): pl.pallas_call(kernel, grid_spec=pltpu.PrefetchScalarGridSpec(num_scalar_...  19.4 us
    ppermute x3, waiting for transfers between devices, fast_body(): lax.ppermute(part, 'cell', HALF_LINE)  10.8 us
    ppermute x8, starting transfers between devices, swap(): return lax.ppermute(value, axis, [(i, i ^ offset) for i in range(size)])  9.01 us
    ppermute x8, waiting for transfers between devices, swap(): return lax.ppermute(value, axis, [(i, i ^ offset) for i in range(size)])  8.49 us
    ppermute x4, starting transfers between devices, fast_body(): across[j] = lax.ppermute(both, ('dp', 'cell'), ACROSS)  7.11 us
    ppermute x3, starting transfers between devices, fast_body(): outward[j] = lax.ppermute(both, 'cell', HALF_LINE)  5.03 us
    ppermute x3, waiting for transfers between devices, fast_body(): outward[j] = lax.ppermute(both, 'cell', HALF_LINE)  4.28 us
    ppermute x3, starting transfers between devices, fast_body(): lax.ppermute(part, 'cell', HALF_LINE)  3.73 us
  transfers between devices with their start and end apart: 19, of which 12 were waited for; matrix products, arithmetic and copies ran while one was open for 4% of the time, Pallas kernels for 15%

profile of v6, /device:TPU:0, one launch (start us, length us, event | category | flops | bytes accessed | tf_op | source)
XLA Modules:
  0.0 79.4 jit_solution(768138025921815873)
XLA Ops:
  0.7 0.7 copy-done.4
  1.3 3.8 %shard_map.85 = (f32[104,512]{1,0:T(8,128)S(1)}, f32[104,512]{1,0:T(8,128)S(1)}) custom-call(s32[1]{0:T(128)} %bitcast.index_ref, f32[64,1000]{1,0:T(8,128)} %shared_ref.5, f32[5,64,1000]{2,1,0:T(8,128)} %refs_4_.5, bf16[1000,1024]{1,0:T(8,128)(2,1)} %other_expression_ref.1, s32[1,1024]{1,0:T(1,128)S(1)} %bitcast.3), custom_call_target="tpu_custom_call" | custom-call | flops 786432000 | bytes 2048000 | tf_op jit(solution)/shard_map/pallas_call | solution.py:378
  5.2 0.5 collective-permute-start
  5.7 1.1 %collective-permute-done = f32[104,512]{1,0:T(8,128)S(1)} collective-permute-done((f32[104,512]{1,0:T(8,128)S(1)}, f32[104,512]{1,0:T(8,128)S(1)}, u32[]{:S(2)}, u32[]{:S(2)}) %collective-permute-start) | collective-permute-done | bytes 213024 | tf_op jit(solution)/shard_map/ppermute | solution.py:399
  6.8 2.9 %collective-permute-start.1 = (f32[104,512]{1,0:T(8,128)S(1)}, f32[104,512]{1,0:T(8,128)S(1)}, u32[]{:S(2)}, u32[]{:S(2)}) collective-permute-start(f32[104,512]{1,0:T(8,128)S(1)} %add.56.own_ref), channel_id=1, source_target_pairs={{0,2},{1,3},{2,0},{3,1},{4,6},{5,7},{6,4},{7,5},{8,10},{9,11},{10,... | collective-permute-start | bytes 638984 | tf_op jit(solution)/shard_map/ppermute | solution.py:399
  9.7 5.6 %collective-permute-done.1.other_ref = f32[104,512]{1,0:T(8,128)S(1)} collective-permute-done((f32[104,512]{1,0:T(8,128)S(1)}, f32[104,512]{1,0:T(8,128)S(1)}, u32[]{:S(2)}, u32[]{:S(2)}) %collective-permute-start.1) | collective-permute-done | bytes 213024 | tf_op jit(solution)/shard_map/ppermute | solution.py:399
  15.3 1.2 %shard_map.86.own_ref = f32[64,512]{1,0:T(8,128)S(1)} custom-call(s32[1]{0:T(128)} %bitcast.index_ref, f32[104,512]{1,0:T(8,128)S(1)} %add.56.own_ref, f32[104,512]{1,0:T(8,128)S(1)} %collective-permute-done.1.other_ref, f32[64,1024]{1,0:T(8,128)S(1)} %copy-done.3, s32[1,1024]{1,0:T(1,128)S(1)} %bitcast.4), custom_call_target="tpu_custom_call" | custom-call | flops 188743680 | bytes 524288 | tf_op jit(solution)/shard_map/pallas_call | solution.py:378
  16.6 0.5 shard_map.87
  17.1 0.8 %collective-permute-done.2.other_ref = f32[64,512]{1,0:T(8,128)S(1)} collective-permute-done((f32[64,512]{1,0:T(8,128)S(1)}, f32[64,512]{1,0:T(8,128)S(1)}, u32[]{:S(2)}, u32[]{:S(2)}) %collective-permute-start.2) | collective-permute-done | bytes 131104 | tf_op jit(solution)/shard_map/ppermute | solution.py:399
  17.9 1.0 %shard_map.88 = (bf16[320,512]{1,0:T(8,128)(2,1)S(1)}, f32[320,256]{1,0:T(8,128)S(1)}) custom-call(s32[1]{0:T(128)} %bitcast.index_ref, s32[1]{0:T(128)} %bitcast.2.place_ref, f32[64,512]{1,0:T(8,128)S(1)} %collective-permute-done.2.other_ref, f32[320,256]{1,0:T(8,128)S(1)} %get-tuple-element.69.own_part_ref, f32[320,128]{1,0:T(8,128)S(1)} %get-tuple-element.70.own_gram_ref, ...), custom_call_target="tpu_custom_call" | custom-call | flops 125829120 | bytes 262144 | tf_op jit(solution)/shard_map/pallas_call | solution.py:378
  18.9 1.9 %collective-permute-start.3 = (f32[320,256]{1,0:T(8,128)S(1)}, f32[320,256]{1,0:T(8,128)S(1)}, u32[]{:S(2)}, u32[]{:S(2)}) collective-permute-start(f32[320,256]{1,0:T(8,128)S(1)} %get-tuple-element.89), channel_id=1, source_target_pairs={{0,4},{4,0},{8,12},{12,8},{1,5},{5,1},{9,13},{13,9},{2,6},{6,2},{1... | collective-permute-start | bytes 983048 | tf_op jit(solution)/shard_map/ppermute | solution.py:531
  20.8 2.2 %shard_map.89 = (f32[64,1024]{1,0:T(8,128)}, f32[320,256]{1,0:T(8,128)S(1)}, f32[320,256]{1,0:T(8,128)S(1)}, f32[320,256]{1,0:T(8,128)S(1)}) custom-call(s32[1]{0:T(128)} %bitcast.index_ref, f32[64,512]{1,0:T(8,128)S(1)} %shard_map.86.own_ref, f32[64,512]{1,0:T(8,128)S(1)} %collective-permute-done.2.other_ref, ...), custom_call_target="tpu_custom_call" | custom-call | flops 655360000 | bytes 2048000 | tf_op jit(solution)/shard_map/pallas_call | solution.py:378
  23.0 0.2 collective-permute-start.5
  23.2 6.4 %collective-permute-done.3 = f32[320,256]{1,0:T(8,128)S(1)} collective-permute-done((f32[320,256]{1,0:T(8,128)S(1)}, f32[320,256]{1,0:T(8,128)S(1)}, u32[]{:S(2)}, u32[]{:S(2)}) %collective-permute-start.3) | collective-permute-done | bytes 327712 | tf_op jit(solution)/shard_map/ppermute | solution.py:531
  29.5 0.7 copy-done.6
  30.3 1.8 %collective-permute-start.4 = (f32[320,256]{1,0:T(8,128)S(1)}, f32[320,256]{1,0:T(8,128)S(1)}, u32[]{:S(2)}, u32[]{:S(2)}) collective-permute-start(f32[320,256]{1,0:T(8,128)S(1)} %add.57), channel_id=1, source_target_pairs={{4,8},{8,4},{20,24},{24,20},{0,16},{12,28},{16,0},{28,12},{5,9},{9... | collective-permute-start | bytes 983048 | tf_op jit(solution)/shard_map/ppermute | solution.py:610
  32.2 1.6 %collective-permute-start.8 = (f32[320,256]{1,0:T(8,128)S(1)}, f32[320,256]{1,0:T(8,128)S(1)}, u32[]{:S(2)}, u32[]{:S(2)}) collective-permute-start(f32[320,256]{1,0:T(8,128)S(1)} %get-tuple-element.108), channel_id=1, source_target_pairs={{0,4},{4,0},{8,12},{12,8},{1,5},{5,1},{9,13},{13,9},{2,6},{6,2},{1... | collective-permute-start | bytes 983048 | tf_op jit(solution)/shard_map/ppermute | solution.py:531
  33.8 2.8 %collective-permute-done.5 = f32[320,256]{1,0:T(8,128)S(1)} collective-permute-done((f32[320,256]{1,0:T(8,128)S(1)}, f32[320,256]{1,0:T(8,128)S(1)}, u32[]{:S(2)}, u32[]{:S(2)}) %collective-permute-start.5) | collective-permute-done | bytes 327712 | tf_op jit(solution)/shard_map/ppermute | solution.py:531
  36.6 1.8 %collective-permute-start.7 = (f32[320,256]{1,0:T(8,128)S(1)}, f32[320,256]{1,0:T(8,128)S(1)}, u32[]{:S(2)}, u32[]{:S(2)}) collective-permute-start(f32[320,256]{1,0:T(8,128)S(1)} %add.59), channel_id=1, source_target_pairs={{4,8},{8,4},{20,24},{24,20},{0,16},{12,28},{16,0},{28,12},{5,9},{9... | collective-permute-start | bytes 983048 | tf_op jit(solution)/shard_map/ppermute | solution.py:610
  38.5 0.9 %collective-permute-done.4 = f32[320,256]{1,0:T(8,128)S(1)} collective-permute-done((f32[320,256]{1,0:T(8,128)S(1)}, f32[320,256]{1,0:T(8,128)S(1)}, u32[]{:S(2)}, u32[]{:S(2)}) %collective-permute-start.4) | collective-permute-done | bytes 327712 | tf_op jit(solution)/shard_map/ppermute | solution.py:610
  39.4 0.7 copy-done.8
  40.2 1.7 %collective-permute-start.6 = (f32[320,256]{1,0:T(8,128)S(1)}, f32[320,256]{1,0:T(8,128)S(1)}, u32[]{:S(2)}, u32[]{:S(2)}) collective-permute-start(f32[320,256]{1,0:T(8,128)S(1)} %add_select_fusion), channel_id=1, source_target_pairs={{0,4},{4,0},{8,12},{12,8},{1,5},{5,1},{9,13},{13,9},{2,6},{6,2},{1... | collective-permute-start | bytes 983048 | tf_op jit(solution)/shard_map/ppermute | solution.py:617
  41.9 1.7 %collective-permute-done.8 = f32[320,256]{1,0:T(8,128)S(1)} collective-permute-done((f32[320,256]{1,0:T(8,128)S(1)}, f32[320,256]{1,0:T(8,128)S(1)}, u32[]{:S(2)}, u32[]{:S(2)}) %collective-permute-start.8) | collective-permute-done | bytes 327712 | tf_op jit(solution)/shard_map/ppermute | solution.py:531
  43.6 0.8 add.60
  44.4 1.8 %collective-permute-start.11 = (f32[320,256]{1,0:T(8,128)}, f32[320,256]{1,0:T(8,128)S(1)}, u32[]{:S(2)}, u32[]{:S(2)}) collective-permute-start(f32[320,256]{1,0:T(8,128)} %add.60), channel_id=1, source_target_pairs={{4,8},{8,4},{20,24},{24,20},{0,16},{12,28},{16,0},{28,12},{5,9},{9... | collective-permute-start | bytes 983048 | tf_op jit(solution)/shard_map/ppermute | solution.py:610
  46.1 0.8 add.62
  46.9 1.6 %collective-permute-start.10 = (f32[320,256]{1,0:T(8,128)}, f32[320,256]{1,0:T(8,128)}, u32[]{:S(2)}, u32[]{:S(2)}) collective-permute-start(f32[320,256]{1,0:T(8,128)} %add.62), channel_id=1, source_target_pairs={{0,4},{4,0},{8,12},{12,8},{1,5},{5,1},{9,13},{13,9},{2,6},{6,2},{1... | collective-permute-start | bytes 983048 | tf_op jit(solution)/shard_map/ppermute | solution.py:619
  48.6 2.3 %collective-permute-done.6 = f32[320,256]{1,0:T(8,128)S(1)} collective-permute-done((f32[320,256]{1,0:T(8,128)S(1)}, f32[320,256]{1,0:T(8,128)S(1)}, u32[]{:S(2)}, u32[]{:S(2)}) %collective-permute-start.6) | collective-permute-done | bytes 327712 | tf_op jit(solution)/shard_map/ppermute | solution.py:617
  51.0 0.1 fusion
  51.1 0.1 concatenate.6
  51.4 1.6 %collective-permute-start.9 = (f32[320,256]{1,0:T(8,128)S(1)}, f32[320,256]{1,0:T(8,128)S(1)}, u32[]{:S(2)}, u32[]{:S(2)}) collective-permute-start(f32[320,256]{1,0:T(8,128)S(1)} %add.61), channel_id=1, source_target_pairs={{4,8},{8,4},{20,24},{24,20},{0,16},{12,28},{16,0},{28,12},{5,9},{9... | collective-permute-start | bytes 983048 | tf_op jit(solution)/shard_map/ppermute | solution.py:610
  53.0 1.6 %collective-permute-start.13 = (f32[80,128]{1,0:T(8,128)S(1)}, f32[80,128]{1,0:T(8,128)S(1)}, u32[]{:S(2)}, u32[]{:S(2)}) collective-permute-start(f32[80,128]{1,0:T(8,128)S(1)} %pad_maximum_fusion.pair_ref), channel_id=1, source_target_pairs={{0,2},{1,3},{2,0},{3,1},{4,6},{5,7},{6,4},{7,5},{8,10},{9,11},{10,... | collective-permute-start | bytes 122888 | tf_op jit(solution)/shard_map/ppermute | solution.py:399
  54.6 1.7 %collective-permute-start.15 = (f32[320,256]{1,0:T(8,128)S(1)}, f32[320,256]{1,0:T(8,128)S(1)}, u32[]{:S(2)}, u32[]{:S(2)}) collective-permute-start(f32[320,256]{1,0:T(8,128)S(1)} %add.68), channel_id=1, source_target_pairs={{0,4},{4,0},{8,12},{12,8},{1,5},{5,1},{9,13},{13,9},{2,6},{6,2},{1... | collective-permute-start | bytes 983048 | tf_op jit(solution)/shard_map/ppermute | solution.py:619
  56.3 0.7 collective-permute-done.10
  57.0 1.1 %select_add_fusion.2.refs_0_ = f32[320,256]{1,0:T(8,128)S(1)} fusion(f32[320,256]{1,0:T(8,128)S(1)} %get-tuple-element.94, f32[320,256]{1,0:T(8,128)} %collective-permute-done.10, f32[320,256]{1,0:T(8,128)S(1)} %collective-permute-done.5, f32[320,256]{1,0:T(8,128)S(1)} %collective-permute-done.7, pred[]{:T(512)S(6)} %or.3), kind=kLoop, calls=%fused_computation.2 | loop fusion | flops 245760 | bytes 1638401 | tf_op jit(solution)/shard_map/add | solution.py:569
  58.1 1.0 %shard_map.90 = (bf16[320,192]{1,0:T(8,128)(2,1)S(1)}, f32[16,256]{1,0:T(8,128)S(1)}) custom-call(s32[1]{0:T(128)} %bitcast.2.place_ref, s32[5]{0:T(128)S(1)} %copy-done.5, f32[80,128]{1,0:T(8,128)S(1)} %pad_maximum_fusion.pair_ref, f32[80,128]{1,0:T(8,128)S(1)} %collective-permute-done.13.other_ref), custom_call_target="tpu_custom_call" | custom-call | flops 1000000 | bytes 200000 | tf_op jit(solution)/shard_map/pallas_call | solution.py:378
  59.1 2.3 %shard_map.91 = (f32[5,64,1000]{2,1,0:T(8,128)}, f32[144,512]{1,0:T(8,128)S(1)}) custom-call(s32[5]{0:T(128)S(1)} %copy-done.5, f32[320,256]{1,0:T(8,128)S(1)} %select_add_fusion.2.refs_0_, f32[320,256]{1,0:T(8,128)S(1)} %select_add_fusion.3.refs_1_, bf16[320,192]{1,0:T(8,128)(2,1)S(1)} %get-tuple-element.103.refs_2_.refs_1_, ...), custom_call_target="tpu_custom_call" | custom-call | flops 251658240 | bytes 1966080 | tf_op jit(solution)/shard_map/pallas_call | solution.py:378
  61.6 1.7 %collective-permute-start.14 = (f32[320,256]{1,0:T(8,128)S(1)}, f32[320,256]{1,0:T(8,128)S(1)}, u32[]{:S(2)}, u32[]{:S(2)}) collective-permute-start(f32[320,256]{1,0:T(8,128)S(1)} %add.67), channel_id=1, source_target_pairs={{0,4},{4,0},{8,12},{12,8},{1,5},{5,1},{9,13},{13,9},{2,6},{6,2},{1... | collective-permute-start | bytes 983048 | tf_op jit(solution)/shard_map/ppermute | solution.py:619
  63.3 1.5 %collective-permute-start.18 = (f32[144,512]{1,0:T(8,128)S(1)}, f32[144,512]{1,0:T(8,128)S(1)}, u32[]{:S(2)}, u32[]{:S(2)}) collective-permute-start(f32[144,512]{1,0:T(8,128)S(1)} %get-tuple-element.123), channel_id=1, source_target_pairs={{0,16},{16,0},{1,17},{17,1},{2,18},{18,2},{3,19},{19,3},{4,20},{20... | collective-permute-start | bytes 884744 | tf_op jit(solution)/shard_map/ppermute | solution.py:399
  64.9 1.9 %shard_map.92 = (f32[5,64,1000]{2,1,0:T(8,128)}, f32[128,256]{1,0:T(8,128)S(1)}) custom-call(s32[5]{0:T(128)S(1)} %copy-done.5, f32[320,256]{1,0:T(8,128)S(1)} %select_add_fusion.1.refs_0_, bf16[320,192]{1,0:T(8,128)(2,1)S(1)} %get-tuple-element.103.refs_2_.refs_1_, ...), custom_call_target="tpu_custom_call", output_to_operand_aliasing={{0}: (6, {})} | custom-call | flops 125829120 | bytes 983040 | tf_op jit(solution)/shard_map/pallas_call | solution.py:378
  66.8 0.9 %collective-permute-start.17 = (f32[128,256]{1,0:T(8,128)S(1)}, f32[128,256]{1,0:T(8,128)S(1)}, u32[]{:S(2)}, u32[]{:S(2)}) collective-permute-start(f32[128,256]{1,0:T(8,128)S(1)} %get-tuple-element.125.own_ref), channel_id=1, source_target_pairs={{0,16},{16,0},{1,17},{17,1},{2,18},{18,2},{3,19},{19,3},{4,20},{20... | collective-permute-start | bytes 393224 | tf_op jit(solution)/shard_map/ppermute | solution.py:399
  67.7 3.6 %collective-permute-done.14 = f32[320,256]{1,0:T(8,128)S(1)} collective-permute-done((f32[320,256]{1,0:T(8,128)S(1)}, f32[320,256]{1,0:T(8,128)S(1)}, u32[]{:S(2)}, u32[]{:S(2)}) %collective-permute-start.14) | collective-permute-done | bytes 327712 | tf_op jit(solution)/shard_map/ppermute | solution.py:619
  71.4 1.9 %shard_map.93 = (f32[5,64,1000]{2,1,0:T(8,128)}, f32[128,256]{1,0:T(8,128)S(1)}) custom-call(s32[5]{0:T(128)S(1)} %copy-done.5, f32[320,256]{1,0:T(8,128)S(1)} %select_add_fusion.refs_0_, bf16[320,192]{1,0:T(8,128)(2,1)S(1)} %get-tuple-element.103.refs_2_.refs_1_, f32[16,256]{1,0:T(8,128)S(1)} %get-tuple-element.100.refs_3_.refs_2_, ...), custom_call_target="tpu_custom_call", output_to_operand_aliasing={{0}: (6, {})} | custom-call | flops 125829120 | bytes 983040 | tf_op jit(solution)/shard_map/pallas_call | solution.py:378
  73.3 1.4 %collective-permute-start.16 = (f32[128,256]{1,0:T(8,128)S(1)}, f32[128,256]{1,0:T(8,128)S(1)}, u32[]{:S(2)}, u32[]{:S(2)}) collective-permute-start(f32[128,256]{1,0:T(8,128)S(1)} %get-tuple-element.127.own_ref), channel_id=1, source_target_pairs={{0,16},{16,0},{1,17},{17,1},{2,18},{18,2},{3,19},{19,3},{4,20},{20... | collective-permute-start | bytes 393224 | tf_op jit(solution)/shard_map/ppermute | solution.py:399
  74.7 1.3 %shard_map.94.rest_0_ = f32[64,1000]{1,0:T(8,128)} custom-call(f32[128,512]{1,0:T(8,128)S(1)} %slice.53.own_ref, f32[128,512]{1,0:T(8,128)S(1)} %slice.54.other_ref, f32[16,256]{1,0:T(8,128)S(1)} %slice.55.gram_own, f32[16,256]{1,0:T(8,128)S(1)} %slice.65.gram_other, f32[64,1000]{1,0:T(8,128)S(1)} %copy-done.2), custom_call_target="tpu_custom_call" | custom-call | flops 37748736 | bytes 786432 | tf_op jit(solution)/shard_map/pallas_call | solution.py:378
  76.0 1.2 %shard_map.95.rest_0_ = f32[64,1000]{1,0:T(8,128)} custom-call(f32[128,256]{1,0:T(8,128)S(1)} %get-tuple-element.125.own_ref, f32[128,256]{1,0:T(8,128)S(1)} %collective-permute-done.17.other_ref, f32[16,256]{1,0:T(8,128)S(1)} %slice.55.gram_own, f32[16,256]{1,0:T(8,128)S(1)} %slice.65.gram_other, ...), custom_call_target="tpu_custom_call", output_to_operand_aliasing={{}: (5, {})} | custom-call | flops 18874368 | bytes 393216 | tf_op jit(solution)/shard_map/pallas_call | solution.py:378
  77.2 1.0 %collective-permute-done.16.other_ref = f32[128,256]{1,0:T(8,128)S(1)} collective-permute-done((f32[128,256]{1,0:T(8,128)S(1)}, f32[128,256]{1,0:T(8,128)S(1)}, u32[]{:S(2)}, u32[]{:S(2)}) %collective-permute-start.16) | collective-permute-done | bytes 131104 | tf_op jit(solution)/shard_map/ppermute | solution.py:399
  78.2 1.2 %shard_map.96 = f32[64,1000]{1,0:T(8,128)} custom-call(f32[128,256]{1,0:T(8,128)S(1)} %get-tuple-element.127.own_ref, f32[128,256]{1,0:T(8,128)S(1)} %collective-permute-done.16.other_ref, f32[16,256]{1,0:T(8,128)S(1)} %slice.55.gram_own, f32[16,256]{1,0:T(8,128)S(1)} %slice.65.gram_other, f32[64,1000]{1,0:T(8,128)S(1)} %copy-done.2, ...), custom_call_target="tpu_custom_call", output_to_operand_aliasing={{}: (5, {})} | custom-call | flops 18874368 | bytes 393216 | tf_op jit(solution)/shard_map/pallas_call | solution.py:378
  (42 shorter events, 0.9 us)
Async XLA Ops:
  0.6 0.7 copy-start.4
  1.3 14.0 %copy-start.3 = (f32[64,1024]{1,0:T(8,128)S(1)}, f32[64,1024]{1,0:T(8,128)}, u32[]{:S(2)}) copy-start(f32[64,1024]{1,0:T(8,128)} %usage_ref.1) | copy-start | bytes 786436
  1.3 15.2 %copy-start = (bf16[1000,1024]{1,0:T(8,128)(2,1)S(1)}, bf16[1000,1024]{1,0:T(8,128)(2,1)}, u32[]{:S(2)}) copy-start(bf16[1000,1024]{1,0:T(8,128)(2,1)} %other_expression_ref.1) | copy-start | bytes 6144004
  5.2 1.6 %collective-permute-start = (f32[104,512]{1,0:T(8,128)S(1)}, f32[104,512]{1,0:T(8,128)S(1)}, u32[]{:S(2)}, u32[]{:S(2)}) collective-permute-start(f32[104,512]{1,0:T(8,128)S(1)} %get-tuple-element.67), channel_id=1, source_target_pairs={{0,1},{1,0},{2,3},{3,2},{4,5},{5,4},{6,7},{7,6},{8,9},{9,8},{10,11... | collective-permute-start | bytes 638984 | tf_op jit(solution)/shard_map/ppermute | solution.py:399
  6.8 8.5 %collective-permute-start.1 = (f32[104,512]{1,0:T(8,128)S(1)}, f32[104,512]{1,0:T(8,128)S(1)}, u32[]{:S(2)}, u32[]{:S(2)}) collective-permute-start(f32[104,512]{1,0:T(8,128)S(1)} %add.56.own_ref), channel_id=1, source_target_pairs={{0,2},{1,3},{2,0},{3,1},{4,6},{5,7},{6,4},{7,5},{8,10},{9,11},{10,... | collective-permute-start | bytes 638984 | tf_op jit(solution)/shard_map/ppermute | solution.py:399
  16.5 1.4 %collective-permute-start.2 = (f32[64,512]{1,0:T(8,128)S(1)}, f32[64,512]{1,0:T(8,128)S(1)}, u32[]{:S(2)}, u32[]{:S(2)}) collective-permute-start(f32[64,512]{1,0:T(8,128)S(1)} %shard_map.86.own_ref), channel_id=1, source_target_pairs={{0,1},{1,0},{2,3},{3,2},{4,5},{5,4},{6,7},{7,6},{8,9},{9,8},{10,11... | collective-permute-start | bytes 393224 | tf_op jit(solution)/shard_map/ppermute | solution.py:399
  18.9 10.6 %collective-permute-start.3 = (f32[320,256]{1,0:T(8,128)S(1)}, f32[320,256]{1,0:T(8,128)S(1)}, u32[]{:S(2)}, u32[]{:S(2)}) collective-permute-start(f32[320,256]{1,0:T(8,128)S(1)} %get-tuple-element.89), channel_id=1, source_target_pairs={{0,4},{4,0},{8,12},{12,8},{1,5},{5,1},{9,13},{13,9},{2,6},{6,2},{1... | collective-permute-start | bytes 983048 | tf_op jit(solution)/shard_map/ppermute | solution.py:531
  23.0 13.6 %collective-permute-start.5 = (f32[320,256]{1,0:T(8,128)S(1)}, f32[320,256]{1,0:T(8,128)S(1)}, u32[]{:S(2)}, u32[]{:S(2)}) collective-permute-start(f32[320,256]{1,0:T(8,128)S(1)} %get-tuple-element.94), channel_id=1, source_target_pairs={{0,4},{4,0},{8,12},{12,8},{1,5},{5,1},{9,13},{13,9},{2,6},{6,2},{1... | collective-permute-start | bytes 983048 | tf_op jit(solution)/shard_map/ppermute | solution.py:531
  29.5 0.7 copy-start.6
  30.3 9.1 %collective-permute-start.4 = (f32[320,256]{1,0:T(8,128)S(1)}, f32[320,256]{1,0:T(8,128)S(1)}, u32[]{:S(2)}, u32[]{:S(2)}) collective-permute-start(f32[320,256]{1,0:T(8,128)S(1)} %add.57), channel_id=1, source_target_pairs={{4,8},{8,4},{20,24},{24,20},{0,16},{12,28},{16,0},{28,12},{5,9},{9... | collective-permute-start | bytes 983048 | tf_op jit(solution)/shard_map/ppermute | solution.py:610
  32.2 11.4 %collective-permute-start.8 = (f32[320,256]{1,0:T(8,128)S(1)}, f32[320,256]{1,0:T(8,128)S(1)}, u32[]{:S(2)}, u32[]{:S(2)}) collective-permute-start(f32[320,256]{1,0:T(8,128)S(1)} %get-tuple-element.108), channel_id=1, source_target_pairs={{0,4},{4,0},{8,12},{12,8},{1,5},{5,1},{9,13},{13,9},{2,6},{6,2},{1... | collective-permute-start | bytes 983048 | tf_op jit(solution)/shard_map/ppermute | solution.py:531
  36.6 9.5 %collective-permute-start.7 = (f32[320,256]{1,0:T(8,128)S(1)}, f32[320,256]{1,0:T(8,128)S(1)}, u32[]{:S(2)}, u32[]{:S(2)}) collective-permute-start(f32[320,256]{1,0:T(8,128)S(1)} %add.59), channel_id=1, source_target_pairs={{4,8},{8,4},{20,24},{24,20},{0,16},{12,28},{16,0},{28,12},{5,9},{9... | collective-permute-start | bytes 983048 | tf_op jit(solution)/shard_map/ppermute | solution.py:610
  39.4 0.7 copy-start.8
  40.2 10.7 %copy-start.7 = (f32[320,256]{1,0:T(8,128)S(1)}, f32[320,256]{1,0:T(8,128)}, u32[]{:S(2)}) copy-start(f32[320,256]{1,0:T(8,128)} %copy-done.6) | copy-start | bytes 983044
  40.2 10.7 %copy-start.9 = (f32[320,256]{1,0:T(8,128)S(1)}, f32[320,256]{1,0:T(8,128)}, u32[]{:S(2)}) copy-start(f32[320,256]{1,0:T(8,128)} %copy-done.8) | copy-start | bytes 983044
  40.2 10.7 %collective-permute-start.6 = (f32[320,256]{1,0:T(8,128)S(1)}, f32[320,256]{1,0:T(8,128)S(1)}, u32[]{:S(2)}, u32[]{:S(2)}) collective-permute-start(f32[320,256]{1,0:T(8,128)S(1)} %add_select_fusion), channel_id=1, source_target_pairs={{0,4},{4,0},{8,12},{12,8},{1,5},{5,1},{9,13},{13,9},{2,6},{6,2},{1... | collective-permute-start | bytes 983048 | tf_op jit(solution)/shard_map/ppermute | solution.py:617
  44.4 10.2 %collective-permute-start.11 = (f32[320,256]{1,0:T(8,128)}, f32[320,256]{1,0:T(8,128)S(1)}, u32[]{:S(2)}, u32[]{:S(2)}) collective-permute-start(f32[320,256]{1,0:T(8,128)} %add.60), channel_id=1, source_target_pairs={{4,8},{8,4},{20,24},{24,20},{0,16},{12,28},{16,0},{28,12},{5,9},{9... | collective-permute-start | bytes 983048 | tf_op jit(solution)/shard_map/ppermute | solution.py:610
  46.9 10.1 %collective-permute-start.10 = (f32[320,256]{1,0:T(8,128)}, f32[320,256]{1,0:T(8,128)}, u32[]{:S(2)}, u32[]{:S(2)}) collective-permute-start(f32[320,256]{1,0:T(8,128)} %add.62), channel_id=1, source_target_pairs={{0,4},{4,0},{8,12},{12,8},{1,5},{5,1},{9,13},{13,9},{2,6},{6,2},{1... | collective-permute-start | bytes 983048 | tf_op jit(solution)/shard_map/ppermute | solution.py:619
  51.2 1.8 %collective-permute-start.12 = (f32[40,128]{1,0:T(8,128)S(1)}, f32[40,128]{1,0:T(8,128)S(1)}, u32[]{:S(2)}, u32[]{:S(2)}) collective-permute-start(f32[40,128]{1,0:T(8,128)S(1)} %concatenate.6), channel_id=1, source_target_pairs={{0,1},{1,0},{2,3},{3,2},{4,5},{5,4},{6,7},{7,6},{8,9},{9,8},{10,11... | collective-permute-start | bytes 61448 | tf_op jit(solution)/shard_map/ppermute | solution.py:399
  51.4 10.2 %collective-permute-start.9 = (f32[320,256]{1,0:T(8,128)S(1)}, f32[320,256]{1,0:T(8,128)S(1)}, u32[]{:S(2)}, u32[]{:S(2)}) collective-permute-start(f32[320,256]{1,0:T(8,128)S(1)} %add.61), channel_id=1, source_target_pairs={{4,8},{8,4},{20,24},{24,20},{0,16},{12,28},{16,0},{28,12},{5,9},{9... | collective-permute-start | bytes 983048 | tf_op jit(solution)/shard_map/ppermute | solution.py:610
  53.0 5.1 %copy-start.5 = (s32[5]{0:T(128)S(1)}, s32[5]{0:T(128)}, u32[]{:S(2)}) copy-start(s32[5]{0:T(128)} %size_ref.7) | copy-start | bytes 64
  53.0 6.1 %copy-start.1 = (f32[5,64,1000]{2,1,0:T(8,128)S(1)}, f32[5,64,1000]{2,1,0:T(8,128)}, u32[]{:S(2)}) copy-start(f32[5,64,1000]{2,1,0:T(8,128)} %refs_4_.5) | copy-start | bytes 3840004
  53.0 6.1 %copy-start.2 = (f32[64,1000]{1,0:T(8,128)S(1)}, f32[64,1000]{1,0:T(8,128)}, u32[]{:S(2)}) copy-start(f32[64,1000]{1,0:T(8,128)} %shared_ref.5) | copy-start | bytes 768004
  53.0 5.1 %collective-permute-start.13 = (f32[80,128]{1,0:T(8,128)S(1)}, f32[80,128]{1,0:T(8,128)S(1)}, u32[]{:S(2)}, u32[]{:S(2)}) collective-permute-start(f32[80,128]{1,0:T(8,128)S(1)} %pad_maximum_fusion.pair_ref), channel_id=1, source_target_pairs={{0,2},{1,3},{2,0},{3,1},{4,6},{5,7},{6,4},{7,5},{8,10},{9,11},{10,... | collective-permute-start | bytes 122888 | tf_op jit(solution)/shard_map/ppermute | solution.py:399
  54.6 10.1 %collective-permute-start.15 = (f32[320,256]{1,0:T(8,128)S(1)}, f32[320,256]{1,0:T(8,128)S(1)}, u32[]{:S(2)}, u32[]{:S(2)}) collective-permute-start(f32[320,256]{1,0:T(8,128)S(1)} %add.68), channel_id=1, source_target_pairs={{0,4},{4,0},{8,12},{12,8},{1,5},{5,1},{9,13},{13,9},{2,6},{6,2},{1... | collective-permute-start | bytes 983048 | tf_op jit(solution)/shard_map/ppermute | solution.py:619
  61.6 9.7 %collective-permute-start.14 = (f32[320,256]{1,0:T(8,128)S(1)}, f32[320,256]{1,0:T(8,128)S(1)}, u32[]{:S(2)}, u32[]{:S(2)}) collective-permute-start(f32[320,256]{1,0:T(8,128)S(1)} %add.67), channel_id=1, source_target_pairs={{0,4},{4,0},{8,12},{12,8},{1,5},{5,1},{9,13},{13,9},{2,6},{6,2},{1... | collective-permute-start | bytes 983048 | tf_op jit(solution)/shard_map/ppermute | solution.py:619
  63.3 11.4 %collective-permute-start.18 = (f32[144,512]{1,0:T(8,128)S(1)}, f32[144,512]{1,0:T(8,128)S(1)}, u32[]{:S(2)}, u32[]{:S(2)}) collective-permute-start(f32[144,512]{1,0:T(8,128)S(1)} %get-tuple-element.123), channel_id=1, source_target_pairs={{0,16},{16,0},{1,17},{17,1},{2,18},{18,2},{3,19},{19,3},{4,20},{20... | collective-permute-start | bytes 884744 | tf_op jit(solution)/shard_map/ppermute | solution.py:399
  66.8 9.2 %collective-permute-start.17 = (f32[128,256]{1,0:T(8,128)S(1)}, f32[128,256]{1,0:T(8,128)S(1)}, u32[]{:S(2)}, u32[]{:S(2)}) collective-permute-start(f32[128,256]{1,0:T(8,128)S(1)} %get-tuple-element.125.own_ref), channel_id=1, source_target_pairs={{0,16},{16,0},{1,17},{17,1},{2,18},{18,2},{3,19},{19,3},{4,20},{20... | collective-permute-start | bytes 393224 | tf_op jit(solution)/shard_map/ppermute | solution.py:399
  73.3 5.0 %collective-permute-start.16 = (f32[128,256]{1,0:T(8,128)S(1)}, f32[128,256]{1,0:T(8,128)S(1)}, u32[]{:S(2)}, u32[]{:S(2)}) collective-permute-start(f32[128,256]{1,0:T(8,128)S(1)} %get-tuple-element.127.own_ref), channel_id=1, source_target_pairs={{0,16},{16,0},{1,17},{17,1},{2,18},{18,2},{3,19},{19,3},{4,20},{20... | collective-permute-start | bytes 393224 | tf_op jit(solution)/shard_map/ppermute | solution.py:399

commit v7 on v5

--- a/solution.py
+++ b/solution.py
@@ -608,7 +608,7 @@
             part, got = after(token, own[j], inward[j])
             both = part + got
             across[j] = lax.ppermute(both, ("dp", "cell"), ACROSS)
-            token = both if j == 2 else got
+            token = both[:8, :128] if j == 2 else got
         elif kind == "outward":
             part, got = after(token, own[j], across[j])
             both, token = part + got, got

time: 79.6 us -> 79.6 us (level)
    ppermute x4, waiting for transfers between devices: 0.01 us -> 4.82 us  [fast_body(): across[j] = lax.ppermute(both, ('dp', 'cell'), ACROSS)]
    ppermute x3, waiting for transfers between devices: 13.2 us -> 9.85 us  [fast_body(): lax.ppermute(part, 'cell', HALF_LINE)]
    ppermute x1, waiting for transfers between devices: 2 us -> 0.74 us  [fast_body(): inward[last] = outward[0] = lax.ppermute(mixed, 'cell', HALF_LINE)]
where the time goes in v7:
time: 79.6 us; the launch traced here: 79.4 us
  waiting for transfers between devices  28.2 us (35%)
  starting transfers between devices  26.5 us (33%)
  Pallas kernels  19.5 us (24%)
  other arithmetic  3.48 us (4%)
  local copies, waits for them, and re-layouts  0.88 us (1%)
  between operations  0.88 us (1%)
    pallas_call x12, Pallas kernels, call(): pl.pallas_call(kernel, grid_spec=pltpu.PrefetchScalarGridSpec(num_scalar_...  19.5 us
    ppermute x3, waiting for transfers between devices, fast_body(): lax.ppermute(part, 'cell', HALF_LINE)  9.85 us
    ppermute x8, starting transfers between devices, swap(): return lax.ppermute(value, axis, [(i, i ^ offset) for i in range(size)])  9.03 us
    ppermute x8, waiting for transfers between devices, swap(): return lax.ppermute(value, axis, [(i, i ^ offset) for i in range(size)])  8.48 us
    ppermute x4, starting transfers between devices, fast_body(): across[j] = lax.ppermute(both, ('dp', 'cell'), ACROSS)  7.14 us
    ppermute x3, starting transfers between devices, fast_body(): outward[j] = lax.ppermute(both, 'cell', HALF_LINE)  4.93 us
    ppermute x4, waiting for transfers between devices, fast_body(): across[j] = lax.ppermute(both, ('dp', 'cell'), ACROSS)  4.82 us
    ppermute x3, waiting for transfers between devices, fast_body(): outward[j] = lax.ppermute(both, 'cell', HALF_LINE)  4.28 us
  transfers between devices with their start and end apart: 19, of which 10 were waited for; matrix products, arithmetic and copies ran while one was open for 5% of the time, Pallas kernels for 15%

profile of v7, /device:TPU:0, one launch (start us, length us, event | category | flops | bytes accessed | tf_op | source)
XLA Modules:
  0.0 79.4 jit_solution(4422786323178233237)
XLA Ops:
  0.7 0.7 copy-done.4
  1.3 3.8 %shard_map.85 = (f32[104,512]{1,0:T(8,128)S(1)}, f32[104,512]{1,0:T(8,128)S(1)}) custom-call(s32[1]{0:T(128)} %bitcast.index_ref, f32[64,1000]{1,0:T(8,128)} %shared_ref.5, f32[5,64,1000]{2,1,0:T(8,128)} %refs_4_.5, bf16[1000,1024]{1,0:T(8,128)(2,1)} %other_expression_ref.1, s32[1,1024]{1,0:T(1,128)S(1)} %bitcast.3), custom_call_target="tpu_custom_call" | custom-call | flops 786432000 | bytes 2048000 | tf_op jit(solution)/shard_map/pallas_call | solution.py:378
  5.2 0.5 collective-permute-start
  5.7 1.1 %collective-permute-done = f32[104,512]{1,0:T(8,128)S(1)} collective-permute-done((f32[104,512]{1,0:T(8,128)S(1)}, f32[104,512]{1,0:T(8,128)S(1)}, u32[]{:S(2)}, u32[]{:S(2)}) %collective-permute-start) | collective-permute-done | bytes 213024 | tf_op jit(solution)/shard_map/ppermute | solution.py:399
  6.8 2.9 %collective-permute-start.1 = (f32[104,512]{1,0:T(8,128)S(1)}, f32[104,512]{1,0:T(8,128)S(1)}, u32[]{:S(2)}, u32[]{:S(2)}) collective-permute-start(f32[104,512]{1,0:T(8,128)S(1)} %add.62.own_ref), channel_id=1, source_target_pairs={{0,2},{1,3},{2,0},{3,1},{4,6},{5,7},{6,4},{7,5},{8,10},{9,11},{10,... | collective-permute-start | bytes 638984 | tf_op jit(solution)/shard_map/ppermute | solution.py:399
  9.7 5.6 %collective-permute-done.1.other_ref = f32[104,512]{1,0:T(8,128)S(1)} collective-permute-done((f32[104,512]{1,0:T(8,128)S(1)}, f32[104,512]{1,0:T(8,128)S(1)}, u32[]{:S(2)}, u32[]{:S(2)}) %collective-permute-start.1) | collective-permute-done | bytes 213024 | tf_op jit(solution)/shard_map/ppermute | solution.py:399
  15.3 1.2 %shard_map.86.own_ref = f32[64,512]{1,0:T(8,128)S(1)} custom-call(s32[1]{0:T(128)} %bitcast.index_ref, f32[104,512]{1,0:T(8,128)S(1)} %add.62.own_ref, f32[104,512]{1,0:T(8,128)S(1)} %collective-permute-done.1.other_ref, f32[64,1024]{1,0:T(8,128)S(1)} %copy-done.3, s32[1,1024]{1,0:T(1,128)S(1)} %bitcast.4), custom_call_target="tpu_custom_call" | custom-call | flops 188743680 | bytes 524288 | tf_op jit(solution)/shard_map/pallas_call | solution.py:378
  16.6 0.5 shard_map.87
  17.1 0.8 %collective-permute-done.2.other_ref = f32[64,512]{1,0:T(8,128)S(1)} collective-permute-done((f32[64,512]{1,0:T(8,128)S(1)}, f32[64,512]{1,0:T(8,128)S(1)}, u32[]{:S(2)}, u32[]{:S(2)}) %collective-permute-start.2) | collective-permute-done | bytes 131104 | tf_op jit(solution)/shard_map/ppermute | solution.py:399
  17.9 1.0 %shard_map.88 = (bf16[320,512]{1,0:T(8,128)(2,1)S(1)}, f32[320,256]{1,0:T(8,128)S(1)}) custom-call(s32[1]{0:T(128)} %bitcast.index_ref, s32[1]{0:T(128)} %bitcast.2.place_ref, f32[64,512]{1,0:T(8,128)S(1)} %collective-permute-done.2.other_ref, f32[320,256]{1,0:T(8,128)S(1)} %get-tuple-element.73.own_part_ref, f32[320,128]{1,0:T(8,128)S(1)} %get-tuple-element.74.own_gram_ref, ...), custom_call_target="tpu_custom_call" | custom-call | flops 125829120 | bytes 262144 | tf_op jit(solution)/shard_map/pallas_call | solution.py:378
  18.9 1.9 %collective-permute-start.3 = (f32[320,256]{1,0:T(8,128)S(1)}, f32[320,256]{1,0:T(8,128)S(1)}, u32[]{:S(2)}, u32[]{:S(2)}) collective-permute-start(f32[320,256]{1,0:T(8,128)S(1)} %get-tuple-element.105), channel_id=1, source_target_pairs={{0,4},{4,0},{8,12},{12,8},{1,5},{5,1},{9,13},{13,9},{2,6},{6,2},{1... | collective-permute-start | bytes 983048 | tf_op jit(solution)/shard_map/ppermute | solution.py:531
  20.8 2.2 %shard_map.89 = (f32[64,1024]{1,0:T(8,128)}, f32[320,256]{1,0:T(8,128)S(1)}, f32[320,256]{1,0:T(8,128)S(1)}, f32[320,256]{1,0:T(8,128)S(1)}) custom-call(s32[1]{0:T(128)} %bitcast.index_ref, f32[64,512]{1,0:T(8,128)S(1)} %shard_map.86.own_ref, f32[64,512]{1,0:T(8,128)S(1)} %collective-permute-done.2.other_ref, ...), custom_call_target="tpu_custom_call" | custom-call | flops 655360000 | bytes 2048000 | tf_op jit(solution)/shard_map/pallas_call | solution.py:378
  23.0 0.2 collective-permute-start.5
  23.2 6.4 %collective-permute-done.3 = f32[320,256]{1,0:T(8,128)S(1)} collective-permute-done((f32[320,256]{1,0:T(8,128)S(1)}, f32[320,256]{1,0:T(8,128)S(1)}, u32[]{:S(2)}, u32[]{:S(2)}) %collective-permute-start.3) | collective-permute-done | bytes 327712 | tf_op jit(solution)/shard_map/ppermute | solution.py:531
  29.6 1.9 %collective-permute-start.4 = (f32[320,256]{1,0:T(8,128)S(1)}, f32[320,256]{1,0:T(8,128)S(1)}, u32[]{:S(2)}, u32[]{:S(2)}) collective-permute-start(f32[320,256]{1,0:T(8,128)S(1)} %add.63), channel_id=1, source_target_pairs={{4,8},{8,4},{20,24},{24,20},{0,16},{12,28},{16,0},{28,12},{5,9},{9... | collective-permute-start | bytes 983048 | tf_op jit(solution)/shard_map/ppermute | solution.py:610
  31.4 1.6 %collective-permute-start.10 = (f32[320,256]{1,0:T(8,128)S(1)}, f32[320,256]{1,0:T(8,128)S(1)}, u32[]{:S(2)}, u32[]{:S(2)}) collective-permute-start(f32[320,256]{1,0:T(8,128)S(1)} %get-tuple-element.116), channel_id=1, source_target_pairs={{0,4},{4,0},{8,12},{12,8},{1,5},{5,1},{9,13},{13,9},{2,6},{6,2},{1... | collective-permute-start | bytes 983048 | tf_op jit(solution)/shard_map/ppermute | solution.py:531
  33.1 3.5 %collective-permute-done.5 = f32[320,256]{1,0:T(8,128)S(1)} collective-permute-done((f32[320,256]{1,0:T(8,128)S(1)}, f32[320,256]{1,0:T(8,128)S(1)}, u32[]{:S(2)}, u32[]{:S(2)}) %collective-permute-start.5) | collective-permute-done | bytes 327712 | tf_op jit(solution)/shard_map/ppermute | solution.py:531
  36.6 1.9 %collective-permute-start.7 = (f32[320,256]{1,0:T(8,128)S(1)}, f32[320,256]{1,0:T(8,128)S(1)}, u32[]{:S(2)}, u32[]{:S(2)}) collective-permute-start(f32[320,256]{1,0:T(8,128)S(1)} %add.65), channel_id=1, source_target_pairs={{4,8},{8,4},{20,24},{24,20},{0,16},{12,28},{16,0},{28,12},{5,9},{9... | collective-permute-start | bytes 983048 | tf_op jit(solution)/shard_map/ppermute | solution.py:610
  38.5 1.7 %collective-permute-start.6 = (f32[320,256]{1,0:T(8,128)S(1)}, f32[320,256]{1,0:T(8,128)S(1)}, u32[]{:S(2)}, u32[]{:S(2)}) collective-permute-start(f32[320,256]{1,0:T(8,128)S(1)} %add_select_fusion), channel_id=1, source_target_pairs={{0,4},{4,0},{8,12},{12,8},{1,5},{5,1},{9,13},{13,9},{2,6},{6,2},{1... | collective-permute-start | bytes 983048 | tf_op jit(solution)/shard_map/ppermute | solution.py:617
  40.2 4.8 %collective-permute-done.7 = f32[320,256]{1,0:T(8,128)S(1)} collective-permute-done((f32[320,256]{1,0:T(8,128)S(1)}, f32[320,256]{1,0:T(8,128)S(1)}, u32[]{:S(2)}, u32[]{:S(2)}) %collective-permute-start.7) | collective-permute-done | bytes 327712 | tf_op jit(solution)/shard_map/ppermute | solution.py:610
  45.0 0.8 %add.68 = f32[320,256]{1,0:T(8,128)} add(f32[320,256]{1,0:T(8,128)S(1)} %get-tuple-element.116, f32[320,256]{1,0:T(8,128)S(1)} %collective-permute-done.10) | non-fusion elementwise | flops 81920 | bytes 983040 | tf_op jit(solution)/shard_map/add | solution.py:609
  45.9 1.6 %collective-permute-start.11 = (f32[320,256]{1,0:T(8,128)}, f32[320,256]{1,0:T(8,128)S(1)}, u32[]{:S(2)}, u32[]{:S(2)}) collective-permute-start(f32[320,256]{1,0:T(8,128)} %add.68), channel_id=1, source_target_pairs={{4,8},{8,4},{20,24},{24,20},{0,16},{12,28},{16,0},{28,12},{5,9},{9... | collective-permute-start | bytes 983048 | tf_op jit(solution)/shard_map/ppermute | solution.py:610
  47.4 0.8 add.67
  48.2 1.6 %collective-permute-start.9 = (f32[320,256]{1,0:T(8,128)}, f32[320,256]{1,0:T(8,128)}, u32[]{:S(2)}, u32[]{:S(2)}) collective-permute-start(f32[320,256]{1,0:T(8,128)} %add.67), channel_id=1, source_target_pairs={{0,4},{4,0},{8,12},{12,8},{1,5},{5,1},{9,13},{13,9},{2,6},{6,2},{1... | collective-permute-start | bytes 983048 | tf_op jit(solution)/shard_map/ppermute | solution.py:619
  49.9 0.7 collective-permute-done.6
  50.6 0.2 select_add_fusion.4
  50.9 0.1 concatenate.6
  51.1 1.9 %collective-permute-start.8 = (f32[320,256]{1,0:T(8,128)S(1)}, f32[320,256]{1,0:T(8,128)S(1)}, u32[]{:S(2)}, u32[]{:S(2)}) collective-permute-start(f32[320,256]{1,0:T(8,128)S(1)} %add.66), channel_id=1, source_target_pairs={{4,8},{8,4},{20,24},{24,20},{0,16},{12,28},{16,0},{28,12},{5,9},{9... | collective-permute-start | bytes 983048 | tf_op jit(solution)/shard_map/ppermute | solution.py:610
  53.0 1.6 %collective-permute-start.13 = (f32[80,128]{1,0:T(8,128)S(1)}, f32[80,128]{1,0:T(8,128)S(1)}, u32[]{:S(2)}, u32[]{:S(2)}) collective-permute-start(f32[80,128]{1,0:T(8,128)S(1)} %pad_maximum_fusion.pair_ref), channel_id=1, source_target_pairs={{0,2},{1,3},{2,0},{3,1},{4,6},{5,7},{6,4},{7,5},{8,10},{9,11},{10,... | collective-permute-start | bytes 122888 | tf_op jit(solution)/shard_map/ppermute | solution.py:399
  54.6 1.7 %collective-permute-start.15 = (f32[320,256]{1,0:T(8,128)S(1)}, f32[320,256]{1,0:T(8,128)S(1)}, u32[]{:S(2)}, u32[]{:S(2)}) collective-permute-start(f32[320,256]{1,0:T(8,128)S(1)} %add.76), channel_id=1, source_target_pairs={{0,4},{4,0},{8,12},{12,8},{1,5},{5,1},{9,13},{13,9},{2,6},{6,2},{1... | collective-permute-start | bytes 983048 | tf_op jit(solution)/shard_map/ppermute | solution.py:619
  56.3 0.7 collective-permute-done.9
  57.1 1.1 %select_add_fusion.3.refs_0_ = f32[320,256]{1,0:T(8,128)S(1)} fusion(f32[320,256]{1,0:T(8,128)S(1)} %get-tuple-element.98, f32[320,256]{1,0:T(8,128)} %collective-permute-done.9, f32[320,256]{1,0:T(8,128)S(1)} %collective-permute-done.5, f32[320,256]{1,0:T(8,128)S(1)} %copy-done.7, pred[]{:T(512)S(6)} %or.3), kind=kLoop, calls=%fused_computation.3 | loop fusion | flops 245760 | bytes 1638401 | tf_op jit(solution)/shard_map/add | solution.py:569
  58.1 1.0 %shard_map.90 = (bf16[320,192]{1,0:T(8,128)(2,1)S(1)}, f32[16,256]{1,0:T(8,128)S(1)}) custom-call(s32[1]{0:T(128)} %bitcast.2.place_ref, s32[5]{0:T(128)S(1)} %copy-done.5, f32[80,128]{1,0:T(8,128)S(1)} %pad_maximum_fusion.pair_ref, f32[80,128]{1,0:T(8,128)S(1)} %collective-permute-done.13.other_ref), custom_call_target="tpu_custom_call" | custom-call | flops 1000000 | bytes 200000 | tf_op jit(solution)/shard_map/pallas_call | solution.py:378
  59.1 0.1 select_add_fusion.2.refs_1_
  59.2 2.4 %shard_map.91 = (f32[5,64,1000]{2,1,0:T(8,128)}, f32[144,512]{1,0:T(8,128)S(1)}) custom-call(s32[5]{0:T(128)S(1)} %copy-done.5, f32[320,256]{1,0:T(8,128)S(1)} %select_add_fusion.3.refs_0_, f32[320,256]{1,0:T(8,128)S(1)} %select_add_fusion.2.refs_1_, bf16[320,192]{1,0:T(8,128)(2,1)S(1)} %get-tuple-element.111.refs_2_.refs_1_, ...), custom_call_target="tpu_custom_call" | custom-call | flops 251658240 | bytes 1966080 | tf_op jit(solution)/shard_map/pallas_call | solution.py:378
  61.6 1.6 %collective-permute-start.14 = (f32[320,256]{1,0:T(8,128)S(1)}, f32[320,256]{1,0:T(8,128)S(1)}, u32[]{:S(2)}, u32[]{:S(2)}) collective-permute-start(f32[320,256]{1,0:T(8,128)S(1)} %add.75), channel_id=1, source_target_pairs={{0,4},{4,0},{8,12},{12,8},{1,5},{5,1},{9,13},{13,9},{2,6},{6,2},{1... | collective-permute-start | bytes 983048 | tf_op jit(solution)/shard_map/ppermute | solution.py:619
  63.3 1.5 %collective-permute-start.18 = (f32[144,512]{1,0:T(8,128)S(1)}, f32[144,512]{1,0:T(8,128)S(1)}, u32[]{:S(2)}, u32[]{:S(2)}) collective-permute-start(f32[144,512]{1,0:T(8,128)S(1)} %get-tuple-element.131), channel_id=1, source_target_pairs={{0,16},{16,0},{1,17},{17,1},{2,18},{18,2},{3,19},{19,3},{4,20},{20... | collective-permute-start | bytes 884744 | tf_op jit(solution)/shard_map/ppermute | solution.py:399
  64.8 0.1 select_add_fusion.1.refs_0_
  64.9 1.9 %shard_map.92 = (f32[5,64,1000]{2,1,0:T(8,128)}, f32[128,256]{1,0:T(8,128)S(1)}) custom-call(s32[5]{0:T(128)S(1)} %copy-done.5, f32[320,256]{1,0:T(8,128)S(1)} %select_add_fusion.1.refs_0_, bf16[320,192]{1,0:T(8,128)(2,1)S(1)} %get-tuple-element.111.refs_2_.refs_1_, ...), custom_call_target="tpu_custom_call", output_to_operand_aliasing={{0}: (6, {})} | custom-call | flops 125829120 | bytes 983040 | tf_op jit(solution)/shard_map/pallas_call | solution.py:378
  66.8 1.0 %collective-permute-start.17 = (f32[128,256]{1,0:T(8,128)S(1)}, f32[128,256]{1,0:T(8,128)S(1)}, u32[]{:S(2)}, u32[]{:S(2)}) collective-permute-start(f32[128,256]{1,0:T(8,128)S(1)} %get-tuple-element.133.own_ref), channel_id=1, source_target_pairs={{0,16},{16,0},{1,17},{17,1},{2,18},{18,2},{3,19},{19,3},{4,20},{20... | collective-permute-start | bytes 393224 | tf_op jit(solution)/shard_map/ppermute | solution.py:399
  67.7 3.5 %collective-permute-done.14 = f32[320,256]{1,0:T(8,128)S(1)} collective-permute-done((f32[320,256]{1,0:T(8,128)S(1)}, f32[320,256]{1,0:T(8,128)S(1)}, u32[]{:S(2)}, u32[]{:S(2)}) %collective-permute-start.14) | collective-permute-done | bytes 327712 | tf_op jit(solution)/shard_map/ppermute | solution.py:619
  71.3 0.1 select_add_fusion.refs_0_
  71.3 1.9 %shard_map.93 = (f32[5,64,1000]{2,1,0:T(8,128)}, f32[128,256]{1,0:T(8,128)S(1)}) custom-call(s32[5]{0:T(128)S(1)} %copy-done.5, f32[320,256]{1,0:T(8,128)S(1)} %select_add_fusion.refs_0_, bf16[320,192]{1,0:T(8,128)(2,1)S(1)} %get-tuple-element.111.refs_2_.refs_1_, f32[16,256]{1,0:T(8,128)S(1)} %get-tuple-element.104.refs_3_.refs_2_, ...), custom_call_target="tpu_custom_call", output_to_operand_aliasing={{0}: (6, {})} | custom-call | flops 125829120 | bytes 983040 | tf_op jit(solution)/shard_map/pallas_call | solution.py:378
  73.2 1.4 %collective-permute-start.16 = (f32[128,256]{1,0:T(8,128)S(1)}, f32[128,256]{1,0:T(8,128)S(1)}, u32[]{:S(2)}, u32[]{:S(2)}) collective-permute-start(f32[128,256]{1,0:T(8,128)S(1)} %get-tuple-element.135.own_ref), channel_id=1, source_target_pairs={{0,16},{16,0},{1,17},{17,1},{2,18},{18,2},{3,19},{19,3},{4,20},{20... | collective-permute-start | bytes 393224 | tf_op jit(solution)/shard_map/ppermute | solution.py:399
  74.7 1.3 %shard_map.94.rest_0_ = f32[64,1000]{1,0:T(8,128)} custom-call(f32[128,512]{1,0:T(8,128)S(1)} %slice.61.own_ref, f32[128,512]{1,0:T(8,128)S(1)} %slice.62.other_ref, f32[16,256]{1,0:T(8,128)S(1)} %slice.63.gram_own, f32[16,256]{1,0:T(8,128)S(1)} %slice.73.gram_other, f32[64,1000]{1,0:T(8,128)S(1)} %copy-done.2), custom_call_target="tpu_custom_call" | custom-call | flops 37748736 | bytes 786432 | tf_op jit(solution)/shard_map/pallas_call | solution.py:378
  76.0 1.2 %shard_map.95.rest_0_ = f32[64,1000]{1,0:T(8,128)} custom-call(f32[128,256]{1,0:T(8,128)S(1)} %get-tuple-element.133.own_ref, f32[128,256]{1,0:T(8,128)S(1)} %collective-permute-done.17.other_ref, f32[16,256]{1,0:T(8,128)S(1)} %slice.63.gram_own, f32[16,256]{1,0:T(8,128)S(1)} %slice.73.gram_other, ...), custom_call_target="tpu_custom_call", output_to_operand_aliasing={{}: (5, {})} | custom-call | flops 18874368 | bytes 393216 | tf_op jit(solution)/shard_map/pallas_call | solution.py:378
  77.2 1.0 %collective-permute-done.16.other_ref = f32[128,256]{1,0:T(8,128)S(1)} collective-permute-done((f32[128,256]{1,0:T(8,128)S(1)}, f32[128,256]{1,0:T(8,128)S(1)}, u32[]{:S(2)}, u32[]{:S(2)}) %collective-permute-start.16) | collective-permute-done | bytes 131104 | tf_op jit(solution)/shard_map/ppermute | solution.py:399
  78.2 1.2 %shard_map.96 = f32[64,1000]{1,0:T(8,128)} custom-call(f32[128,256]{1,0:T(8,128)S(1)} %get-tuple-element.135.own_ref, f32[128,256]{1,0:T(8,128)S(1)} %collective-permute-done.16.other_ref, f32[16,256]{1,0:T(8,128)S(1)} %slice.63.gram_own, f32[16,256]{1,0:T(8,128)S(1)} %slice.73.gram_other, f32[64,1000]{1,0:T(8,128)S(1)} %copy-done.2, ...), custom_call_target="tpu_custom_call", output_to_operand_aliasing={{}: (5, {})} | custom-call | flops 18874368 | bytes 393216 | tf_op jit(solution)/shard_map/pallas_call | solution.py:378
  (39 shorter events, 0.6 us)
Async XLA Ops:
  0.6 0.7 copy-start.4
  1.3 14.0 %copy-start.3 = (f32[64,1024]{1,0:T(8,128)S(1)}, f32[64,1024]{1,0:T(8,128)}, u32[]{:S(2)}) copy-start(f32[64,1024]{1,0:T(8,128)} %usage_ref.1) | copy-start | bytes 786436
  1.3 15.2 %copy-start = (bf16[1000,1024]{1,0:T(8,128)(2,1)S(1)}, bf16[1000,1024]{1,0:T(8,128)(2,1)}, u32[]{:S(2)}) copy-start(bf16[1000,1024]{1,0:T(8,128)(2,1)} %other_expression_ref.1) | copy-start | bytes 6144004
  5.2 1.6 %collective-permute-start = (f32[104,512]{1,0:T(8,128)S(1)}, f32[104,512]{1,0:T(8,128)S(1)}, u32[]{:S(2)}, u32[]{:S(2)}) collective-permute-start(f32[104,512]{1,0:T(8,128)S(1)} %get-tuple-element.71), channel_id=1, source_target_pairs={{0,1},{1,0},{2,3},{3,2},{4,5},{5,4},{6,7},{7,6},{8,9},{9,8},{10,11... | collective-permute-start | bytes 638984 | tf_op jit(solution)/shard_map/ppermute | solution.py:399
  6.8 8.5 %collective-permute-start.1 = (f32[104,512]{1,0:T(8,128)S(1)}, f32[104,512]{1,0:T(8,128)S(1)}, u32[]{:S(2)}, u32[]{:S(2)}) collective-permute-start(f32[104,512]{1,0:T(8,128)S(1)} %add.62.own_ref), channel_id=1, source_target_pairs={{0,2},{1,3},{2,0},{3,1},{4,6},{5,7},{6,4},{7,5},{8,10},{9,11},{10,... | collective-permute-start | bytes 638984 | tf_op jit(solution)/shard_map/ppermute | solution.py:399
  16.5 1.4 %collective-permute-start.2 = (f32[64,512]{1,0:T(8,128)S(1)}, f32[64,512]{1,0:T(8,128)S(1)}, u32[]{:S(2)}, u32[]{:S(2)}) collective-permute-start(f32[64,512]{1,0:T(8,128)S(1)} %shard_map.86.own_ref), channel_id=1, source_target_pairs={{0,1},{1,0},{2,3},{3,2},{4,5},{5,4},{6,7},{7,6},{8,9},{9,8},{10,11... | collective-permute-start | bytes 393224 | tf_op jit(solution)/shard_map/ppermute | solution.py:399
  18.9 10.6 %collective-permute-start.3 = (f32[320,256]{1,0:T(8,128)S(1)}, f32[320,256]{1,0:T(8,128)S(1)}, u32[]{:S(2)}, u32[]{:S(2)}) collective-permute-start(f32[320,256]{1,0:T(8,128)S(1)} %get-tuple-element.105), channel_id=1, source_target_pairs={{0,4},{4,0},{8,12},{12,8},{1,5},{5,1},{9,13},{13,9},{2,6},{6,2},{1... | collective-permute-start | bytes 983048 | tf_op jit(solution)/shard_map/ppermute | solution.py:531
  23.0 13.6 %collective-permute-start.5 = (f32[320,256]{1,0:T(8,128)S(1)}, f32[320,256]{1,0:T(8,128)S(1)}, u32[]{:S(2)}, u32[]{:S(2)}) collective-permute-start(f32[320,256]{1,0:T(8,128)S(1)} %get-tuple-element.98), channel_id=1, source_target_pairs={{0,4},{4,0},{8,12},{12,8},{1,5},{5,1},{9,13},{13,9},{2,6},{6,2},{1... | collective-permute-start | bytes 983048 | tf_op jit(solution)/shard_map/ppermute | solution.py:531
  29.6 8.9 %collective-permute-start.4 = (f32[320,256]{1,0:T(8,128)S(1)}, f32[320,256]{1,0:T(8,128)S(1)}, u32[]{:S(2)}, u32[]{:S(2)}) collective-permute-start(f32[320,256]{1,0:T(8,128)S(1)} %add.63), channel_id=1, source_target_pairs={{4,8},{8,4},{20,24},{24,20},{0,16},{12,28},{16,0},{28,12},{5,9},{9... | collective-permute-start | bytes 983048 | tf_op jit(solution)/shard_map/ppermute | solution.py:610
  31.4 13.6 %collective-permute-start.10 = (f32[320,256]{1,0:T(8,128)S(1)}, f32[320,256]{1,0:T(8,128)S(1)}, u32[]{:S(2)}, u32[]{:S(2)}) collective-permute-start(f32[320,256]{1,0:T(8,128)S(1)} %get-tuple-element.116), channel_id=1, source_target_pairs={{0,4},{4,0},{8,12},{12,8},{1,5},{5,1},{9,13},{13,9},{2,6},{6,2},{1... | collective-permute-start | bytes 983048 | tf_op jit(solution)/shard_map/ppermute | solution.py:531
  36.6 8.4 %collective-permute-start.7 = (f32[320,256]{1,0:T(8,128)S(1)}, f32[320,256]{1,0:T(8,128)S(1)}, u32[]{:S(2)}, u32[]{:S(2)}) collective-permute-start(f32[320,256]{1,0:T(8,128)S(1)} %add.65), channel_id=1, source_target_pairs={{4,8},{8,4},{20,24},{24,20},{0,16},{12,28},{16,0},{28,12},{5,9},{9... | collective-permute-start | bytes 983048 | tf_op jit(solution)/shard_map/ppermute | solution.py:610
  38.5 12.1 %collective-permute-start.6 = (f32[320,256]{1,0:T(8,128)S(1)}, f32[320,256]{1,0:T(8,128)S(1)}, u32[]{:S(2)}, u32[]{:S(2)}) collective-permute-start(f32[320,256]{1,0:T(8,128)S(1)} %add_select_fusion), channel_id=1, source_target_pairs={{0,4},{4,0},{8,12},{12,8},{1,5},{5,1},{9,13},{13,9},{2,6},{6,2},{1... | collective-permute-start | bytes 983048 | tf_op jit(solution)/shard_map/ppermute | solution.py:617
  45.0 5.8 %copy-start.6 = (f32[320,256]{1,0:T(8,128)}, f32[320,256]{1,0:T(8,128)S(1)}, u32[]{:S(2)}) copy-start(f32[320,256]{1,0:T(8,128)S(1)} %collective-permute-done.7) | copy-start | bytes 983044
  45.9 8.7 %collective-permute-start.11 = (f32[320,256]{1,0:T(8,128)}, f32[320,256]{1,0:T(8,128)S(1)}, u32[]{:S(2)}, u32[]{:S(2)}) collective-permute-start(f32[320,256]{1,0:T(8,128)} %add.68), channel_id=1, source_target_pairs={{4,8},{8,4},{20,24},{24,20},{0,16},{12,28},{16,0},{28,12},{5,9},{9... | collective-permute-start | bytes 983048 | tf_op jit(solution)/shard_map/ppermute | solution.py:610
  48.2 8.8 %collective-permute-start.9 = (f32[320,256]{1,0:T(8,128)}, f32[320,256]{1,0:T(8,128)}, u32[]{:S(2)}, u32[]{:S(2)}) collective-permute-start(f32[320,256]{1,0:T(8,128)} %add.67), channel_id=1, source_target_pairs={{0,4},{4,0},{8,12},{12,8},{1,5},{5,1},{9,13},{13,9},{2,6},{6,2},{1... | collective-permute-start | bytes 983048 | tf_op jit(solution)/shard_map/ppermute | solution.py:619
  51.0 6.1 %copy-start.7 = (f32[320,256]{1,0:T(8,128)S(1)}, f32[320,256]{1,0:T(8,128)}, u32[]{:S(2)}) copy-start(f32[320,256]{1,0:T(8,128)} %copy-done.6) | copy-start | bytes 983044
  51.0 2.0 %collective-permute-start.12 = (f32[40,128]{1,0:T(8,128)S(1)}, f32[40,128]{1,0:T(8,128)S(1)}, u32[]{:S(2)}, u32[]{:S(2)}) collective-permute-start(f32[40,128]{1,0:T(8,128)S(1)} %concatenate.6), channel_id=1, source_target_pairs={{0,1},{1,0},{2,3},{3,2},{4,5},{5,4},{6,7},{7,6},{8,9},{9,8},{10,11... | collective-permute-start | bytes 61448 | tf_op jit(solution)/shard_map/ppermute | solution.py:399
  51.1 10.5 %collective-permute-start.8 = (f32[320,256]{1,0:T(8,128)S(1)}, f32[320,256]{1,0:T(8,128)S(1)}, u32[]{:S(2)}, u32[]{:S(2)}) collective-permute-start(f32[320,256]{1,0:T(8,128)S(1)} %add.66), channel_id=1, source_target_pairs={{4,8},{8,4},{20,24},{24,20},{0,16},{12,28},{16,0},{28,12},{5,9},{9... | collective-permute-start | bytes 983048 | tf_op jit(solution)/shard_map/ppermute | solution.py:610
  53.0 5.1 %copy-start.5 = (s32[5]{0:T(128)S(1)}, s32[5]{0:T(128)}, u32[]{:S(2)}) copy-start(s32[5]{0:T(128)} %size_ref.7) | copy-start | bytes 64
  53.0 5.1 %collective-permute-start.13 = (f32[80,128]{1,0:T(8,128)S(1)}, f32[80,128]{1,0:T(8,128)S(1)}, u32[]{:S(2)}, u32[]{:S(2)}) collective-permute-start(f32[80,128]{1,0:T(8,128)S(1)} %pad_maximum_fusion.pair_ref), channel_id=1, source_target_pairs={{0,2},{1,3},{2,0},{3,1},{4,6},{5,7},{6,4},{7,5},{8,10},{9,11},{10,... | collective-permute-start | bytes 122888 | tf_op jit(solution)/shard_map/ppermute | solution.py:399
  54.6 4.6 %copy-start.1 = (f32[5,64,1000]{2,1,0:T(8,128)S(1)}, f32[5,64,1000]{2,1,0:T(8,128)}, u32[]{:S(2)}) copy-start(f32[5,64,1000]{2,1,0:T(8,128)} %refs_4_.5) | copy-start | bytes 3840004
  54.6 4.6 %copy-start.2 = (f32[64,1000]{1,0:T(8,128)S(1)}, f32[64,1000]{1,0:T(8,128)}, u32[]{:S(2)}) copy-start(f32[64,1000]{1,0:T(8,128)} %shared_ref.5) | copy-start | bytes 768004
  54.6 10.2 %collective-permute-start.15 = (f32[320,256]{1,0:T(8,128)S(1)}, f32[320,256]{1,0:T(8,128)S(1)}, u32[]{:S(2)}, u32[]{:S(2)}) collective-permute-start(f32[320,256]{1,0:T(8,128)S(1)} %add.76), channel_id=1, source_target_pairs={{0,4},{4,0},{8,12},{12,8},{1,5},{5,1},{9,13},{13,9},{2,6},{6,2},{1... | collective-permute-start | bytes 983048 | tf_op jit(solution)/shard_map/ppermute | solution.py:619
  61.6 9.6 %collective-permute-start.14 = (f32[320,256]{1,0:T(8,128)S(1)}, f32[320,256]{1,0:T(8,128)S(1)}, u32[]{:S(2)}, u32[]{:S(2)}) collective-permute-start(f32[320,256]{1,0:T(8,128)S(1)} %add.75), channel_id=1, source_target_pairs={{0,4},{4,0},{8,12},{12,8},{1,5},{5,1},{9,13},{13,9},{2,6},{6,2},{1... | collective-permute-start | bytes 983048 | tf_op jit(solution)/shard_map/ppermute | solution.py:619
  63.3 11.4 %collective-permute-start.18 = (f32[144,512]{1,0:T(8,128)S(1)}, f32[144,512]{1,0:T(8,128)S(1)}, u32[]{:S(2)}, u32[]{:S(2)}) collective-permute-start(f32[144,512]{1,0:T(8,128)S(1)} %get-tuple-element.131), channel_id=1, source_target_pairs={{0,16},{16,0},{1,17},{17,1},{2,18},{18,2},{3,19},{19,3},{4,20},{20... | collective-permute-start | bytes 884744 | tf_op jit(solution)/shard_map/ppermute | solution.py:399
  66.8 9.2 %collective-permute-start.17 = (f32[128,256]{1,0:T(8,128)S(1)}, f32[128,256]{1,0:T(8,128)S(1)}, u32[]{:S(2)}, u32[]{:S(2)}) collective-permute-start(f32[128,256]{1,0:T(8,128)S(1)} %get-tuple-element.133.own_ref), channel_id=1, source_target_pairs={{0,16},{16,0},{1,17},{17,1},{2,18},{18,2},{3,19},{19,3},{4,20},{20... | collective-permute-start | bytes 393224 | tf_op jit(solution)/shard_map/ppermute | solution.py:399
  73.2 5.0 %collective-permute-start.16 = (f32[128,256]{1,0:T(8,128)S(1)}, f32[128,256]{1,0:T(8,128)S(1)}, u32[]{:S(2)}, u32[]{:S(2)}) collective-permute-start(f32[128,256]{1,0:T(8,128)S(1)} %get-tuple-element.135.own_ref), channel_id=1, source_target_pairs={{0,16},{16,0},{1,17},{17,1},{2,18},{18,2},{3,19},{19,3},{4,20},{20... | collective-permute-start | bytes 393224 | tf_op jit(solution)/shard_map/ppermute | solution.py:399
